TPU v7x, 256 devices: a whole 4x4x8 slice. The times are simulated.
256 devices in a mesh: row: 16 (over x, y_hi, core), col: 16 (over z, y_lo).
Axes of the slice: x: 4, y: 4 (y_hi: 2, y_lo: 2; y = y_hi * 2 + y_lo), z: 8, core: 2. Of those that a mesh axis runs over, the one named last changes fastest.
Arguments:
- images: bfloat16 [32768, 1152], P(('row', 'col')), may hold values from -0.1875 to 0.1875
- texts: bfloat16 [32768, 1152], P(('row', 'col')), may hold values from -6 to 6
- head_weight: bfloat16 [1152, 1152], replicated, may hold values from -0.1875 to 0.1875
- head_bias: float32 [1152], replicated, may hold values from -3 to 3
- logit_scale: float32 [1], replicated, may hold values from 8 to 30
- logit_shift: float32 [1], replicated, may hold values from -6 to -2
- loss_scale: float32 [1], replicated, may hold values from 32768 to 65536
- clip_norm: float32 [1], replicated, may hold values from 72 to 144
Outputs:
- image_grad: float32 [32768, 1152], P(('row', 'col'))
- weight_grad: float32 [1152, 1152], replicated
- bias_grad: float32 [1152], replicated
- loss: float32 [1], replicated
All inputs are finite; a program needn't handle non-finite values.
Results may differ from a plain program's by a relative error of at most 0.0054.
Values may be sent and summed in bfloat16 or wider, within the bound.
No kernel may reach another device: no remote copies, remote signals or barrier semaphores. Data moves between devices by JAX's collectives and lax.ppermute only.
A program may use at most 64 MiB of HBM per device.

v0:
```python
import jax
import jax.numpy as jnp
from jax import lax
from jax.sharding import PartitionSpec as P

EPS = 1e-06


def passed_along(block, axis, distance):
    devices = range(lax.axis_size(axis))
    route = [((i - distance) % len(devices), i) for i in devices]
    return lax.ppermute(block, axis, route)


def local(images, texts, head_weight, head_bias, logit_scale, logit_shift, loss_scale, clip_norm):
    own_rows = images.shape[0]
    cycle_size = lax.axis_size("row")
    group_size = lax.axis_size("col")
    cycle_place = lax.axis_index("row")
    total_rows = own_rows * cycle_size * group_size
    image_full = images.astype(jnp.float32)
    inv_image = lax.rsqrt(jnp.sum(image_full * image_full, axis=1, keepdims=True) + EPS)
    x_full = image_full * inv_image
    x_b = x_full.astype(jnp.bfloat16)
    projected = jnp.dot(texts, head_weight, preferred_element_type=jnp.float32) + head_bias
    inv_text = lax.rsqrt(jnp.sum(projected * projected, axis=1, keepdims=True) + EPS)
    y_full = projected * inv_text
    y_b = y_full.astype(jnp.bfloat16)
    scale = logit_scale[0]
    shift_value = logit_shift[0]
    factor_loss = -loss_scale[0] / total_rows
    mine = cycle_place * own_rows + jnp.arange(own_rows, dtype=jnp.int32)

    def tile_work(piece, start):
        logits = scale * jnp.dot(x_b, piece.T, preferred_element_type=jnp.float32) + shift_value
        columns = start + jnp.arange(piece.shape[0], dtype=jnp.int32)
        signs = jnp.where(mine[:, None] == columns[None, :], jnp.float32(1.0), jnp.float32(-1.0))
        loss_part = jnp.sum(jax.nn.softplus(-signs * logits))
        weights = (factor_loss * signs * jax.nn.sigmoid(-signs * logits)).astype(jnp.bfloat16)
        image_part = jnp.dot(weights, piece, preferred_element_type=jnp.float32)
        text_part = lax.dot_general(
            weights, x_b, (((0,), (0,)), ((), ())), preferred_element_type=jnp.float32
        )
        return (loss_part, image_part, text_part)

    zero_loss = jnp.float32(0.0)
    zero_image = jnp.zeros((own_rows, images.shape[1]), jnp.float32)

    def cycle_step(step, carry):
        loss_sum, image_sum, moving, moving_grads = carry
        anchor = jnp.mod(cycle_place - step, cycle_size)
        loss_part, image_part, text_part = tile_work(moving, anchor * own_rows)
        moving = passed_along(moving, "row", 1)
        moving_grads = passed_along(moving_grads + text_part, "row", 1)
        return (loss_sum + loss_part, image_sum + image_part, moving, moving_grads)

    start_grads = jnp.zeros((own_rows, images.shape[1]), jnp.float32)
    loss_sum, image_sum, moving, text_sums = lax.fori_loop(
        0, cycle_size, cycle_step, (zero_loss, zero_image, y_b, start_grads)
    )
    text_side = scale * text_sums
    image_side = scale * image_sum
    image_grad = (
        image_side - x_full * jnp.sum(x_full * image_side, axis=1, keepdims=True)
    ) * inv_image
    text_back = (text_side - y_full * jnp.sum(y_full * text_side, axis=1, keepdims=True)) * inv_text
    local_weight = lax.dot_general(
        texts,
        text_back.astype(jnp.bfloat16),
        (((0,), (0,)), ((), ())),
        preferred_element_type=jnp.float32,
    )
    local_bias = jnp.sum(text_back, axis=0)
    raw_weight, raw_bias, loss_total = lax.psum(
        (local_weight, local_bias, loss_sum), ("row", "col")
    )
    total_norm = jnp.sqrt(jnp.sum(raw_weight * raw_weight) + jnp.sum(raw_bias * raw_bias))
    factor = jnp.minimum(jnp.float32(1.0), clip_norm[0] / total_norm)
    return (
        image_grad,
        raw_weight * factor,
        raw_bias * factor,
        jnp.reshape(loss_total / total_rows, (1,)),
    )


def solution(mesh):
    placed = (P(("row", "col"), None), P(("row", "col"), None), P(), P(), P(), P(), P(), P())
    return jax.shard_map(
        local,
        mesh=mesh,
        in_specs=placed,
        out_specs=(P(("row", "col"), None), P(), P(), P()),
        check_vma=False,
    )
```

profile of v0, /device:TPU:1, one launch (start us, length us, event | category | flops | bytes accessed | tf_op | source)
XLA Modules:
  0.0 679.8 jit_solution(215711547748679643)
XLA Ops:
  13.7 351.7 %while.22 = (s32[]{:T(128)}, f32[]{:T(128)}, f32[128,1152]{1,0:T(8,128)}, bf16[128,1152]{1,0:T(8,128)(2,1)}, f32[128,1152]{1,0:T(8,128)S(1)}, /*index=5*/s32[]{:...) while((s32[]{:T(128)}, f32[]{:T(128)}, ...), condition=%wide.region_4.5_spmd.clone, body=%wide.region_2.4_spmd.clone.sunk | while | flops 114163984 | bytes 8131000 | solution.py:58
  20.0 4.3 collective-permute-start.1
  26.9 7.6 %collective-permute-done = bf16[128,1152]{1,0:T(8,128)(2,1)} collective-permute-done((bf16[128,1152]{1,0:T(8,128)(2,1)S(1)}, bf16[128,1152]{1,0:T(8,128)(2,1)}, u32[]{:S(2)}, u32[]{:S(2)}) %collective-permute-start) | collective-permute-done | bytes 294944 | tf_op jit(solution)/shard_map/while/body/eval_jaxpr/ppermute | solution.py:12
  47.7 7.4 %collective-permute-done = bf16[128,1152]{1,0:T(8,128)(2,1)} collective-permute-done((bf16[128,1152]{1,0:T(8,128)(2,1)S(1)}, bf16[128,1152]{1,0:T(8,128)(2,1)}, u32[]{:S(2)}, u32[]{:S(2)}) %collective-permute-start) | collective-permute-done | bytes 294944 | tf_op jit(solution)/shard_map/while/body/eval_jaxpr/ppermute | solution.py:12
  68.2 7.4 %collective-permute-done = bf16[128,1152]{1,0:T(8,128)(2,1)} collective-permute-done((bf16[128,1152]{1,0:T(8,128)(2,1)S(1)}, bf16[128,1152]{1,0:T(8,128)(2,1)}, u32[]{:S(2)}, u32[]{:S(2)}) %collective-permute-start) | collective-permute-done | bytes 294944 | tf_op jit(solution)/shard_map/while/body/eval_jaxpr/ppermute | solution.py:12
  88.8 7.4 %collective-permute-done = bf16[128,1152]{1,0:T(8,128)(2,1)} collective-permute-done((bf16[128,1152]{1,0:T(8,128)(2,1)S(1)}, bf16[128,1152]{1,0:T(8,128)(2,1)}, u32[]{:S(2)}, u32[]{:S(2)}) %collective-permute-start) | collective-permute-done | bytes 294944 | tf_op jit(solution)/shard_map/while/body/eval_jaxpr/ppermute | solution.py:12
  109.4 7.4 %collective-permute-done = bf16[128,1152]{1,0:T(8,128)(2,1)} collective-permute-done((bf16[128,1152]{1,0:T(8,128)(2,1)S(1)}, bf16[128,1152]{1,0:T(8,128)(2,1)}, u32[]{:S(2)}, u32[]{:S(2)}) %collective-permute-start) | collective-permute-done | bytes 294944 | tf_op jit(solution)/shard_map/while/body/eval_jaxpr/ppermute | solution.py:12
  130.8 7.5 %collective-permute-done = bf16[128,1152]{1,0:T(8,128)(2,1)} collective-permute-done((bf16[128,1152]{1,0:T(8,128)(2,1)S(1)}, bf16[128,1152]{1,0:T(8,128)(2,1)}, u32[]{:S(2)}, u32[]{:S(2)}) %collective-permute-start) | collective-permute-done | bytes 294944 | tf_op jit(solution)/shard_map/while/body/eval_jaxpr/ppermute | solution.py:12
  152.2 8.7 %collective-permute-done = bf16[128,1152]{1,0:T(8,128)(2,1)} collective-permute-done((bf16[128,1152]{1,0:T(8,128)(2,1)S(1)}, bf16[128,1152]{1,0:T(8,128)(2,1)}, u32[]{:S(2)}, u32[]{:S(2)}) %collective-permute-start) | collective-permute-done | bytes 294944 | tf_op jit(solution)/shard_map/while/body/eval_jaxpr/ppermute | solution.py:12
  173.7 9.9 %collective-permute-done = bf16[128,1152]{1,0:T(8,128)(2,1)} collective-permute-done((bf16[128,1152]{1,0:T(8,128)(2,1)S(1)}, bf16[128,1152]{1,0:T(8,128)(2,1)}, u32[]{:S(2)}, u32[]{:S(2)}) %collective-permute-start) | collective-permute-done | bytes 294944 | tf_op jit(solution)/shard_map/while/body/eval_jaxpr/ppermute | solution.py:12
  195.1 11.1 %collective-permute-done = bf16[128,1152]{1,0:T(8,128)(2,1)} collective-permute-done((bf16[128,1152]{1,0:T(8,128)(2,1)S(1)}, bf16[128,1152]{1,0:T(8,128)(2,1)}, u32[]{:S(2)}, u32[]{:S(2)}) %collective-permute-start) | collective-permute-done | bytes 294944 | tf_op jit(solution)/shard_map/while/body/eval_jaxpr/ppermute | solution.py:12
  216.6 12.3 %collective-permute-done = bf16[128,1152]{1,0:T(8,128)(2,1)} collective-permute-done((bf16[128,1152]{1,0:T(8,128)(2,1)S(1)}, bf16[128,1152]{1,0:T(8,128)(2,1)}, u32[]{:S(2)}, u32[]{:S(2)}) %collective-permute-start) | collective-permute-done | bytes 294944 | tf_op jit(solution)/shard_map/while/body/eval_jaxpr/ppermute | solution.py:12
  238.5 13.1 %collective-permute-done = bf16[128,1152]{1,0:T(8,128)(2,1)} collective-permute-done((bf16[128,1152]{1,0:T(8,128)(2,1)S(1)}, bf16[128,1152]{1,0:T(8,128)(2,1)}, u32[]{:S(2)}, u32[]{:S(2)}) %collective-permute-start) | collective-permute-done | bytes 294944 | tf_op jit(solution)/shard_map/while/body/eval_jaxpr/ppermute | solution.py:12
  261.1 13.1 %collective-permute-done = bf16[128,1152]{1,0:T(8,128)(2,1)} collective-permute-done((bf16[128,1152]{1,0:T(8,128)(2,1)S(1)}, bf16[128,1152]{1,0:T(8,128)(2,1)}, u32[]{:S(2)}, u32[]{:S(2)}) %collective-permute-start) | collective-permute-done | bytes 294944 | tf_op jit(solution)/shard_map/while/body/eval_jaxpr/ppermute | solution.py:12
  283.8 13.1 %collective-permute-done = bf16[128,1152]{1,0:T(8,128)(2,1)} collective-permute-done((bf16[128,1152]{1,0:T(8,128)(2,1)S(1)}, bf16[128,1152]{1,0:T(8,128)(2,1)}, u32[]{:S(2)}, u32[]{:S(2)}) %collective-permute-start) | collective-permute-done | bytes 294944 | tf_op jit(solution)/shard_map/while/body/eval_jaxpr/ppermute | solution.py:12
  306.5 13.1 %collective-permute-done = bf16[128,1152]{1,0:T(8,128)(2,1)} collective-permute-done((bf16[128,1152]{1,0:T(8,128)(2,1)S(1)}, bf16[128,1152]{1,0:T(8,128)(2,1)}, u32[]{:S(2)}, u32[]{:S(2)}) %collective-permute-start) | collective-permute-done | bytes 294944 | tf_op jit(solution)/shard_map/while/body/eval_jaxpr/ppermute | solution.py:12
  329.1 13.1 %collective-permute-done = bf16[128,1152]{1,0:T(8,128)(2,1)} collective-permute-done((bf16[128,1152]{1,0:T(8,128)(2,1)S(1)}, bf16[128,1152]{1,0:T(8,128)(2,1)}, u32[]{:S(2)}, u32[]{:S(2)}) %collective-permute-start) | collective-permute-done | bytes 294944 | tf_op jit(solution)/shard_map/while/body/eval_jaxpr/ppermute | solution.py:12
  351.8 13.1 %collective-permute-done = bf16[128,1152]{1,0:T(8,128)(2,1)} collective-permute-done((bf16[128,1152]{1,0:T(8,128)(2,1)S(1)}, bf16[128,1152]{1,0:T(8,128)(2,1)}, u32[]{:S(2)}, u32[]{:S(2)}) %collective-permute-start) | collective-permute-done | bytes 294944 | tf_op jit(solution)/shard_map/while/body/eval_jaxpr/ppermute | solution.py:12
  366.7 4.5 convolution_bitcast_fusion
  373.2 90.8 %all-reduce = (f32[1152]{0:T(1024)S(1)}, f32[]{:T(128)}) all-reduce(f32[1152]{0:T(1024)S(1)} %fusion.17, f32[]{:T(128)} %get-tuple-element.273), channel_id=1, replica_groups=mesh['row'=16,'col'=16] {'row','col'}, use_global_device_ids=true, to_apply=%region_10.11 | all-reduce | flops 1153 | bytes 9224 | tf_op jit(solution)/shard_map/psum | solution.py:74
  468.7 184.7 %all-reduce.3.cloned.1.call-done = f32[1152,1152]{0,1:T(8,128)} async-done(((f32[1152,1152]{0,1:T(8,128)}), f32[1152,1152]{0,1:T(8,128)}) %all-reduce.3.cloned.1.call-update) | async-done | bytes 5308432 | tf_op jit(solution)/shard_map/psum | solution.py:74
  653.4 4.5 multiply_reduce_fusion
  659.8 5.2 broadcast_multiply_fusion
  665.0 6.9 %copy.12 = f32[1152,1152]{1,0:T(8,128)} copy(f32[1152,1152]{0,1:T(8,128)} %broadcast_multiply_fusion) | data formatting | bytes 10616832
  (182 shorter events, 184.6 us)
Async XLA Ops:
  7.2 646.2 %all-reduce.3.cloned.1.call-start = ((), (), s32[]{:S(2)}) async-start(), calls=%async_computation | async-start | bytes 10616832 | tf_op jit(solution)/shard_map/psum | solution.py:74
  20.0 14.5 %collective-permute-start.1 = (f32[128,1152]{1,0:T(8,128)}, f32[128,1152]{1,0:T(8,128)S(1)}, u32[]{:S(2)}, u32[]{:S(2)}) collective-permute-start(f32[128,1152]{1,0:T(8,128)} %convolution_add_fusion.6), channel_id=1, source_target_pairs={{240,0},{0,16},{16,32},{32,48},{48,64},{64,80},{80,96},{96,112},{1... | collective-permute-start | bytes 1769480 | tf_op jit(solution)/shard_map/while/body/eval_jaxpr/ppermute | solution.py:12
  40.8 14.3 %collective-permute-start.1 = (f32[128,1152]{1,0:T(8,128)}, f32[128,1152]{1,0:T(8,128)S(1)}, u32[]{:S(2)}, u32[]{:S(2)}) collective-permute-start(f32[128,1152]{1,0:T(8,128)} %convolution_add_fusion.6), channel_id=1, source_target_pairs={{240,0},{0,16},{16,32},{32,48},{48,64},{64,80},{80,96},{96,112},{1... | collective-permute-start | bytes 1769480 | tf_op jit(solution)/shard_map/while/body/eval_jaxpr/ppermute | solution.py:12
  81.9 14.3 %collective-permute-start.1 = (f32[128,1152]{1,0:T(8,128)}, f32[128,1152]{1,0:T(8,128)S(1)}, u32[]{:S(2)}, u32[]{:S(2)}) collective-permute-start(f32[128,1152]{1,0:T(8,128)} %convolution_add_fusion.6), channel_id=1, source_target_pairs={{240,0},{0,16},{16,32},{32,48},{48,64},{64,80},{80,96},{96,112},{1... | collective-permute-start | bytes 1769480 | tf_op jit(solution)/shard_map/while/body/eval_jaxpr/ppermute | solution.py:12
  123.0 15.7 %collective-permute-start.1 = (f32[128,1152]{1,0:T(8,128)}, f32[128,1152]{1,0:T(8,128)S(1)}, u32[]{:S(2)}, u32[]{:S(2)}) collective-permute-start(f32[128,1152]{1,0:T(8,128)} %convolution_add_fusion.6), channel_id=1, source_target_pairs={{240,0},{0,16},{16,32},{32,48},{48,64},{64,80},{80,96},{96,112},{1... | collective-permute-start | bytes 1769480 | tf_op jit(solution)/shard_map/while/body/eval_jaxpr/ppermute | solution.py:12
  145.0 16.4 %collective-permute-start.1 = (f32[128,1152]{1,0:T(8,128)}, f32[128,1152]{1,0:T(8,128)S(1)}, u32[]{:S(2)}, u32[]{:S(2)}) collective-permute-start(f32[128,1152]{1,0:T(8,128)} %convolution_add_fusion.6), channel_id=1, source_target_pairs={{240,0},{0,16},{16,32},{32,48},{48,64},{64,80},{80,96},{96,112},{1... | collective-permute-start | bytes 1769480 | tf_op jit(solution)/shard_map/while/body/eval_jaxpr/ppermute | solution.py:12
  167.7 16.4 %collective-permute-start.1 = (f32[128,1152]{1,0:T(8,128)}, f32[128,1152]{1,0:T(8,128)S(1)}, u32[]{:S(2)}, u32[]{:S(2)}) collective-permute-start(f32[128,1152]{1,0:T(8,128)} %convolution_add_fusion.6), channel_id=1, source_target_pairs={{240,0},{0,16},{16,32},{32,48},{48,64},{64,80},{80,96},{96,112},{1... | collective-permute-start | bytes 1769480 | tf_op jit(solution)/shard_map/while/body/eval_jaxpr/ppermute | solution.py:12
  168.2 15.4 %collective-permute-start = (bf16[128,1152]{1,0:T(8,128)(2,1)S(1)}, bf16[128,1152]{1,0:T(8,128)(2,1)}, u32[]{:S(2)}, u32[]{:S(2)}) collective-permute-start(bf16[128,1152]{1,0:T(8,128)(2,1)S(1)} %copy.21), channel_id=1, source_target_pairs={{240,0},{0,16},{16,32},{32,48},{48,64},{64,80},{80,96},{96,112},{1... | collective-permute-start | bytes 884744 | tf_op jit(solution)/shard_map/while/body/eval_jaxpr/ppermute | solution.py:12
  190.3 16.4 %collective-permute-start.1 = (f32[128,1152]{1,0:T(8,128)}, f32[128,1152]{1,0:T(8,128)S(1)}, u32[]{:S(2)}, u32[]{:S(2)}) collective-permute-start(f32[128,1152]{1,0:T(8,128)} %convolution_add_fusion.6), channel_id=1, source_target_pairs={{240,0},{0,16},{16,32},{32,48},{48,64},{64,80},{80,96},{96,112},{1... | collective-permute-start | bytes 1769480 | tf_op jit(solution)/shard_map/while/body/eval_jaxpr/ppermute | solution.py:12
  190.3 15.9 %collective-permute-start = (bf16[128,1152]{1,0:T(8,128)(2,1)S(1)}, bf16[128,1152]{1,0:T(8,128)(2,1)}, u32[]{:S(2)}, u32[]{:S(2)}) collective-permute-start(bf16[128,1152]{1,0:T(8,128)(2,1)S(1)} %copy.21), channel_id=1, source_target_pairs={{240,0},{0,16},{16,32},{32,48},{48,64},{64,80},{80,96},{96,112},{1... | collective-permute-start | bytes 884744 | tf_op jit(solution)/shard_map/while/body/eval_jaxpr/ppermute | solution.py:12
  213.0 16.4 %collective-permute-start.1 = (f32[128,1152]{1,0:T(8,128)}, f32[128,1152]{1,0:T(8,128)S(1)}, u32[]{:S(2)}, u32[]{:S(2)}) collective-permute-start(f32[128,1152]{1,0:T(8,128)} %convolution_add_fusion.6), channel_id=1, source_target_pairs={{240,0},{0,16},{16,32},{32,48},{48,64},{64,80},{80,96},{96,112},{1... | collective-permute-start | bytes 1769480 | tf_op jit(solution)/shard_map/while/body/eval_jaxpr/ppermute | solution.py:12
  213.0 15.9 %collective-permute-start = (bf16[128,1152]{1,0:T(8,128)(2,1)S(1)}, bf16[128,1152]{1,0:T(8,128)(2,1)}, u32[]{:S(2)}, u32[]{:S(2)}) collective-permute-start(bf16[128,1152]{1,0:T(8,128)(2,1)S(1)} %copy.21), channel_id=1, source_target_pairs={{240,0},{0,16},{16,32},{32,48},{48,64},{64,80},{80,96},{96,112},{1... | collective-permute-start | bytes 884744 | tf_op jit(solution)/shard_map/while/body/eval_jaxpr/ppermute | solution.py:12
  235.7 16.4 %collective-permute-start.1 = (f32[128,1152]{1,0:T(8,128)}, f32[128,1152]{1,0:T(8,128)S(1)}, u32[]{:S(2)}, u32[]{:S(2)}) collective-permute-start(f32[128,1152]{1,0:T(8,128)} %convolution_add_fusion.6), channel_id=1, source_target_pairs={{240,0},{0,16},{16,32},{32,48},{48,64},{64,80},{80,96},{96,112},{1... | collective-permute-start | bytes 1769480 | tf_op jit(solution)/shard_map/while/body/eval_jaxpr/ppermute | solution.py:12
  235.7 15.9 %collective-permute-start = (bf16[128,1152]{1,0:T(8,128)(2,1)S(1)}, bf16[128,1152]{1,0:T(8,128)(2,1)}, u32[]{:S(2)}, u32[]{:S(2)}) collective-permute-start(bf16[128,1152]{1,0:T(8,128)(2,1)S(1)} %copy.21), channel_id=1, source_target_pairs={{240,0},{0,16},{16,32},{32,48},{48,64},{64,80},{80,96},{96,112},{1... | collective-permute-start | bytes 884744 | tf_op jit(solution)/shard_map/while/body/eval_jaxpr/ppermute | solution.py:12
  258.3 16.4 %collective-permute-start.1 = (f32[128,1152]{1,0:T(8,128)}, f32[128,1152]{1,0:T(8,128)S(1)}, u32[]{:S(2)}, u32[]{:S(2)}) collective-permute-start(f32[128,1152]{1,0:T(8,128)} %convolution_add_fusion.6), channel_id=1, source_target_pairs={{240,0},{0,16},{16,32},{32,48},{48,64},{64,80},{80,96},{96,112},{1... | collective-permute-start | bytes 1769480 | tf_op jit(solution)/shard_map/while/body/eval_jaxpr/ppermute | solution.py:12
  258.3 15.9 %collective-permute-start = (bf16[128,1152]{1,0:T(8,128)(2,1)S(1)}, bf16[128,1152]{1,0:T(8,128)(2,1)}, u32[]{:S(2)}, u32[]{:S(2)}) collective-permute-start(bf16[128,1152]{1,0:T(8,128)(2,1)S(1)} %copy.21), channel_id=1, source_target_pairs={{240,0},{0,16},{16,32},{32,48},{48,64},{64,80},{80,96},{96,112},{1... | collective-permute-start | bytes 884744 | tf_op jit(solution)/shard_map/while/body/eval_jaxpr/ppermute | solution.py:12
  281.0 16.4 %collective-permute-start.1 = (f32[128,1152]{1,0:T(8,128)}, f32[128,1152]{1,0:T(8,128)S(1)}, u32[]{:S(2)}, u32[]{:S(2)}) collective-permute-start(f32[128,1152]{1,0:T(8,128)} %convolution_add_fusion.6), channel_id=1, source_target_pairs={{240,0},{0,16},{16,32},{32,48},{48,64},{64,80},{80,96},{96,112},{1... | collective-permute-start | bytes 1769480 | tf_op jit(solution)/shard_map/while/body/eval_jaxpr/ppermute | solution.py:12
  281.0 15.9 %collective-permute-start = (bf16[128,1152]{1,0:T(8,128)(2,1)S(1)}, bf16[128,1152]{1,0:T(8,128)(2,1)}, u32[]{:S(2)}, u32[]{:S(2)}) collective-permute-start(bf16[128,1152]{1,0:T(8,128)(2,1)S(1)} %copy.21), channel_id=1, source_target_pairs={{240,0},{0,16},{16,32},{32,48},{48,64},{64,80},{80,96},{96,112},{1... | collective-permute-start | bytes 884744 | tf_op jit(solution)/shard_map/while/body/eval_jaxpr/ppermute | solution.py:12
  303.7 16.4 %collective-permute-start.1 = (f32[128,1152]{1,0:T(8,128)}, f32[128,1152]{1,0:T(8,128)S(1)}, u32[]{:S(2)}, u32[]{:S(2)}) collective-permute-start(f32[128,1152]{1,0:T(8,128)} %convolution_add_fusion.6), channel_id=1, source_target_pairs={{240,0},{0,16},{16,32},{32,48},{48,64},{64,80},{80,96},{96,112},{1... | collective-permute-start | bytes 1769480 | tf_op jit(solution)/shard_map/while/body/eval_jaxpr/ppermute | solution.py:12
  303.7 15.9 %collective-permute-start = (bf16[128,1152]{1,0:T(8,128)(2,1)S(1)}, bf16[128,1152]{1,0:T(8,128)(2,1)}, u32[]{:S(2)}, u32[]{:S(2)}) collective-permute-start(bf16[128,1152]{1,0:T(8,128)(2,1)S(1)} %copy.21), channel_id=1, source_target_pairs={{240,0},{0,16},{16,32},{32,48},{48,64},{64,80},{80,96},{96,112},{1... | collective-permute-start | bytes 884744 | tf_op jit(solution)/shard_map/while/body/eval_jaxpr/ppermute | solution.py:12
  326.3 16.4 %collective-permute-start.1 = (f32[128,1152]{1,0:T(8,128)}, f32[128,1152]{1,0:T(8,128)S(1)}, u32[]{:S(2)}, u32[]{:S(2)}) collective-permute-start(f32[128,1152]{1,0:T(8,128)} %convolution_add_fusion.6), channel_id=1, source_target_pairs={{240,0},{0,16},{16,32},{32,48},{48,64},{64,80},{80,96},{96,112},{1... | collective-permute-start | bytes 1769480 | tf_op jit(solution)/shard_map/while/body/eval_jaxpr/ppermute | solution.py:12
  326.3 15.9 %collective-permute-start = (bf16[128,1152]{1,0:T(8,128)(2,1)S(1)}, bf16[128,1152]{1,0:T(8,128)(2,1)}, u32[]{:S(2)}, u32[]{:S(2)}) collective-permute-start(bf16[128,1152]{1,0:T(8,128)(2,1)S(1)} %copy.21), channel_id=1, source_target_pairs={{240,0},{0,16},{16,32},{32,48},{48,64},{64,80},{80,96},{96,112},{1... | collective-permute-start | bytes 884744 | tf_op jit(solution)/shard_map/while/body/eval_jaxpr/ppermute | solution.py:12
  349.0 16.4 %collective-permute-start.1 = (f32[128,1152]{1,0:T(8,128)}, f32[128,1152]{1,0:T(8,128)S(1)}, u32[]{:S(2)}, u32[]{:S(2)}) collective-permute-start(f32[128,1152]{1,0:T(8,128)} %convolution_add_fusion.6), channel_id=1, source_target_pairs={{240,0},{0,16},{16,32},{32,48},{48,64},{64,80},{80,96},{96,112},{1... | collective-permute-start | bytes 1769480 | tf_op jit(solution)/shard_map/while/body/eval_jaxpr/ppermute | solution.py:12
  349.0 15.9 %collective-permute-start = (bf16[128,1152]{1,0:T(8,128)(2,1)S(1)}, bf16[128,1152]{1,0:T(8,128)(2,1)}, u32[]{:S(2)}, u32[]{:S(2)}) collective-permute-start(bf16[128,1152]{1,0:T(8,128)(2,1)S(1)} %copy.21), channel_id=1, source_target_pairs={{240,0},{0,16},{16,32},{32,48},{48,64},{64,80},{80,96},{96,112},{1... | collective-permute-start | bytes 884744 | tf_op jit(solution)/shard_map/while/body/eval_jaxpr/ppermute | solution.py:12
  (29 other events, 245.5 us)
Sparse Core Ops, SparseCore 0:
  371.4 281.9 all-reduce.2
where the time goes:
time: 684 us; the launch traced here: 680 us
  waiting for transfers between devices  355 us (52%)
  matrix products  126 us (18%)
  blocking collectives  90.8 us (13%)
  starting transfers between devices  36.4 us (5%)
  local copies, waits for them, and re-layouts  22.4 us (3%)
  other arithmetic  20.1 us (3%)
  between operations  19.3 us (3%)
  loops' own time  9.48 us (1%)
    psum x1, waiting for transfers between devices, local(): lax.psum((local_weight, local_bias, loss_sum), ('row', 'col'))  185 us
    ppermute x32, waiting for transfers between devices, passed_along(): return lax.ppermute(block, axis, route)  171 us
    psum x1, blocking collectives, local(): lax.psum((local_weight, local_bias, loss_sum), ('row', 'col'))  90.8 us
    dot_general x16, matrix products, tile_work(): jnp.dot(x_b, piece.T, preferred_element_type=jnp.float32)  50.5 us
    ppermute x32, starting transfers between devices, passed_along(): return lax.ppermute(block, axis, route)  36.3 us
    dot_general x16, matrix products, tile_work(): image_part = jnp.dot(weights, piece, preferred_element_type=jnp.float32)  35.1 us
    dot_general x16, matrix products, tile_work(): lax.dot_general(weights, x_b, (((0,), (0,)), ((), ())), preferred_element...  34.2 us
    while x48, local copies, waits for them, and re-layouts  15.5 us
  transfers between devices with their start and end apart: 33, of which 28 were waited for; matrix products, arithmetic and copies ran while one was open for 6% of the time, Pallas kernels for 0%

commit v1 on v0

v1 whole, which is shorter than its diff:
```python
import jax
import jax.numpy as jnp
from jax import lax
from jax.sharding import Mesh, PartitionSpec as P

EPS = 1e-06
ALL = ("x", "yh", "core", "z", "yl")
NX, NYH, NC, NZ, NYL = 4, 2, 2, 8, 2
F32, BF16 = jnp.float32, jnp.bfloat16


def place(x, yh, core, z, yl):
    return (((x * NYH + yh) * NC + core) * NZ + z) * NYL + yl


def groups_first():
    out = []
    for z in range(NZ):
        for yh in range(NYH):
            for yl in range(NYL):
                out.append([place(x, yh, 0, z, yl) for x in range(NX)])
        for x in range(NX):
            out.append([place(x, yh, 1, z, yl) for yh in range(NYH) for yl in range(NYL)])
    return out


def groups_second():
    out = []
    for x in range(NX):
        out.append([place(x, yh, 0, z, yl) for yh in range(NYH) for z in range(NZ) for yl in range(NYL)])
    for yh in range(NYH):
        for yl in range(NYL):
            out.append([place(x, yh, 1, z, yl) for x in range(NX) for z in range(NZ)])
    return out


def shifted(block, axis, distance):
    size = lax.axis_size(axis)
    return lax.ppermute(block, axis, [(i, (i + distance) % size) for i in range(size)])


def split_hi_lo(value):
    hi = value.astype(BF16)
    return hi, (value - hi.astype(F32)).astype(BF16)


def local(images, texts, head_weight, head_bias, logit_scale, logit_shift, loss_scale, clip_norm):
    own, d = images.shape
    total_rows = own * 256
    core = lax.axis_index("core")
    yc = ("yh", "core")
    txt = [texts] + [shifted(texts, "core", 1), shifted(texts, "yh", 1)]
    txt.append(lax.ppermute(texts, yc, [(0, 3), (1, 2), (2, 1), (3, 0)]))
    img = [images] + [shifted(images, "x", s) for s in (2, 1, 3)]
    t = jnp.concatenate(txt, 0)
    im = jnp.concatenate(img, 0).astype(F32)

    inv_x = lax.rsqrt(jnp.sum(im * im, axis=1, keepdims=True) + EPS)
    x_full = im * inv_x
    x_b = x_full.astype(BF16)
    u = jnp.dot(t, head_weight, preferred_element_type=F32) + head_bias
    inv_u = lax.rsqrt(jnp.sum(u * u, axis=1, keepdims=True) + EPS)
    y_full = u * inv_u
    y_b = y_full.astype(BF16)
    scale = logit_scale[0]
    z = scale * lax.dot_general(x_b, y_b, (((1,), (1,)), ((), ())), preferred_element_type=F32) + logit_shift[0]
    rows = lax.broadcasted_iota(jnp.int32, z.shape, 0)
    cols = lax.broadcasted_iota(jnp.int32, z.shape, 1)
    signs = jnp.where((rows == cols) & (rows < own), F32(1.0), F32(-1.0))
    v = -signs * z
    loss_part = jnp.sum(jax.nn.softplus(v))
    g = ((-loss_scale[0] / total_rows) * signs * jax.nn.sigmoid(v)).astype(BF16)
    dx = scale * jnp.dot(g, y_b, preferred_element_type=F32)
    dy = scale * lax.dot_general(g, x_b, (((0,), (0,)), ((), ())), preferred_element_type=F32)
    ig = (dx - x_full * jnp.sum(x_full * dx, axis=1, keepdims=True)) * inv_x
    du = (dy - y_full * jnp.sum(y_full * dy, axis=1, keepdims=True)) * inv_u
    bias_part = jnp.sum(du, axis=0)
    extra = jnp.concatenate([bias_part, loss_part[None], jnp.zeros((16 * 128 - d - 1,), F32)]).reshape(16, 128)
    hi, lo = split_hi_lo(extra)
    du_b = du.astype(BF16)
    half0 = du_b[:, :640]
    half1 = jnp.concatenate(
        [du_b[:, 640:], jnp.concatenate([hi, lo, jnp.zeros((480, 128), BF16)], 0)], 1
    )
    keep = jnp.where(core == 0, half0, half1)
    give = jnp.where(core == 0, half1, half0)
    got = shifted(give, "core", 1)
    tail = keep[:32, 512:].astype(F32) + got[:32, 512:].astype(F32)
    got = got.reshape(2, 2, own, 640)[:, ::-1].reshape(4 * own, 640)
    both = keep.astype(F32) + got.astype(F32)
    t_hi, t_lo = split_hi_lo(tail[:16] + tail[16:])
    rw = lax.dot_general(t, both.astype(BF16), (((0,), (0,)), ((), ())), preferred_element_type=F32).astype(BF16)
    block = jnp.zeros((1152, 128), BF16).at[:16].set(t_hi).at[16:32].set(t_lo)
    rw = jnp.concatenate([rw[:, :512], jnp.where(core == 0, rw[:, 512:], block)], 1)
    back = [ig[:own]] + [shifted(ig[own * k: own * (k + 1)].astype(BF16), "x", -s).astype(F32) for k, s in ((1, 2), (2, 1), (3, 3))]
    image_grad = back[0] + back[1] + back[2] + back[3]

    r1 = lax.all_to_all(rw.reshape(4, 288, 640), ALL, 0, 0, axis_index_groups=groups_first(), tiled=True)
    s1 = jnp.sum(r1.astype(F32), axis=0)
    pos1 = jnp.where(core == 0, lax.axis_index("x"), lax.axis_index(("yh", "yl")))
    flag = ((core == 1) & (pos1 == 0)).astype(F32)
    e_hi, e_lo = split_hi_lo((s1[:16, 512:] + s1[16:32, 512:]) * flag)
    tiles = s1.astype(BF16).reshape(18, 16, 5, 128).transpose(0, 2, 1, 3).reshape(1440, 128)
    zero16 = jnp.zeros((16, 128), BF16)
    tiles = jnp.concatenate([tiles, zero16, zero16, zero16, e_hi, e_lo, zero16], 0).reshape(32, 48, 128)
    r2 = lax.all_to_all(tiles, ALL, 0, 0, axis_index_groups=groups_second(), tiled=True)
    s2 = jnp.sum(r2.astype(F32), axis=0)
    pos2 = jnp.where(core == 0, lax.axis_index(("yh", "z", "yl")), lax.axis_index(("x", "z")))
    f_hi, f_lo = split_hi_lo(s2[:16] + s2[16:32])
    special = jnp.concatenate([f_hi, f_lo, zero16], 0)
    mine = jnp.where(pos2 == 31, special, s2.astype(BF16))
    a1 = lax.all_to_all(jnp.broadcast_to(mine, (32, 48, 128)), ALL, 0, 0, axis_index_groups=groups_second(), tiled=True)
    a2 = lax.all_to_all(jnp.broadcast_to(a1.reshape(1, 1536, 128), (4, 1536, 128)), ALL, 0, 0, axis_index_groups=groups_first(), tiled=True)
    other = shifted(a2, "core", 1)
    h0 = jnp.where(core == 0, a2, other)
    h1 = jnp.where(core == 0, other, a2)
    e = h1[0, 93 * 16:94 * 16].astype(F32) + h1[0, 94 * 16:95 * 16].astype(F32)
    ev = e.reshape(-1)
    raw_bias, loss_total = ev[:d], ev[d]

    def unpack(h):
        return h[:, :1440].reshape(4, 18, 5, 16, 128).transpose(0, 1, 3, 2, 4).reshape(1152, 640)

    raw_weight = jnp.concatenate([unpack(h0), unpack(h1)[:, :512]], 1).astype(F32)
    norm = jnp.sqrt(jnp.sum(raw_weight * raw_weight) + jnp.sum(raw_bias * raw_bias))
    factor = jnp.minimum(F32(1.0), clip_norm[0] / norm)
    return (image_grad, raw_weight * factor, raw_bias * factor, (loss_total / total_rows)[None])


def solution(mesh):
    fine = Mesh(mesh.devices.reshape(NX, NYH, NC, NZ, NYL), ALL)
    placed = (P(ALL, None), P(ALL, None), P(), P(), P(), P(), P(), P())
    return jax.shard_map(
        local, mesh=fine, in_specs=placed, out_specs=(P(ALL, None), P(), P(), P()), check_vma=False
    )
```

time: 684 us -> 171 us (0.25)
  waiting for transfers between devices: 355 us -> 57 us
  matrix products: 126 us -> 12.7 us
  blocking collectives: 90.8 us -> 18.7 us
  between operations: 19.3 us -> 6.84 us
  loops' own time: 9.48 us -> 0 us
    psum x1 -> x0, waiting for transfers between devices: 185 us -> none  [local(): lax.psum((local_weight, local_bias, loss_sum), ('row', 'col'))]
    ppermute x32 -> x11, waiting for transfers between devices: 171 us -> 22.6 us  [the longest x10 22.6 us: shifted(): lax.ppermute(block, axis, [(i, (i + distance) % size) for i in range(size)])]
    dot_general x50 -> x5, matrix products: 126 us -> 12.7 us  [the longest x1 4.56 us: local(): dx = scale * jnp.dot(g, y_b, preferred_element_type=F32)]
    psum x1 -> x0, blocking collectives: 90.8 us -> none  [local(): lax.psum((local_weight, local_bias, loss_sum), ('row', 'col'))]
    all_to_all x0 -> x3, waiting for transfers between devices: none -> 34.5 us  [the longest x1 14 us: local(): lax.all_to_all(tiles, ALL, 0, 0, axis_index_groups=groups_second(), tiled...]
    ppermute x32 -> x11, starting transfers between devices: 36.3 us -> 16.4 us  [the longest x10 15.5 us: shifted(): lax.ppermute(block, axis, [(i, (i + distance) % size) for i in range(size)])]
    all_to_all x0 -> x3, starting transfers between devices: none -> 19.1 us  [the longest x1 10.3 us: local(): lax.all_to_all(tiles, ALL, 0, 0, axis_index_groups=groups_second(), tiled...]
    all_to_all x0 -> x1, blocking collectives: none -> 18.7 us  [local(): lax.all_to_all(jnp.broadcast_to(mine, (32, 48, 128)), ALL, 0, 0, axis_ind...]
  transfers between devices with their start and end apart: 33 -> 14, of which waited for: 28 -> 8; matrix products, arithmetic and copies ran while one was open for 6% -> 7% of each run, Pallas kernels for 0% -> 0%
where the time goes in v1:
time: 171 us; the launch traced here: 170 us
  waiting for transfers between devices  57 us (33%)
  starting transfers between devices  35.5 us (21%)
  other arithmetic  22.5 us (13%)
  blocking collectives  18.7 us (11%)
  local copies, waits for them, and re-layouts  17 us (10%)
  matrix products  12.7 us (7%)
  between operations  6.84 us (4%)
    ppermute x10, waiting for transfers between devices, shifted(): lax.ppermute(block, axis, [(i, (i + distance) % size) for i in range(size)])  22.6 us
    all_to_all x1, blocking collectives, local(): lax.all_to_all(jnp.broadcast_to(mine, (32, 48, 128)), ALL, 0, 0, axis_ind...  18.7 us
    ppermute x10, starting transfers between devices, shifted(): lax.ppermute(block, axis, [(i, (i + distance) % size) for i in range(size)])  15.5 us
    all_to_all x1, waiting for transfers between devices, local(): lax.all_to_all(tiles, ALL, 0, 0, axis_index_groups=groups_second(), tiled...  14 us
    all_to_all x1, waiting for transfers between devices, local(): lax.all_to_all(rw.reshape(4, 288, 640), ALL, 0, 0, axis_index_groups=grou...  12.2 us
    all_to_all x1, starting transfers between devices, local(): lax.all_to_all(tiles, ALL, 0, 0, axis_index_groups=groups_second(), tiled...  10.3 us
    all_to_all x1, waiting for transfers between devices, local(): lax.all_to_all(jnp.broadcast_to(a1.reshape(1, 1536, 128), (4, 1536, 128))...  8.3 us
    unnamed x45, local copies, waits for them, and re-layouts  6.26 us
  transfers between devices with their start and end apart: 14, of which 8 were waited for; matrix products, arithmetic and copies ran while one was open for 7% of the time, Pallas kernels for 0%

profile of v1, /device:TPU:1, one launch (start us, length us, event | category | flops | bytes accessed | tf_op | source)
XLA Modules:
  0.0 170.4 jit_solution(18347281796048960820)
XLA Ops:
  0.7 3.8 %collective-permute-start.4 = (bf16[128,1152]{1,0:T(8,128)(2,1)}, bf16[128,1152]{1,0:T(8,128)(2,1)}, u32[]{:S(2)}, u32[]{:S(2)}) collective-permute-start(bf16[128,1152]{1,0:T(8,128)(2,1)} %param.13), channel_id=1, source_target_pairs={{0,32},{32,0},{1,33},{33,1},{2,34},{34,2},{3,35},{35,3},{4,36},{36... | collective-permute-start | bytes 884744 | tf_op jit(solution)/shard_map/ppermute | solution.py:39
  6.7 2.5 %collective-permute-start = (bf16[128,1152]{1,0:T(8,128)(2,1)}, bf16[128,1152]{1,0:T(8,128)(2,1)S(1)}, u32[]{:S(2)}, u32[]{:S(2)}) collective-permute-start(bf16[128,1152]{1,0:T(8,128)(2,1)} %param.12), channel_id=1, source_target_pairs={{0,128},{64,192},{128,0},{192,64},{1,129},{65,193},{129,1},{193,65... | collective-permute-start | bytes 884744 | tf_op jit(solution)/shard_map/ppermute | solution.py:39
  15.5 7.3 %collective-permute-done = bf16[128,1152]{1,0:T(8,128)(2,1)S(1)} collective-permute-done((bf16[128,1152]{1,0:T(8,128)(2,1)}, bf16[128,1152]{1,0:T(8,128)(2,1)S(1)}, u32[]{:S(2)}, u32[]{:S(2)}) %collective-permute-start) | collective-permute-done | bytes 294944 | tf_op jit(solution)/shard_map/ppermute | solution.py:39
  25.4 2.0 %multiply_reduce_fusion.1 = (f32[512]{0:T(512)S(1)}, f32[512,1152]{1,0:T(8,128)S(1)}) fusion(f32[1152]{0:T(1024)S(1)} %copy-done.15, bf16[512,1152]{1,0:T(8,128)(2,1)S(1)} %constant_dynamic-update-slice_fusion, bf16[1152,1152]{1,0:T(8,128)(2,1)S(1)} %copy-done), kind=kOutput, calls=%fused_computation.21 | convolution fusion | flops 1360723456 | bytes 6199808 | tf_op jit(solution)/shard_map/dot_general | solution.py:61
  27.4 2.2 %fusion.13 = (f32[]{:T(128)}, f32[512,512]{1,0:T(8,128)S(1)}) fusion(f32[]{:T(128)} %bitcast.45, f32[512,1152]{1,0:T(8,128)S(1)} %get-tuple-element.44, f32[512]{0:T(512)S(1)} %add_rsqrt_fusion, f32[512]{0:T(512)S(1)} %add_rsqrt_fusion.1, bf16[128,1152]{1,0:T(8,128)(2,1)S(1)} %collective-permute-done.2, bf16[128,1152]{1,0:T(8,128)(2,1)S(1)} %collective-permute-done.1, ...), kind=kOutput, calls=%fused_computation.38 | convolution fusion | flops 614727680 | bytes 4592140 | tf_op jit(solution)/shard_map/dot_general | solution.py:66
  36.5 1.7 %collective-permute-done.9 = bf16[512,640]{1,0:T(8,128)(2,1)S(1)} collective-permute-done((bf16[512,640]{1,0:T(8,128)(2,1)S(1)}, bf16[512,640]{1,0:T(8,128)(2,1)S(1)}, u32[]{:S(2)}, u32[]{:S(2)}) %collective-permute-start.9) | collective-permute-done | bytes 655392 | tf_op jit(solution)/shard_map/ppermute | solution.py:39
  39.1 2.0 %rev.3 = bf16[2,2,128,640]{3,2,1,0:T(8,128)(2,1)} reverse(bf16[2,2,128,640]{3,2,1,0:T(8,128)(2,1)} %bitcast.59), dimensions={1} | reverse | bytes 1310720 | tf_op jit(solution)/shard_map/rev | solution.py:89
  41.1 2.8 %convolution_convert_fusion = bf16[1152,640]{1,0:T(8,128)(2,1)S(1)} fusion(bf16[512,1152]{1,0:T(8,128)(2,1)} %copy-done.14, bf16[512,640]{1,0:T(8,128)(2,1)} %bitcast.60, bf16[512,640]{1,0:T(8,128)(2,1)} %copy-done.13), kind=kOutput, calls=%fused_computation.6 | convolution fusion | flops 757022720 | bytes 3964928 | tf_op jit(solution)/shard_map/dot_general | solution.py:92
  45.2 4.5 %all-to-all-start = ((bf16[4,288,640]{2,1,0:T(8,128)(2,1)}), bf16[4,288,640]{2,1,0:T(8,128)(2,1)}, u32[]{:S(2)}, u32[]{:S(2)}) async-start(bf16[4,288,640]{2,1,0:T(8,128)(2,1)} %bitcast.51), calls=%async_computation | async-start | bytes 2949120 | tf_op jit(solution)/shard_map/all_to_all | solution.py:98
  49.7 12.2 %all-to-all-done = bf16[4,288,640]{2,1,0:T(8,128)(2,1)} async-done(((bf16[4,288,640]{2,1,0:T(8,128)(2,1)}), bf16[4,288,640]{2,1,0:T(8,128)(2,1)}, u32[]{:S(2)}, u32[]{:S(2)}) %all-to-all-start) | async-done | bytes 1474592 | tf_op jit(solution)/shard_map/all_to_all | solution.py:98
  64.4 2.2 %convert_element_type.141 = bf16[18,16,5,128]{3,2,1,0:T(8,128)(2,1)} reshape(bf16[288,640]{1,0:T(8,128)(2,1)} %convert_element_type.140) | data formatting | bytes 737280 | tf_op jit(solution)/shard_map/convert_element_type | solution.py:103
  68.5 10.3 %all-to-all-start.1 = ((bf16[32,48,128]{2,1,0:T(8,128)(2,1)}), bf16[32,48,128]{2,1,0:T(8,128)(2,1)S(1)}, u32[]{:S(2)}, u32[]{:S(2)}) async-start(bf16[32,48,128]{2,1,0:T(8,128)(2,1)} %bitcast.57), calls=%async_computation.1 | async-start | bytes 786432 | tf_op jit(solution)/shard_map/all_to_all | solution.py:106
  78.8 14.0 %all-to-all-done.1 = bf16[32,48,128]{2,1,0:T(8,128)(2,1)S(1)} async-done(((bf16[32,48,128]{2,1,0:T(8,128)(2,1)}), bf16[32,48,128]{2,1,0:T(8,128)(2,1)S(1)}, u32[]{:S(2)}, u32[]{:S(2)}) %all-to-all-start.1) | async-done | bytes 393248 | tf_op jit(solution)/shard_map/all_to_all | solution.py:106
  93.0 18.7 %all_to_all.20 = bf16[32,48,128]{2,1,0:T(8,128)(2,1)S(1)} all-to-all(bf16[32,48,128]{2,1,0:T(8,128)(2,1)S(1)} %broadcast_in_dim.40), channel_id=1, replica_groups={{0,1,2,3,4,5,6,7,8,9,10,11,12,13,14,15,32,33,34,35,36,37,38,39,40,41,42..., dimensions={0} | all-to-all | bytes 786432 | tf_op jit(solution)/shard_map/all_to_all | solution.py:112
  113.1 4.3 %all-to-all-start.3 = ((bf16[4,1536,128]{2,1,0:T(8,128)(2,1)}), bf16[4,1536,128]{2,1,0:T(8,128)(2,1)}, u32[]{:S(2)}, u32[]{:S(2)}) async-start(bf16[4,1536,128]{2,1,0:T(8,128)(2,1)} %broadcast_in_dim.42), calls=%async_computation.3 | async-start | bytes 3145728 | tf_op jit(solution)/shard_map/all_to_all | solution.py:113
  117.5 4.6 %fusion.4 = (f32[512]{0:T(512)S(1)}, f32[512,1152]{1,0:T(8,128)}) fusion(f32[512]{0:T(512)S(1)} %add_rsqrt_fusion.1, bf16[128,1152]{1,0:T(8,128)(2,1)} %copy-done.11, bf16[128,1152]{1,0:T(8,128)(2,1)S(1)} %copy-done.8, bf16[128,1152]{1,0:T(8,128)(2,1)S(1)} %copy-done.10, bf16[128,1152]{1,0:T(8,128)(2,1)S(1)} %copy-done.6, f32[512,1152]{1,0:T(8,128)} %copy-done.3, ...), kind=kOutput, calls=%fused_computation.15 | convolution fusion | flops 614596096 | bytes 6953480 | tf_op jit(solution)/shard_map/dot_general | solution.py:73
  122.1 8.3 %all-to-all-done.3 = bf16[4,1536,128]{2,1,0:T(8,128)(2,1)} async-done(((bf16[4,1536,128]{2,1,0:T(8,128)(2,1)}), bf16[4,1536,128]{2,1,0:T(8,128)(2,1)}, u32[]{:S(2)}, u32[]{:S(2)}) %all-to-all-start.3) | async-done | bytes 1572896 | tf_op jit(solution)/shard_map/all_to_all | solution.py:113
  130.4 2.0 %collective-permute-start.10 = (bf16[4,1536,128]{2,1,0:T(8,128)(2,1)}, bf16[4,1536,128]{2,1,0:T(8,128)(2,1)S(1)}, u32[]{:S(2)}, u32[]{:S(2)}) collective-permute-start(bf16[4,1536,128]{2,1,0:T(8,128)(2,1)} %all-to-all-done.3), channel_id=1, source_target_pairs={{0,16},{16,0},{1,17},{17,1},{2,18},{18,2},{3,19},{19,3},{4,20},{20... | collective-permute-start | bytes 4718600 | tf_op jit(solution)/shard_map/ppermute | solution.py:39
  132.4 2.2 %fusion.31 = (bf16[512,1152]{1,0:T(8,128)(2,1)S(1)}, f32[512,1152]{1,0:T(8,128)S(1)}) fusion(f32[512,1152]{1,0:T(8,128)} %get-tuple-element.46, f32[512]{0:T(512)S(1)} %get-tuple-element.45, f32[512]{0:T(512)S(1)} %add_rsqrt_fusion.1, bf16[128,1152]{1,0:T(8,128)(2,1)} %copy-done.11, bf16[128,1152]{1,0:T(8,128)(2,1)S(1)} %copy-done.8, ...), kind=kLoop, calls=%fused_computation.82 | loop fusion | flops 7667712 | bytes 7081984 | tf_op jit(solution)/shard_map/convert.3
  138.3 6.6 %collective-permute-done.6 = bf16[128,1152]{1,0:T(8,128)(2,1)S(1)} collective-permute-done((bf16[128,1152]{1,0:T(8,128)(2,1)S(1)}, bf16[128,1152]{1,0:T(8,128)(2,1)S(1)}, u32[]{:S(2)}, u32[]{:S(2)}) %collective-permute-start.6) | collective-permute-done | bytes 294944 | tf_op jit(solution)/shard_map/ppermute | solution.py:39
  144.9 6.5 %collective-permute-done.8 = bf16[128,1152]{1,0:T(8,128)(2,1)S(1)} collective-permute-done((bf16[128,1152]{1,0:T(8,128)(2,1)S(1)}, bf16[128,1152]{1,0:T(8,128)(2,1)S(1)}, u32[]{:S(2)}, u32[]{:S(2)}) %collective-permute-start.8) | collective-permute-done | bytes 294944 | tf_op jit(solution)/shard_map/ppermute | solution.py:39
  155.7 2.0 %slice_select_fusion = bf16[4,1440,128]{2,1,0:T(8,128)(2,1)S(1)} fusion(bf16[4,1536,128]{2,1,0:T(8,128)(2,1)S(1)} %collective-permute-done.10, bf16[4,1536,128]{2,1,0:T(8,128)(2,1)} %all-to-all-done.3, pred[]{:T(512)S(6)} %eq.24), kind=kLoop, calls=%fused_computation.26 | loop fusion | flops 737280 | bytes 4423681 | tf_op jit(solution)/shard_map/jit(_where)/select_n | solution.py:115
  159.7 2.0 %fusion = f32[]{:T(128)} fusion(bf16[1152,512]{1,0:T(8,128)(2,1)S(1)} %slice.149, bf16[1152,640]{1,0:T(8,128)(2,1)S(1)} %bitcast.47), kind=kLoop, calls=%fused_computation.2 | loop fusion | flops 7962623 | bytes 2654212 | tf_op jit(solution)/shard_map/reduce_sum | solution.py:125
  163.6 4.5 %convert_multiply_fusion = f32[1152,1152]{1,0:T(8,128)} fusion(f32[]{:T(128)S(6)} %min.3, bf16[1152,512]{1,0:T(8,128)(2,1)} %copy-done.2, bf16[1152,640]{1,0:T(8,128)(2,1)} %bitcast.48), kind=kLoop, calls=%fused_computation | loop fusion | flops 6635520 | bytes 7962628 | tf_op jit(solution)/shard_map/mul | solution.py:127
  (103 shorter events, 34.6 us)
Async XLA Ops:
  0.6 24.7 %copy-start = (bf16[1152,1152]{1,0:T(8,128)(2,1)S(1)}, bf16[1152,1152]{1,0:T(8,128)(2,1)}, u32[]{:S(2)}) copy-start(bf16[1152,1152]{1,0:T(8,128)(2,1)} %param.14) | copy-start | bytes 7962628
  0.6 24.7 %copy-start.15 = (f32[1152]{0:T(1024)S(1)}, f32[1152]{0:T(1024)}, u32[]{:S(2)}) copy-start(f32[1152]{0:T(1024)} %param.15) | copy-start | bytes 13828
  0.7 23.7 %collective-permute-start.4 = (bf16[128,1152]{1,0:T(8,128)(2,1)}, bf16[128,1152]{1,0:T(8,128)(2,1)}, u32[]{:S(2)}, u32[]{:S(2)}) collective-permute-start(bf16[128,1152]{1,0:T(8,128)(2,1)} %param.13), channel_id=1, source_target_pairs={{0,32},{32,0},{1,33},{33,1},{2,34},{34,2},{3,35},{35,3},{4,36},{36... | collective-permute-start | bytes 884744 | tf_op jit(solution)/shard_map/ppermute | solution.py:39
  4.5 8.7 %collective-permute-start.3 = (bf16[128,1152]{1,0:T(8,128)(2,1)}, bf16[128,1152]{1,0:T(8,128)(2,1)}, u32[]{:S(2)}, u32[]{:S(2)}) collective-permute-start(bf16[128,1152]{1,0:T(8,128)(2,1)} %param.13), channel_id=1, source_target_pairs={{0,16},{16,0},{1,17},{17,1},{2,18},{18,2},{3,19},{19,3},{4,20},{20... | collective-permute-start | bytes 884744 | tf_op jit(solution)/shard_map/ppermute | solution.py:39
  5.4 10.1 %collective-permute-start.1 = (bf16[128,1152]{1,0:T(8,128)(2,1)}, bf16[128,1152]{1,0:T(8,128)(2,1)S(1)}, u32[]{:S(2)}, u32[]{:S(2)}) collective-permute-start(bf16[128,1152]{1,0:T(8,128)(2,1)} %param.12), channel_id=1, source_target_pairs={{0,64},{64,128},{128,192},{192,0},{1,65},{65,129},{129,193},{193,1... | collective-permute-start | bytes 884744 | tf_op jit(solution)/shard_map/ppermute | solution.py:39
  6.7 16.2 %collective-permute-start = (bf16[128,1152]{1,0:T(8,128)(2,1)}, bf16[128,1152]{1,0:T(8,128)(2,1)S(1)}, u32[]{:S(2)}, u32[]{:S(2)}) collective-permute-start(bf16[128,1152]{1,0:T(8,128)(2,1)} %param.12), channel_id=1, source_target_pairs={{0,128},{64,192},{128,0},{192,64},{1,129},{65,193},{129,1},{193,65... | collective-permute-start | bytes 884744 | tf_op jit(solution)/shard_map/ppermute | solution.py:39
  9.1 13.7 %collective-permute-start.2 = (bf16[128,1152]{1,0:T(8,128)(2,1)}, bf16[128,1152]{1,0:T(8,128)(2,1)S(1)}, u32[]{:S(2)}, u32[]{:S(2)}) collective-permute-start(bf16[128,1152]{1,0:T(8,128)(2,1)} %param.12), channel_id=1, source_target_pairs={{0,192},{64,0},{128,64},{192,128},{1,193},{65,1},{129,65},{193,129... | collective-permute-start | bytes 884744 | tf_op jit(solution)/shard_map/ppermute | solution.py:39
  13.2 16.4 %copy-start.16 = (pred[512]{0:T(512)(128)(4,1)}, pred[512]{0:T(512)(128)(4,1)S(1)}, u32[]{:S(2)}) copy-start(pred[512]{0:T(512)(128)(4,1)S(1)} %iota_compare_fusion.1) | copy-start | bytes 1540
  13.2 12.1 %collective-permute-start.5 = (bf16[128,1152]{1,0:T(8,128)(2,1)}, bf16[128,1152]{1,0:T(8,128)(2,1)S(1)}, u32[]{:S(2)}, u32[]{:S(2)}) collective-permute-start(bf16[128,1152]{1,0:T(8,128)(2,1)} %param.13), channel_id=1, source_target_pairs={{0,48},{16,32},{32,16},{48,0},{1,49},{17,33},{33,17},{49,1},{2,50}... | collective-permute-start | bytes 884744 | tf_op jit(solution)/shard_map/ppermute | solution.py:53
  15.5 14.1 %copy-start.7 = (bf16[128,1152]{1,0:T(8,128)(2,1)}, bf16[128,1152]{1,0:T(8,128)(2,1)S(1)}, u32[]{:S(2)}) copy-start(bf16[128,1152]{1,0:T(8,128)(2,1)S(1)} %collective-permute-done.1) | copy-start | bytes 884740
  22.8 6.8 %copy-start.9 = (bf16[128,1152]{1,0:T(8,128)(2,1)}, bf16[128,1152]{1,0:T(8,128)(2,1)S(1)}, u32[]{:S(2)}) copy-start(bf16[128,1152]{1,0:T(8,128)(2,1)S(1)} %collective-permute-done) | copy-start | bytes 884740
  22.8 6.8 %copy-start.11 = (bf16[128,1152]{1,0:T(8,128)(2,1)}, bf16[128,1152]{1,0:T(8,128)(2,1)S(1)}, u32[]{:S(2)}) copy-start(bf16[128,1152]{1,0:T(8,128)(2,1)S(1)} %collective-permute-done.2) | copy-start | bytes 884740
  35.6 2.6 %collective-permute-start.9 = (bf16[512,640]{1,0:T(8,128)(2,1)S(1)}, bf16[512,640]{1,0:T(8,128)(2,1)S(1)}, u32[]{:S(2)}, u32[]{:S(2)}) collective-permute-start(bf16[512,640]{1,0:T(8,128)(2,1)S(1)} %get-tuple-element.37), channel_id=1, source_target_pairs={{0,16},{16,0},{1,17},{17,1},{2,18},{18,2},{3,19},{19,3},{4,20},{20... | collective-permute-start | bytes 1966088 | tf_op jit(solution)/shard_map/ppermute | solution.py:39
  45.2 16.7 %all-to-all-start = ((bf16[4,288,640]{2,1,0:T(8,128)(2,1)}), bf16[4,288,640]{2,1,0:T(8,128)(2,1)}, u32[]{:S(2)}, u32[]{:S(2)}) async-start(bf16[4,288,640]{2,1,0:T(8,128)(2,1)} %bitcast.51), calls=%async_computation | async-start | bytes 2949120 | tf_op jit(solution)/shard_map/all_to_all | solution.py:98
  68.5 24.3 %all-to-all-start.1 = ((bf16[32,48,128]{2,1,0:T(8,128)(2,1)}), bf16[32,48,128]{2,1,0:T(8,128)(2,1)S(1)}, u32[]{:S(2)}, u32[]{:S(2)}) async-start(bf16[32,48,128]{2,1,0:T(8,128)(2,1)} %bitcast.57), calls=%async_computation.1 | async-start | bytes 786432 | tf_op jit(solution)/shard_map/all_to_all | solution.py:106
  111.7 5.8 %copy-start.6 = (bf16[128,1152]{1,0:T(8,128)(2,1)S(1)}, bf16[128,1152]{1,0:T(8,128)(2,1)}, u32[]{:S(2)}) copy-start(bf16[128,1152]{1,0:T(8,128)(2,1)} %param.12) | copy-start | bytes 884740
  111.7 5.8 %copy-start.8 = (bf16[128,1152]{1,0:T(8,128)(2,1)S(1)}, bf16[128,1152]{1,0:T(8,128)(2,1)}, u32[]{:S(2)}) copy-start(bf16[128,1152]{1,0:T(8,128)(2,1)} %copy-done.7) | copy-start | bytes 884740
  111.7 5.8 %copy-start.10 = (bf16[128,1152]{1,0:T(8,128)(2,1)S(1)}, bf16[128,1152]{1,0:T(8,128)(2,1)}, u32[]{:S(2)}) copy-start(bf16[128,1152]{1,0:T(8,128)(2,1)} %copy-done.9) | copy-start | bytes 884740
  111.7 5.8 %copy-start.17 = (pred[512]{0:T(512)(128)(4,1)S(1)}, pred[512]{0:T(512)(128)(4,1)}, u32[]{:S(2)}) copy-start(pred[512]{0:T(512)(128)(4,1)} %copy-done.16) | copy-start | bytes 1540
  113.1 17.3 %all-to-all-start.3 = ((bf16[4,1536,128]{2,1,0:T(8,128)(2,1)}), bf16[4,1536,128]{2,1,0:T(8,128)(2,1)}, u32[]{:S(2)}, u32[]{:S(2)}) async-start(bf16[4,1536,128]{2,1,0:T(8,128)(2,1)} %broadcast_in_dim.42), calls=%async_computation.3 | async-start | bytes 3145728 | tf_op jit(solution)/shard_map/all_to_all | solution.py:113
  130.4 22.0 %collective-permute-start.10 = (bf16[4,1536,128]{2,1,0:T(8,128)(2,1)}, bf16[4,1536,128]{2,1,0:T(8,128)(2,1)S(1)}, u32[]{:S(2)}, u32[]{:S(2)}) collective-permute-start(bf16[4,1536,128]{2,1,0:T(8,128)(2,1)} %all-to-all-done.3), channel_id=1, source_target_pairs={{0,16},{16,0},{1,17},{17,1},{2,18},{18,2},{3,19},{19,3},{4,20},{20... | collective-permute-start | bytes 4718600 | tf_op jit(solution)/shard_map/ppermute | solution.py:39
  134.6 10.3 %collective-permute-start.6 = (bf16[128,1152]{1,0:T(8,128)(2,1)S(1)}, bf16[128,1152]{1,0:T(8,128)(2,1)S(1)}, u32[]{:S(2)}, u32[]{:S(2)}) collective-permute-start(bf16[128,1152]{1,0:T(8,128)(2,1)S(1)} %get-tuple-element.40), channel_id=1, source_target_pairs={{0,128},{64,192},{128,0},{192,64},{1,129},{65,193},{129,1},{193,65... | collective-permute-start | bytes 884744 | tf_op jit(solution)/shard_map/ppermute | solution.py:39
  135.0 16.4 %collective-permute-start.8 = (bf16[128,1152]{1,0:T(8,128)(2,1)S(1)}, bf16[128,1152]{1,0:T(8,128)(2,1)S(1)}, u32[]{:S(2)}, u32[]{:S(2)}) collective-permute-start(bf16[128,1152]{1,0:T(8,128)(2,1)S(1)} %get-tuple-element.41), channel_id=1, source_target_pairs={{0,64},{64,128},{128,192},{192,0},{1,65},{65,129},{129,193},{193,1... | collective-permute-start | bytes 884744 | tf_op jit(solution)/shard_map/ppermute | solution.py:39
  136.2 15.3 %collective-permute-start.7 = (bf16[128,1152]{1,0:T(8,128)(2,1)S(1)}, bf16[128,1152]{1,0:T(8,128)(2,1)S(1)}, u32[]{:S(2)}, u32[]{:S(2)}) collective-permute-start(bf16[128,1152]{1,0:T(8,128)(2,1)S(1)} %get-tuple-element.42), channel_id=1, source_target_pairs={{0,192},{64,0},{128,64},{192,128},{1,193},{65,1},{129,65},{193,129... | collective-permute-start | bytes 884744 | tf_op jit(solution)/shard_map/ppermute | solution.py:39
  (9 other events, 17.1 us)

commit v2 on v1

v2 whole, which is shorter than its diff:
```python
import jax
import jax.numpy as jnp
from jax import lax
from jax.experimental import pallas as pl
from jax.experimental.pallas import tpu as pltpu
from jax.sharding import Mesh, PartitionSpec as P

EPS = 1e-06
ALL = ("x", "yh", "core", "z", "yl")
NX, NYH, NC, NZ, NYL = 4, 2, 2, 8, 2
F32, BF16 = jnp.float32, jnp.bfloat16
D, OWN = 1152, 128
WIDE = 640
PART = 288
TILES = 96
ONE = 16
TOTAL = 32768
BIG = pltpu.CompilerParams(vmem_limit_bytes=48 * 2**20)
VMEM = pl.BlockSpec(memory_space=pltpu.VMEM)
SMEM = pl.BlockSpec(memory_space=pltpu.SMEM)


def place(x, yh, core, z, yl):
    return (((x * NYH + yh) * NC + core) * NZ + z) * NYL + yl


def every():
    return [
        (x, yh, core, z, yl)
        for x in range(NX) for yh in range(NYH) for core in range(NC) for z in range(NZ) for yl in range(NYL)
    ]


def groups_second():
    out = []
    for x in range(NX):
        out.append([place(x, yh, 0, z, yl) for yh in range(NYH) for z in range(NZ) for yl in range(NYL)])
    for yh in range(NYH):
        for yl in range(NYL):
            out.append([place(x, yh, 1, z, yl) for x in range(NX) for z in range(NZ)])
    return out


def around(distance):
    route = []
    for x, yh, core, z, yl in every():
        if core == 0:
            to = place((x + distance) % NX, yh, core, z, yl)
        else:
            y = (2 * yh + yl + distance) % 4
            to = place(x, y // 2, core, z, y % 2)
        route.append((place(x, yh, core, z, yl), to))
    return route


def shifted(block, axis, distance):
    size = lax.axis_size(axis)
    return lax.ppermute(block, axis, [(i, (i + distance) % size) for i in range(size)])


def hi_lo(value):
    hi = value.astype(BF16)
    return hi, (value - hi.astype(F32)).astype(BF16)


def text_kernel(t0, t1, t2, t3, w_ref, b_ref, y_ref, inv_ref):
    for k, ref in enumerate((t0, t1, t2, t3)):
        rows = slice(k * OWN, (k + 1) * OWN)
        u = jnp.dot(ref[...], w_ref[...], preferred_element_type=F32) + b_ref[...]
        inv = lax.rsqrt(jnp.sum(u * u, axis=1, keepdims=True) + EPS)
        y_ref[rows, :] = u * inv
        inv_ref[rows, :] = jnp.broadcast_to(inv, (OWN, 128))


def pair_kernel(core_ref, scal_ref, i0, i1, i2, i3, y_ref, invu_ref,
                g0, g1, g2, g3, keep_ref, give_ref, xb, yb, gs, invx, ext):
    scale, shift, gfac = scal_ref[0], scal_ref[1], scal_ref[2]
    images = (i0, i1, i2, i3)
    for k, ref in enumerate(images):
        rows = slice(k * OWN, (k + 1) * OWN)
        full = ref[...].astype(F32)
        inv = lax.rsqrt(jnp.sum(full * full, axis=1, keepdims=True) + EPS)
        invx[rows, :] = jnp.broadcast_to(inv, (OWN, 128))
        xb[rows, :] = (full * inv).astype(BF16)
        yb[rows, :] = y_ref[rows, :].astype(BF16)
    loss = jnp.zeros((1, 1), F32)
    for h in range(2):
        rows = slice(h * 256, (h + 1) * 256)
        z = scale * lax.dot_general(
            xb[rows, :], yb[...], (((1,), (1,)), ((), ())), preferred_element_type=F32
        ) + shift
        if h == 0:
            r = lax.broadcasted_iota(jnp.int32, z.shape, 0)
            c = lax.broadcasted_iota(jnp.int32, z.shape, 1)
            same = (r == c) & (r < OWN)
            signs = jnp.where(same, F32(1.0), F32(-1.0))
            v = -signs * z
        else:
            signs = F32(-1.0)
            v = z
        e = jnp.exp(-jnp.abs(v))
        small = e * (1.0 - e * (0.5 - e * F32(1.0 / 3.0)))
        soft = jnp.maximum(v, 0.0) + jnp.where(e < 0.004, small, jnp.log(1.0 + e))
        loss = loss + jnp.sum(jnp.sum(soft, axis=0, keepdims=True), axis=1, keepdims=True)
        part = 1.0 / (1.0 + e)
        gs[rows, :] = (gfac * signs * jnp.where(v >= 0, part, e * part)).astype(BF16)
    for h in range(2):
        dx2 = scale * jnp.dot(gs[h * 256:(h + 1) * 256, :], yb[...], preferred_element_type=F32)
        for j in range(2):
            k = 2 * h + j
            dx = dx2[j * OWN:(j + 1) * OWN]
            inv = invx[k * OWN:(k + 1) * OWN, 0:1]
            full = images[k][...].astype(F32) * inv
            out = (dx - full * jnp.sum(full * dx, axis=1, keepdims=True)) * inv
            target = (g0, g1, g2, g3)[k]
            target[...] = out.astype(target.dtype)
    bias = jnp.zeros((1, D), F32)
    first = core_ref[0] == 0
    for h in range(2):
        rows = slice(h * 256, (h + 1) * 256)
        dy = scale * lax.dot_general(
            gs[:, rows], xb[...], (((0,), (0,)), ((), ())), preferred_element_type=F32
        )
        y = y_ref[rows, :]
        du = (dy - y * jnp.sum(y * dy, axis=1, keepdims=True)) * invu_ref[rows, 0:1]
        bias = bias + jnp.sum(du, axis=0, keepdims=True)
        left, right = du[:, :WIDE].astype(BF16), du[:, WIDE:].astype(BF16)

        @pl.when(first)
        def _():
            keep_ref[rows, :] = left
            give_ref[rows, :D - WIDE] = right

        @pl.when(jnp.logical_not(first))
        def _():
            give_ref[rows, :] = left
            keep_ref[rows, :D - WIDE] = right
    ext[...] = jnp.zeros((ONE, 128), F32)
    for r in range(D // 128):
        ext[r:r + 1, :] = bias[:, r * 128:(r + 1) * 128]
    lane = lax.broadcasted_iota(jnp.int32, (1, 128), 1)
    ext[D // 128:D // 128 + 1, :] = jnp.where(lane == 0, loss, 0.0)
    hi, lo = hi_lo(ext[...])
    rest = jnp.zeros((4 * OWN - 2 * ONE, WIDE - (D - WIDE)), BF16)

    def extras(ref):
        ref[0:ONE, D - WIDE:] = hi
        ref[ONE:2 * ONE, D - WIDE:] = lo
        ref[2 * ONE:, D - WIDE:] = rest

    @pl.when(first)
    def _():
        extras(give_ref)

    @pl.when(jnp.logical_not(first))
    def _():
        extras(keep_ref)


def head_kernel(idx_ref, t0, t1, t2, t3, keep_ref, got_ref, o0, o1, o2, o3, t_all, both, rw):
    for k, ref in enumerate((t0, t1, t2, t3)):
        rows, swap = slice(k * OWN, (k + 1) * OWN), slice((k ^ 1) * OWN, ((k ^ 1) + 1) * OWN)
        t_all[rows, :] = ref[...]
        both[rows, :] = (keep_ref[rows, :].astype(F32) + got_ref[swap, :].astype(F32)).astype(BF16)
    tail = slice(D - WIDE, WIDE)
    last = idx_ref[0] == 1
    e = keep_ref[0:2 * ONE, tail].astype(F32) + got_ref[0:2 * ONE, tail].astype(F32)
    hi, lo = hi_lo(e[:ONE] + e[ONE:])
    for q in range(4):
        rw[q] = lax.dot_general(
            t_all[:, q * PART:(q + 1) * PART], both[...], (((0,), (0,)), ((), ())), preferred_element_type=F32
        ).astype(BF16)

    @pl.when(last)
    def _():
        for q in range(4):
            rw[q, :, tail] = jnp.zeros((PART, 128), BF16)
        rw[0, 0:ONE, tail] = hi
        rw[0, ONE:2 * ONE, tail] = lo

    for s, ref in enumerate((o0, o1, o2, o3)):
        ref[...] = rw[lax.rem(idx_ref[1] + s, 4)]


def tile_kernel(idx_ref, a0, a1, a2, a3, out):
    total = a0[...].astype(F32) + a1[...].astype(F32) + a2[...].astype(F32) + a3[...].astype(F32)
    for t in range(PART // ONE):
        for l in range(WIDE // 128):
            n = t * (WIDE // 128) + l
            out[n * ONE:(n + 1) * ONE, :] = total[t * ONE:(t + 1) * ONE, l * 128:(l + 1) * 128].astype(BF16)
    out[90 * ONE:, :] = jnp.zeros((6 * ONE, 128), BF16)

    @pl.when((idx_ref[0] == 1) & (idx_ref[1] == 0))
    def _():
        hi, lo = hi_lo(total[:ONE, D - WIDE:] + total[ONE:2 * ONE, D - WIDE:])
        out[93 * ONE:94 * ONE, :] = hi
        out[94 * ONE:95 * ONE, :] = lo


def last_kernel(idx_ref, clip_ref, p0, p1, p2, p3, q0, q1, q2, q3, w_ref, b_ref, loss_ref):
    mine, theirs = (p0, p1, p2, p3), (q0, q1, q2, q3)

    def whole(left, right, at_left, at_right):
        extra = jnp.zeros((ONE, 128), F32)
        for s, ref in enumerate(right):
            here = (lax.rem(at_right + 4 - s, 4) == 0).astype(F32)
            pair = ref[93 * ONE:95 * ONE, :].astype(F32)
            extra = extra + here * (pair[:ONE] + pair[ONE:])
        bias = extra[:D // 128]
        total = jnp.zeros((ONE, 128), F32)
        for refs, lanes in ((left, 5), (right, 4)):
            for ref in refs:
                def add(t, acc, ref=ref, lanes=lanes):
                    for l in range(lanes):
                        v = ref[pl.ds(pl.multiple_of(t * 80, 16) + l * ONE, ONE), :].astype(F32)
                        acc = acc + v * v
                    return acc
                total = lax.fori_loop(0, PART // ONE, add, total)
        square = jnp.sum(total, keepdims=True) + jnp.sum(bias * bias, keepdims=True)
        factor = jnp.minimum(F32(1.0), clip_ref[0] / jnp.sqrt(square))
        for refs, lanes, base, at in ((left, 5, 0, at_left), (right, 4, WIDE, at_right)):
            for s, ref in enumerate(refs):
                row0 = lax.rem(at + 4 - s, 4) * PART

                def put(t, carry, ref=ref, lanes=lanes, base=base, row0=row0):
                    for l in range(lanes):
                        v = ref[pl.ds(pl.multiple_of(t * 80, 16) + l * ONE, ONE), :].astype(F32)
                        rows = pl.ds(pl.multiple_of(row0 + t * ONE, ONE), ONE)
                        w_ref[rows, base + l * 128:base + (l + 1) * 128] = v * factor
                    return carry
                lax.fori_loop(0, PART // ONE, put, 0)
        for r in range(D // 128):
            b_ref[0:1, r * 128:(r + 1) * 128] = bias[r:r + 1] * factor
        loss_ref[...] = extra[D // 128:D // 128 + 1, :] * F32(1.0 / TOTAL)

    @pl.when(idx_ref[0] == 0)
    def _():
        whole(mine, theirs, idx_ref[1], idx_ref[2])

    @pl.when(idx_ref[0] == 1)
    def _():
        whole(theirs, mine, idx_ref[2], idx_ref[1])


def sds(shape, kind):
    return jax.ShapeDtypeStruct(shape, kind)


def local(images, texts, head_weight, head_bias, logit_scale, logit_shift, loss_scale, clip_norm):
    core = lax.axis_index("core")
    at_x, at_y = lax.axis_index("x"), lax.axis_index(("yh", "yl"))
    at = jnp.where(core == 0, at_x, at_y)
    at_other = jnp.where(core == 0, at_y, at_x)
    idx = jnp.stack([core, at, at_other]).astype(jnp.int32)
    scal = jnp.stack([logit_scale[0], logit_shift[0], -loss_scale[0] / TOTAL])

    txt = [texts, shifted(texts, "core", 1), shifted(texts, "yh", 1)]
    txt.append(lax.ppermute(texts, ("yh", "core"), [(0, 3), (1, 2), (2, 1), (3, 0)]))
    img = [images] + [shifted(images, "x", s) for s in (2, 1, 3)]

    y_full, inv_u = pl.pallas_call(
        text_kernel,
        out_shape=(sds((4 * OWN, D), F32), sds((4 * OWN, 128), F32)),
        in_specs=[VMEM] * 6, out_specs=(VMEM, VMEM), compiler_params=BIG,
        cost_estimate=pl.CostEstimate(flops=2 * 512 * D * D, bytes_accessed=6_500_000, transcendentals=512),
        name="text_side",
    )(*txt, head_weight, head_bias[None])
    ig0, ig1, ig2, ig3, keep, give = pl.pallas_call(
        pair_kernel,
        out_shape=(sds((OWN, D), F32),) + (sds((OWN, D), BF16),) * 3 + (sds((4 * OWN, WIDE), BF16),) * 2,
        in_specs=[SMEM, SMEM] + [VMEM] * 6, out_specs=(VMEM,) * 6, compiler_params=BIG,
        scratch_shapes=[
            pltpu.VMEM((4 * OWN, D), BF16), pltpu.VMEM((4 * OWN, D), BF16), pltpu.VMEM((4 * OWN, 4 * OWN), BF16),
            pltpu.VMEM((4 * OWN, 128), F32), pltpu.VMEM((ONE, 128), F32),
        ],
        cost_estimate=pl.CostEstimate(flops=6 * 512 * 512 * D, bytes_accessed=6_500_000, transcendentals=800_000),
        name="pairs",
    )(idx, scal, *img, y_full, inv_u)

    got = shifted(give, "core", 1)
    parts = pl.pallas_call(
        head_kernel,
        out_shape=(sds((PART, WIDE), BF16),) * 4,
        in_specs=[SMEM] + [VMEM] * 6, out_specs=(VMEM,) * 4, compiler_params=BIG,
        scratch_shapes=[
            pltpu.VMEM((4 * OWN, D), BF16), pltpu.VMEM((4 * OWN, WIDE), BF16), pltpu.VMEM((4, PART, WIDE), BF16),
        ],
        cost_estimate=pl.CostEstimate(flops=2 * 512 * D * WIDE, bytes_accessed=4_000_000, transcendentals=0),
        name="head",
    )(idx, *txt, keep, got)
    r2, r1, r3 = [lax.ppermute(parts[s], ALL, around(s)) for s in (2, 1, 3)]
    tiles = pl.pallas_call(
        tile_kernel,
        out_shape=sds((TILES * ONE, 128), BF16),
        in_specs=[SMEM] + [VMEM] * 4, out_specs=VMEM, compiler_params=BIG,
        cost_estimate=pl.CostEstimate(flops=4 * PART * WIDE, bytes_accessed=1_900_000, transcendentals=0),
        name="tiles",
    )(idx, parts[0], r1, r2, r3)
    ig1, ig2, ig3, tiles = lax.optimization_barrier((ig1, ig2, ig3, tiles))
    back = [shifted(ig1, "x", -2), shifted(ig2, "x", -1), shifted(ig3, "x", -3)]
    sums = lax.all_to_all(tiles.reshape(32, 48, 128), ALL, 0, 0, axis_index_groups=groups_second(), tiled=True)
    s2 = jnp.sum(sums.astype(F32), axis=0)
    at2 = jnp.where(core == 0, lax.axis_index(("yh", "z", "yl")), lax.axis_index(("x", "z")))
    f_hi, f_lo = hi_lo(s2[:ONE] + s2[ONE:2 * ONE])
    special = jnp.concatenate([f_hi, f_lo, jnp.zeros((ONE, 128), BF16)], 0)
    mine = jnp.where(at2 == 31, special, s2.astype(BF16))
    copies = jnp.broadcast_to(mine, (32, 48, 128))
    a1 = lax.all_to_all(copies, ALL, 0, 0, axis_index_groups=groups_second(), tiled=True)
    a1, back = lax.optimization_barrier((a1, back))
    image_grad = ig0 + back[0].astype(F32) + back[1].astype(F32) + back[2].astype(F32)

    b0 = a1.reshape(TILES * ONE, 128)
    b2, b1, b3 = [lax.ppermute(b0, ALL, around(s)) for s in (2, 1, 3)]
    own_half = (b0, b1, b2, b3)
    other_half = [shifted(b, "core", 1) for b in own_half]
    weight_grad, bias_grad, loss = pl.pallas_call(
        last_kernel,
        out_shape=(sds((D, D), F32), sds((1, D), F32), sds((1, 128), F32)),
        in_specs=[SMEM, SMEM] + [VMEM] * 8, out_specs=(VMEM,) * 3, compiler_params=BIG,
        cost_estimate=pl.CostEstimate(flops=4 * D * D, bytes_accessed=8_500_000, transcendentals=0),
        name="last",
    )(idx, clip_norm, *own_half, *other_half)
    return image_grad, weight_grad, bias_grad.reshape(D), loss[0, :1]


def solution(mesh):
    fine = Mesh(mesh.devices.reshape(NX, NYH, NC, NZ, NYL), ALL)
    placed = (P(ALL, None), P(ALL, None), P(), P(), P(), P(), P(), P())
    return jax.shard_map(
        local, mesh=fine, in_specs=placed, out_specs=(P(ALL, None), P(), P(), P()), check_vma=False
    )
```

time: 171 us -> 125 us (0.73)
  other arithmetic: 22.5 us -> 1.87 us
  Pallas kernels: 0 us -> 19.8 us
  starting transfers between devices: 35.5 us -> 54.3 us
  blocking collectives: 18.7 us -> 0 us
  waiting for transfers between devices: 57 us -> 41.3 us
  local copies, waits for them, and re-layouts: 17 us -> 3.96 us
  matrix products: 12.7 us -> 0 us
  between operations: 6.84 us -> 3.38 us
    all_to_all x3 -> x2, waiting for transfers between devices: 34.5 us -> 10.5 us  [the longest x1 10.5 us: local(): lax.all_to_all(tiles.reshape(32, 48, 128), ALL, 0, 0, axis_index_groups=g...]
    pallas_call x0 -> x5, Pallas kernels: none -> 19.8 us  [the longest x1 6.22 us: local(): pl.pallas_call(last_kernel, out_shape=(sds((D, D), F32), sds((1, D), F32)...]
    all_to_all x1 -> x0, blocking collectives: 18.7 us -> none  [local(): lax.all_to_all(jnp.broadcast_to(mine, (32, 48, 128)), ALL, 0, 0, axis_ind...]
    ppermute x1 -> x7, waiting for transfers between devices: 0.01 us -> 12.8 us  [the longest x3 8.07 us: local(): r2, r1, r3 = [lax.ppermute(parts[s], ALL, around(s)) for s in (2, 1, 3)]]
    dot_general x5 -> x0, matrix products: 12.7 us -> none  [the longest x1 4.56 us: local(): dx = scale * jnp.dot(g, y_b, preferred_element_type=F32)]
    ppermute x1 -> x7, starting transfers between devices: 0.87 us -> 11.9 us  [the longest x3 5 us: local(): r2, r1, r3 = [lax.ppermute(parts[s], ALL, around(s)) for s in (2, 1, 3)]]
    ppermute x10 -> x13, starting transfers between devices: 15.5 us -> 23.6 us  [shifted(): lax.ppermute(block, axis, [(i, (i + distance) % size) for i in range(size)])]
    reduce_sum x6 -> x1, other arithmetic: 7.28 us -> 0.07 us  [local(): s2 = jnp.sum(sums.astype(F32), axis=0)]
  transfers between devices with their start and end apart: 14 -> 22, of which waited for: 8 -> 11; matrix products, arithmetic and copies ran while one was open for 7% -> 2% of each run, Pallas kernels for 0% -> 3%
where the time goes in v2:
time: 125 us; the launch traced here: 124 us
  starting transfers between devices  54.3 us (43%)
  waiting for transfers between devices  41.3 us (33%)
  Pallas kernels  19.8 us (16%)
  local copies, waits for them, and re-layouts  3.96 us (3%)
  between operations  3.38 us (3%)
  other arithmetic  1.87 us (1%)
    ppermute x13, starting transfers between devices, shifted(): lax.ppermute(block, axis, [(i, (i + distance) % size) for i in range(size)])  23.6 us
    ppermute x13, waiting for transfers between devices, shifted(): lax.ppermute(block, axis, [(i, (i + distance) % size) for i in range(size)])  17.9 us
    all_to_all x1, starting transfers between devices, local(): lax.all_to_all(tiles.reshape(32, 48, 128), ALL, 0, 0, axis_index_groups=g...  10.8 us
    all_to_all x1, waiting for transfers between devices, local(): lax.all_to_all(tiles.reshape(32, 48, 128), ALL, 0, 0, axis_index_groups=g...  10.5 us
    ppermute x3, waiting for transfers between devices, local(): r2, r1, r3 = [lax.ppermute(parts[s], ALL, around(s)) for s in (2, 1, 3)]  8.07 us
    all_to_all x1, starting transfers between devices, local(): lax.all_to_all(copies, ALL, 0, 0, axis_index_groups=groups_second(), tile...  7.95 us
    pallas_call x1, Pallas kernels, local(): pl.pallas_call(last_kernel, out_shape=(sds((D, D), F32), sds((1, D), F32)...  6.22 us
    pallas_call x1, Pallas kernels, local(): pl.pallas_call(pair_kernel, out_shape=(sds((OWN, D), F32),) + (sds((OWN,...  5.98 us
  transfers between devices with their start and end apart: 22, of which 11 were waited for; matrix products, arithmetic and copies ran while one was open for 2% of the time, Pallas kernels for 3%

profile of v2, /device:TPU:1, one launch (start us, length us, event | category | flops | bytes accessed | tf_op | source)
XLA Modules:
  0.0 124.5 jit_solution(12099650966803029255)
XLA Ops:
  0.6 4.4 %collective-permute-start.5 = (bf16[128,1152]{1,0:T(8,128)(2,1)}, bf16[128,1152]{1,0:T(8,128)(2,1)S(1)}, u32[]{:S(2)}, u32[]{:S(2)}) collective-permute-start(bf16[128,1152]{1,0:T(8,128)(2,1)} %t0.3), channel_id=1, source_target_pairs={{0,48},{16,32},{32,16},{48,0},{1,49},{17,33},{33,17},{49,1},{2,50}... | collective-permute-start | bytes 884744 | tf_op jit(solution)/shard_map/ppermute | solution.py:258
  5.0 1.8 %collective-permute-start.4 = (bf16[128,1152]{1,0:T(8,128)(2,1)}, bf16[128,1152]{1,0:T(8,128)(2,1)S(1)}, u32[]{:S(2)}, u32[]{:S(2)}) collective-permute-start(bf16[128,1152]{1,0:T(8,128)(2,1)} %t0.3), channel_id=1, source_target_pairs={{0,32},{32,0},{1,33},{33,1},{2,34},{34,2},{3,35},{35,3},{4,36},{36... | collective-permute-start | bytes 884744 | tf_op jit(solution)/shard_map/ppermute | solution.py:58
  6.8 2.4 %collective-permute-start = (bf16[128,1152]{1,0:T(8,128)(2,1)}, bf16[128,1152]{1,0:T(8,128)(2,1)S(1)}, u32[]{:S(2)}, u32[]{:S(2)}) collective-permute-start(bf16[128,1152]{1,0:T(8,128)(2,1)} %i0.1), channel_id=1, source_target_pairs={{0,128},{64,192},{128,0},{192,64},{1,129},{65,193},{129,1},{193,65... | collective-permute-start | bytes 884744 | tf_op jit(solution)/shard_map/ppermute | solution.py:58
  9.2 3.0 %collective-permute-done.5.t3 = bf16[128,1152]{1,0:T(8,128)(2,1)S(1)} collective-permute-done((bf16[128,1152]{1,0:T(8,128)(2,1)}, bf16[128,1152]{1,0:T(8,128)(2,1)S(1)}, u32[]{:S(2)}, u32[]{:S(2)}) %collective-permute-start.5) | collective-permute-done | bytes 294944 | tf_op jit(solution)/shard_map/ppermute | solution.py:258
  12.2 3.4 %collective-permute-start.2 = (bf16[128,1152]{1,0:T(8,128)(2,1)}, bf16[128,1152]{1,0:T(8,128)(2,1)S(1)}, u32[]{:S(2)}, u32[]{:S(2)}) collective-permute-start(bf16[128,1152]{1,0:T(8,128)(2,1)} %i0.1), channel_id=1, source_target_pairs={{0,192},{64,0},{128,64},{192,128},{1,193},{65,1},{129,65},{193,129... | collective-permute-start | bytes 884744 | tf_op jit(solution)/shard_map/ppermute | solution.py:58
  20.4 3.9 %text_side.1 = (f32[512,1152]{1,0:T(8,128)S(1)}, f32[512,128]{1,0:T(8,128)S(1)}) custom-call(bf16[128,1152]{1,0:T(8,128)(2,1)S(1)} %copy-done.1, bf16[128,1152]{1,0:T(8,128)(2,1)S(1)} %collective-permute-done.3.t1, bf16[128,1152]{1,0:T(8,128)(2,1)S(1)} %collective-permute-done.4.t2, bf16[128,1152]{1,0:T(8,128)(2,1)S(1)} %collective-permute-done.5.t3, ...), custom_call_target="tpu_custom_call" | custom-call | flops 1358954496 | bytes 6500000 | tf_op jit(solution)/shard_map/text_side/pallas_call | solution.py:261
  25.8 6.0 %pairs.1 = (f32[128,1152]{1,0:T(8,128)S(1)}, bf16[128,1152]{1,0:T(8,128)(2,1)S(1)}, bf16[128,1152]{1,0:T(8,128)(2,1)S(1)}, bf16[128,1152]{1,0:T(8,128)(2,1)S(1)}...) custom-call(s32[3]{0:T(128)S(1)} %pad_add_fusion.core_ref.idx_ref, f32[3]{0:T(128)S(1)} %pad_maximum_fusion.scal_ref, ...), custom_call_target="tpu_custom_call" | custom-call | flops 1811939328 | bytes 6500000 | tf_op jit(solution)/shard_map/pairs/pallas_call | solution.py:268
  31.8 2.1 %collective-permute-done.6.got_ref = bf16[512,640]{1,0:T(8,128)(2,1)S(1)} collective-permute-done((bf16[512,640]{1,0:T(8,128)(2,1)S(1)}, bf16[512,640]{1,0:T(8,128)(2,1)S(1)}, u32[]{:S(2)}, u32[]{:S(2)}) %collective-permute-start.6) | collective-permute-done | bytes 655392 | tf_op jit(solution)/shard_map/ppermute | solution.py:58
  33.9 2.2 %head.1 = (bf16[288,640]{1,0:T(8,128)(2,1)S(1)}, bf16[288,640]{1,0:T(8,128)(2,1)S(1)}, bf16[288,640]{1,0:T(8,128)(2,1)S(1)}, bf16[288,640]{1,0:T(8,128)(2,1)S(1)}) custom-call(s32[3]{0:T(128)S(1)} %pad_add_fusion.core_ref.idx_ref, bf16[128,1152]{1,0:T(8,128)(2,1)S(1)} %copy-done.2, bf16[128,1152]{1,0:T(8,128)(2,1)S(1)} %collective-permute-done.3.t1, ...), custom_call_target="tpu_custom_call" | custom-call | flops 754974720 | bytes 4000000 | tf_op jit(solution)/shard_map/head/pallas_call | solution.py:281
  37.4 2.6 %collective-permute-start.8 = (bf16[288,640]{1,0:T(8,128)(2,1)S(1)}, bf16[288,640]{1,0:T(8,128)(2,1)S(1)}, u32[]{:S(2)}, u32[]{:S(2)}) collective-permute-start(bf16[288,640]{1,0:T(8,128)(2,1)S(1)} %get-tuple-element.37), channel_id=1, source_target_pairs={{0,128},{1,129},{2,130},{3,131},{4,132},{5,133},{6,134},{7,135},{8... | collective-permute-start | bytes 1105928 | tf_op jit(solution)/shard_map/ppermute | solution.py:291
  41.1 3.1 %collective-permute-done.7.a1 = bf16[288,640]{1,0:T(8,128)(2,1)S(1)} collective-permute-done((bf16[288,640]{1,0:T(8,128)(2,1)S(1)}, bf16[288,640]{1,0:T(8,128)(2,1)S(1)}, u32[]{:S(2)}, u32[]{:S(2)}) %collective-permute-start.7) | collective-permute-done | bytes 368672 | tf_op jit(solution)/shard_map/ppermute | solution.py:291
  44.2 5.0 %collective-permute-done.8.a2 = bf16[288,640]{1,0:T(8,128)(2,1)S(1)} collective-permute-done((bf16[288,640]{1,0:T(8,128)(2,1)S(1)}, bf16[288,640]{1,0:T(8,128)(2,1)S(1)}, u32[]{:S(2)}, u32[]{:S(2)}) %collective-permute-start.8) | collective-permute-done | bytes 368672 | tf_op jit(solution)/shard_map/ppermute | solution.py:291
  50.7 10.8 %all-to-all-start = ((bf16[32,48,128]{2,1,0:T(8,128)(2,1)}), bf16[32,48,128]{2,1,0:T(8,128)(2,1)S(1)}, u32[]{:S(2)}, u32[]{:S(2)}) async-start(bf16[32,48,128]{2,1,0:T(8,128)(2,1)} %bitcast.3), calls=%async_computation | async-start | bytes 786432 | tf_op jit(solution)/shard_map/all_to_all | solution.py:301
  61.5 10.5 %all-to-all-done = bf16[32,48,128]{2,1,0:T(8,128)(2,1)S(1)} async-done(((bf16[32,48,128]{2,1,0:T(8,128)(2,1)}), bf16[32,48,128]{2,1,0:T(8,128)(2,1)S(1)}, u32[]{:S(2)}, u32[]{:S(2)}) %all-to-all-start) | async-done | bytes 393248 | tf_op jit(solution)/shard_map/all_to_all | solution.py:301
  73.0 7.9 %all-to-all-start.1 = ((bf16[32,48,128]{2,1,0:T(8,128)(2,1)}), bf16[32,48,128]{2,1,0:T(8,128)(2,1)S(1)}, u32[]{:S(2)}, u32[]{:S(2)}) async-start(bf16[32,48,128]{2,1,0:T(8,128)(2,1)} %broadcast_in_dim.11), calls=%async_computation.1 | async-start | bytes 786432 | tf_op jit(solution)/shard_map/all_to_all | solution.py:308
  81.0 2.8 %collective-permute-start.10 = (bf16[128,1152]{1,0:T(8,128)(2,1)S(1)}, bf16[128,1152]{1,0:T(8,128)(2,1)S(1)}, u32[]{:S(2)}, u32[]{:S(2)}) collective-permute-start(bf16[128,1152]{1,0:T(8,128)(2,1)S(1)} %get-tuple-element.40), channel_id=1, source_target_pairs={{0,128},{64,192},{128,0},{192,64},{1,129},{65,193},{129,1},{193,65... | collective-permute-start | bytes 884744 | tf_op jit(solution)/shard_map/ppermute | solution.py:58
  85.3 5.9 %collective-permute-done.10 = bf16[128,1152]{1,0:T(8,128)(2,1)S(1)} collective-permute-done((bf16[128,1152]{1,0:T(8,128)(2,1)S(1)}, bf16[128,1152]{1,0:T(8,128)(2,1)S(1)}, u32[]{:S(2)}, u32[]{:S(2)}) %collective-permute-start.10) | collective-permute-done | bytes 294944 | tf_op jit(solution)/shard_map/ppermute | solution.py:58
  91.2 7.3 %collective-permute-done.11 = bf16[128,1152]{1,0:T(8,128)(2,1)S(1)} collective-permute-done((bf16[128,1152]{1,0:T(8,128)(2,1)S(1)}, bf16[128,1152]{1,0:T(8,128)(2,1)S(1)}, u32[]{:S(2)}, u32[]{:S(2)}) %collective-permute-start.11) | collective-permute-done | bytes 294944 | tf_op jit(solution)/shard_map/ppermute | solution.py:58
  99.6 2.5 %collective-permute-start.14 = (bf16[1536,128]{1,0:T(8,128)(2,1)S(1)}, bf16[1536,128]{1,0:T(8,128)(2,1)S(1)}, u32[]{:S(2)}, u32[]{:S(2)}) collective-permute-start(bf16[1536,128]{1,0:T(8,128)(2,1)S(1)} %bitcast.8), channel_id=1, source_target_pairs={{0,128},{1,129},{2,130},{3,131},{4,132},{5,133},{6,134},{7,135},{8... | collective-permute-start | bytes 1179656 | tf_op jit(solution)/shard_map/ppermute | solution.py:313
  102.9 1.9 %collective-permute-start.16 = (bf16[1536,128]{1,0:T(8,128)(2,1)S(1)}, bf16[1536,128]{1,0:T(8,128)(2,1)S(1)}, u32[]{:S(2)}, u32[]{:S(2)}) collective-permute-start(bf16[1536,128]{1,0:T(8,128)(2,1)S(1)} %bitcast.10), channel_id=1, source_target_pairs={{0,16},{16,0},{1,17},{17,1},{2,18},{18,2},{3,19},{19,3},{4,20},{20... | collective-permute-start | bytes 1179656 | tf_op jit(solution)/shard_map/ppermute | solution.py:58
  104.8 1.8 %collective-permute-done.15.p3 = bf16[1536,128]{1,0:T(8,128)(2,1)S(1)} collective-permute-done((bf16[1536,128]{1,0:T(8,128)(2,1)S(1)}, bf16[1536,128]{1,0:T(8,128)(2,1)S(1)}, u32[]{:S(2)}, u32[]{:S(2)}) %collective-permute-start.15) | collective-permute-done | bytes 393248 | tf_op jit(solution)/shard_map/ppermute | solution.py:313
  106.6 5.8 %collective-permute-start.19 = (bf16[1536,128]{1,0:T(8,128)(2,1)S(1)}, bf16[1536,128]{1,0:T(8,128)(2,1)S(1)}, u32[]{:S(2)}, u32[]{:S(2)}) collective-permute-start(bf16[1536,128]{1,0:T(8,128)(2,1)S(1)} %collective-permute-done.15.p3), channel_id=1, source_target_pairs={{0,16},{16,0},{1,17},{17,1},{2,18},{18,2},{3,19},{19,3},{4,20},{20... | collective-permute-start | bytes 1179656 | tf_op jit(solution)/shard_map/ppermute | solution.py:58
  112.4 3.9 %collective-permute-start.17 = (bf16[1536,128]{1,0:T(8,128)(2,1)S(1)}, bf16[1536,128]{1,0:T(8,128)(2,1)S(1)}, u32[]{:S(2)}, u32[]{:S(2)}) collective-permute-start(bf16[1536,128]{1,0:T(8,128)(2,1)S(1)} %collective-permute-done.13.p1), channel_id=1, source_target_pairs={{0,16},{16,0},{1,17},{17,1},{2,18},{18,2},{3,19},{19,3},{4,20},{20... | collective-permute-start | bytes 1179656 | tf_op jit(solution)/shard_map/ppermute | solution.py:58
  117.7 6.2 %last.1 = (f32[1152,1152]{1,0:T(8,128)}, f32[1,1152]{1,0:T(1,128)S(1)}, f32[1,128]{1,0:T(1,128)}) custom-call(s32[3]{0:T(128)S(1)} %pad_add_fusion.core_ref.idx_ref, f32[1]{0:T(128)S(6)} %copy.15.clip_ref, bf16[1536,128]{1,0:T(8,128)(2,1)S(1)} %bitcast.11, bf16[1536,128]{1,0:T(8,128)(2,1)S(1)} %collective-permute-done.13.p1, ...), custom_call_target="tpu_custom_call" | custom-call | flops 5308416 | bytes 8500000 | tf_op jit(solution)/shard_map/last/pallas_call | solution.py:316
  (44 shorter events, 13.8 us)
Async XLA Ops:
  0.6 25.1 %copy-start = (bf16[128,1152]{1,0:T(8,128)(2,1)S(1)}, bf16[128,1152]{1,0:T(8,128)(2,1)}, u32[]{:S(2)}) copy-start(bf16[128,1152]{1,0:T(8,128)(2,1)} %i0.1) | copy-start | bytes 884740
  0.6 11.5 %collective-permute-start.5 = (bf16[128,1152]{1,0:T(8,128)(2,1)}, bf16[128,1152]{1,0:T(8,128)(2,1)S(1)}, u32[]{:S(2)}, u32[]{:S(2)}) collective-permute-start(bf16[128,1152]{1,0:T(8,128)(2,1)} %t0.3), channel_id=1, source_target_pairs={{0,48},{16,32},{32,16},{48,0},{1,49},{17,33},{33,17},{49,1},{2,50}... | collective-permute-start | bytes 884744 | tf_op jit(solution)/shard_map/ppermute | solution.py:258
  5.0 14.4 %collective-permute-start.4 = (bf16[128,1152]{1,0:T(8,128)(2,1)}, bf16[128,1152]{1,0:T(8,128)(2,1)S(1)}, u32[]{:S(2)}, u32[]{:S(2)}) collective-permute-start(bf16[128,1152]{1,0:T(8,128)(2,1)} %t0.3), channel_id=1, source_target_pairs={{0,32},{32,0},{1,33},{33,1},{2,34},{34,2},{3,35},{35,3},{4,36},{36... | collective-permute-start | bytes 884744 | tf_op jit(solution)/shard_map/ppermute | solution.py:58
  6.8 12.6 %collective-permute-start.3 = (bf16[128,1152]{1,0:T(8,128)(2,1)}, bf16[128,1152]{1,0:T(8,128)(2,1)S(1)}, u32[]{:S(2)}, u32[]{:S(2)}) collective-permute-start(bf16[128,1152]{1,0:T(8,128)(2,1)} %t0.3), channel_id=1, source_target_pairs={{0,16},{16,0},{1,17},{17,1},{2,18},{18,2},{3,19},{19,3},{4,20},{20... | collective-permute-start | bytes 884744 | tf_op jit(solution)/shard_map/ppermute | solution.py:58
  6.8 18.9 %collective-permute-start.1 = (bf16[128,1152]{1,0:T(8,128)(2,1)}, bf16[128,1152]{1,0:T(8,128)(2,1)S(1)}, u32[]{:S(2)}, u32[]{:S(2)}) collective-permute-start(bf16[128,1152]{1,0:T(8,128)(2,1)} %i0.1), channel_id=1, source_target_pairs={{0,64},{64,128},{128,192},{192,0},{1,65},{65,129},{129,193},{193,1... | collective-permute-start | bytes 884744 | tf_op jit(solution)/shard_map/ppermute | solution.py:58
  6.8 18.9 %collective-permute-start = (bf16[128,1152]{1,0:T(8,128)(2,1)}, bf16[128,1152]{1,0:T(8,128)(2,1)S(1)}, u32[]{:S(2)}, u32[]{:S(2)}) collective-permute-start(bf16[128,1152]{1,0:T(8,128)(2,1)} %i0.1), channel_id=1, source_target_pairs={{0,128},{64,192},{128,0},{192,64},{1,129},{65,193},{129,1},{193,65... | collective-permute-start | bytes 884744 | tf_op jit(solution)/shard_map/ppermute | solution.py:58
  12.2 13.6 %collective-permute-start.2 = (bf16[128,1152]{1,0:T(8,128)(2,1)}, bf16[128,1152]{1,0:T(8,128)(2,1)S(1)}, u32[]{:S(2)}, u32[]{:S(2)}) collective-permute-start(bf16[128,1152]{1,0:T(8,128)(2,1)} %i0.1), channel_id=1, source_target_pairs={{0,192},{64,0},{128,64},{192,128},{1,193},{65,1},{129,65},{193,129... | collective-permute-start | bytes 884744 | tf_op jit(solution)/shard_map/ppermute | solution.py:58
  25.7 8.2 %copy-start.2 = (bf16[128,1152]{1,0:T(8,128)(2,1)S(1)}, bf16[128,1152]{1,0:T(8,128)(2,1)}, u32[]{:S(2)}) copy-start(bf16[128,1152]{1,0:T(8,128)(2,1)} %t0.3) | copy-start | bytes 884740
  31.7 2.2 %collective-permute-start.6 = (bf16[512,640]{1,0:T(8,128)(2,1)S(1)}, bf16[512,640]{1,0:T(8,128)(2,1)S(1)}, u32[]{:S(2)}, u32[]{:S(2)}) collective-permute-start(bf16[512,640]{1,0:T(8,128)(2,1)S(1)} %get-tuple-element.34), channel_id=1, source_target_pairs={{0,16},{16,0},{1,17},{17,1},{2,18},{18,2},{3,19},{19,3},{4,20},{20... | collective-permute-start | bytes 1966088 | tf_op jit(solution)/shard_map/ppermute | solution.py:58
  36.1 8.1 %collective-permute-start.7 = (bf16[288,640]{1,0:T(8,128)(2,1)S(1)}, bf16[288,640]{1,0:T(8,128)(2,1)S(1)}, u32[]{:S(2)}, u32[]{:S(2)}) collective-permute-start(bf16[288,640]{1,0:T(8,128)(2,1)S(1)} %get-tuple-element.36), channel_id=1, source_target_pairs={{0,64},{1,65},{2,66},{3,67},{4,68},{5,69},{6,70},{7,71},{8,72},{9,... | collective-permute-start | bytes 1105928 | tf_op jit(solution)/shard_map/ppermute | solution.py:291
  37.4 11.8 %collective-permute-start.8 = (bf16[288,640]{1,0:T(8,128)(2,1)S(1)}, bf16[288,640]{1,0:T(8,128)(2,1)S(1)}, u32[]{:S(2)}, u32[]{:S(2)}) collective-permute-start(bf16[288,640]{1,0:T(8,128)(2,1)S(1)} %get-tuple-element.37), channel_id=1, source_target_pairs={{0,128},{1,129},{2,130},{3,131},{4,132},{5,133},{6,134},{7,135},{8... | collective-permute-start | bytes 1105928 | tf_op jit(solution)/shard_map/ppermute | solution.py:291
  40.0 9.1 %collective-permute-start.9 = (bf16[288,640]{1,0:T(8,128)(2,1)S(1)}, bf16[288,640]{1,0:T(8,128)(2,1)S(1)}, u32[]{:S(2)}, u32[]{:S(2)}) collective-permute-start(bf16[288,640]{1,0:T(8,128)(2,1)S(1)} %get-tuple-element.38), channel_id=1, source_target_pairs={{0,192},{1,193},{2,194},{3,195},{4,196},{5,197},{6,198},{7,199},{8... | collective-permute-start | bytes 1105928 | tf_op jit(solution)/shard_map/ppermute | solution.py:291
  50.7 21.4 %all-to-all-start = ((bf16[32,48,128]{2,1,0:T(8,128)(2,1)}), bf16[32,48,128]{2,1,0:T(8,128)(2,1)S(1)}, u32[]{:S(2)}, u32[]{:S(2)}) async-start(bf16[32,48,128]{2,1,0:T(8,128)(2,1)} %bitcast.3), calls=%async_computation | async-start | bytes 786432 | tf_op jit(solution)/shard_map/all_to_all | solution.py:301
  73.0 26.6 %all-to-all-start.1 = ((bf16[32,48,128]{2,1,0:T(8,128)(2,1)}), bf16[32,48,128]{2,1,0:T(8,128)(2,1)S(1)}, u32[]{:S(2)}, u32[]{:S(2)}) async-start(bf16[32,48,128]{2,1,0:T(8,128)(2,1)} %broadcast_in_dim.11), calls=%async_computation.1 | async-start | bytes 786432 | tf_op jit(solution)/shard_map/all_to_all | solution.py:308
  81.0 10.2 %collective-permute-start.10 = (bf16[128,1152]{1,0:T(8,128)(2,1)S(1)}, bf16[128,1152]{1,0:T(8,128)(2,1)S(1)}, u32[]{:S(2)}, u32[]{:S(2)}) collective-permute-start(bf16[128,1152]{1,0:T(8,128)(2,1)S(1)} %get-tuple-element.40), channel_id=1, source_target_pairs={{0,128},{64,192},{128,0},{192,64},{1,129},{65,193},{129,1},{193,65... | collective-permute-start | bytes 884744 | tf_op jit(solution)/shard_map/ppermute | solution.py:58
  83.8 14.7 %collective-permute-start.11 = (bf16[128,1152]{1,0:T(8,128)(2,1)S(1)}, bf16[128,1152]{1,0:T(8,128)(2,1)S(1)}, u32[]{:S(2)}, u32[]{:S(2)}) collective-permute-start(bf16[128,1152]{1,0:T(8,128)(2,1)S(1)} %get-tuple-element.41), channel_id=1, source_target_pairs={{0,192},{64,0},{128,64},{192,128},{1,193},{65,1},{129,65},{193,129... | collective-permute-start | bytes 884744 | tf_op jit(solution)/shard_map/ppermute | solution.py:58
  84.7 14.9 %collective-permute-start.12 = (bf16[128,1152]{1,0:T(8,128)(2,1)S(1)}, bf16[128,1152]{1,0:T(8,128)(2,1)S(1)}, u32[]{:S(2)}, u32[]{:S(2)}) collective-permute-start(bf16[128,1152]{1,0:T(8,128)(2,1)S(1)} %get-tuple-element.42), channel_id=1, source_target_pairs={{0,64},{64,128},{128,192},{192,0},{1,65},{65,129},{129,193},{193,1... | collective-permute-start | bytes 884744 | tf_op jit(solution)/shard_map/ppermute | solution.py:58
  99.6 6.9 %collective-permute-start.15 = (bf16[1536,128]{1,0:T(8,128)(2,1)S(1)}, bf16[1536,128]{1,0:T(8,128)(2,1)S(1)}, u32[]{:S(2)}, u32[]{:S(2)}) collective-permute-start(bf16[1536,128]{1,0:T(8,128)(2,1)S(1)} %bitcast.7), channel_id=1, source_target_pairs={{0,192},{1,193},{2,194},{3,195},{4,196},{5,197},{6,198},{7,199},{8... | collective-permute-start | bytes 1179656 | tf_op jit(solution)/shard_map/ppermute | solution.py:313
  99.6 12.7 %collective-permute-start.14 = (bf16[1536,128]{1,0:T(8,128)(2,1)S(1)}, bf16[1536,128]{1,0:T(8,128)(2,1)S(1)}, u32[]{:S(2)}, u32[]{:S(2)}) collective-permute-start(bf16[1536,128]{1,0:T(8,128)(2,1)S(1)} %bitcast.8), channel_id=1, source_target_pairs={{0,128},{1,129},{2,130},{3,131},{4,132},{5,133},{6,134},{7,135},{8... | collective-permute-start | bytes 1179656 | tf_op jit(solution)/shard_map/ppermute | solution.py:313
  102.2 10.2 %collective-permute-start.13 = (bf16[1536,128]{1,0:T(8,128)(2,1)S(1)}, bf16[1536,128]{1,0:T(8,128)(2,1)S(1)}, u32[]{:S(2)}, u32[]{:S(2)}) collective-permute-start(bf16[1536,128]{1,0:T(8,128)(2,1)S(1)} %bitcast.9), channel_id=1, source_target_pairs={{0,64},{1,65},{2,66},{3,67},{4,68},{5,69},{6,70},{7,71},{8,72},{9,... | collective-permute-start | bytes 1179656 | tf_op jit(solution)/shard_map/ppermute | solution.py:313
  102.9 14.4 %collective-permute-start.16 = (bf16[1536,128]{1,0:T(8,128)(2,1)S(1)}, bf16[1536,128]{1,0:T(8,128)(2,1)S(1)}, u32[]{:S(2)}, u32[]{:S(2)}) collective-permute-start(bf16[1536,128]{1,0:T(8,128)(2,1)S(1)} %bitcast.10), channel_id=1, source_target_pairs={{0,16},{16,0},{1,17},{17,1},{2,18},{18,2},{3,19},{19,3},{4,20},{20... | collective-permute-start | bytes 1179656 | tf_op jit(solution)/shard_map/ppermute | solution.py:58
  106.6 10.7 %collective-permute-start.19 = (bf16[1536,128]{1,0:T(8,128)(2,1)S(1)}, bf16[1536,128]{1,0:T(8,128)(2,1)S(1)}, u32[]{:S(2)}, u32[]{:S(2)}) collective-permute-start(bf16[1536,128]{1,0:T(8,128)(2,1)S(1)} %collective-permute-done.15.p3), channel_id=1, source_target_pairs={{0,16},{16,0},{1,17},{17,1},{2,18},{18,2},{3,19},{19,3},{4,20},{20... | collective-permute-start | bytes 1179656 | tf_op jit(solution)/shard_map/ppermute | solution.py:58
  112.4 4.9 %collective-permute-start.18 = (bf16[1536,128]{1,0:T(8,128)(2,1)S(1)}, bf16[1536,128]{1,0:T(8,128)(2,1)S(1)}, u32[]{:S(2)}, u32[]{:S(2)}) collective-permute-start(bf16[1536,128]{1,0:T(8,128)(2,1)S(1)} %collective-permute-done.14.p2), channel_id=1, source_target_pairs={{0,16},{16,0},{1,17},{17,1},{2,18},{18,2},{3,19},{19,3},{4,20},{20... | collective-permute-start | bytes 1179656 | tf_op jit(solution)/shard_map/ppermute | solution.py:58
  112.4 5.3 %collective-permute-start.17 = (bf16[1536,128]{1,0:T(8,128)(2,1)S(1)}, bf16[1536,128]{1,0:T(8,128)(2,1)S(1)}, u32[]{:S(2)}, u32[]{:S(2)}) collective-permute-start(bf16[1536,128]{1,0:T(8,128)(2,1)S(1)} %collective-permute-done.13.p1), channel_id=1, source_target_pairs={{0,16},{16,0},{1,17},{17,1},{2,18},{18,2},{3,19},{19,3},{4,20},{20... | collective-permute-start | bytes 1179656 | tf_op jit(solution)/shard_map/ppermute | solution.py:58
  (2 other events, 2.4 us)

commit v3 on v2

v3 whole, which is shorter than its diff:
```python
import jax
import jax.numpy as jnp
from jax import lax
from jax.experimental import pallas as pl
from jax.experimental.pallas import tpu as pltpu
from jax.sharding import Mesh, PartitionSpec as P

EPS = 1e-06
ALL = ("x", "yh", "core", "z", "yl")
NX, NYH, NC, NZ, NYL = 4, 2, 2, 8, 2
F32, BF16 = jnp.float32, jnp.bfloat16
D, OWN = 1152, 128
WIDE = 640
PART = 288
TILES = 96
ONE = 16
TOTAL = 32768


def room(mib):
    return pltpu.CompilerParams(vmem_limit_bytes=mib * 2**20)


VMEM = pl.BlockSpec(memory_space=pltpu.VMEM)
SMEM = pl.BlockSpec(memory_space=pltpu.SMEM)
ANY = pl.BlockSpec(memory_space=pl.ANY)


def place(x, yh, core, z, yl):
    return (((x * NYH + yh) * NC + core) * NZ + z) * NYL + yl


def every():
    return [
        (x, yh, core, z, yl)
        for x in range(NX) for yh in range(NYH) for core in range(NC) for z in range(NZ) for yl in range(NYL)
    ]


def groups_second():
    out = []
    for x in range(NX):
        out.append([place(x, yh, 0, z, yl) for yh in range(NYH) for z in range(NZ) for yl in range(NYL)])
    for yh in range(NYH):
        for yl in range(NYL):
            out.append([place(x, yh, 1, z, yl) for x in range(NX) for z in range(NZ)])
    return out


def around(distance):
    route = []
    for x, yh, core, z, yl in every():
        if core == 0:
            to = place((x + distance) % NX, yh, core, z, yl)
        else:
            y = (2 * yh + yl + distance) % 4
            to = place(x, y // 2, core, z, y % 2)
        route.append((place(x, yh, core, z, yl), to))
    return route


def shifted(block, axis, distance):
    size = lax.axis_size(axis)
    return lax.ppermute(block, axis, [(i, (i + distance) % size) for i in range(size)])


def hi_lo(value):
    hi = value.astype(BF16)
    return hi, (value - hi.astype(F32)).astype(BF16)


def text_kernel(t_ref, w_ref, b_ref, y_ref, inv_ref):
    u = jnp.dot(t_ref[...], w_ref[...], preferred_element_type=F32) + b_ref[...]
    inv = lax.rsqrt(jnp.sum(u * u, axis=1, keepdims=True) + EPS)
    y_ref[...] = u * inv
    inv_ref[...] = jnp.broadcast_to(inv, (OWN, 128))


def pair_kernel(core_ref, scal_ref, i0, i1, i2, i3, y0, y1, y2, y3, v0, v1, v2, v3,
                gs, keep_ref, give_ref, xb, yb, ext):
    scale, shift, gfac = scal_ref[0], scal_ref[1], scal_ref[2]
    for k, ref in enumerate((i0, i1, i2, i3)):
        rows = slice(k * OWN, (k + 1) * OWN)
        full = ref[...].astype(F32)
        inv = lax.rsqrt(jnp.sum(full * full, axis=1, keepdims=True) + EPS)
        xb[rows, :] = (full * inv).astype(BF16)
        yb[rows, :] = (y0, y1, y2, y3)[k][...].astype(BF16)
    loss = jnp.zeros((1, 1), F32)
    for h in range(2):
        rows = slice(h * 256, (h + 1) * 256)
        z = scale * lax.dot_general(
            xb[rows, :], yb[...], (((1,), (1,)), ((), ())), preferred_element_type=F32
        ) + shift
        if h == 0:
            r = lax.broadcasted_iota(jnp.int32, z.shape, 0)
            c = lax.broadcasted_iota(jnp.int32, z.shape, 1)
            same = (r == c) & (r < OWN)
            signs = jnp.where(same, F32(1.0), F32(-1.0))
            v = -signs * z
        else:
            signs = F32(-1.0)
            v = z
        e = jnp.exp(-jnp.abs(v))
        small = e * (1.0 - e * (0.5 - e * F32(1.0 / 3.0)))
        soft = jnp.maximum(v, 0.0) + jnp.where(e < 0.004, small, jnp.log(1.0 + e))
        loss = loss + jnp.sum(jnp.sum(soft, axis=0, keepdims=True), axis=1, keepdims=True)
        part = 1.0 / (1.0 + e)
        gs[rows, :] = (gfac * signs * jnp.where(v >= 0, part, e * part)).astype(BF16)
    bias = jnp.zeros((1, D), F32)
    first = core_ref[0] == 0
    for h in range(2):
        rows = slice(h * 256, (h + 1) * 256)
        dy = scale * lax.dot_general(
            gs[:, rows], xb[...], (((0,), (0,)), ((), ())), preferred_element_type=F32
        )
        for j in range(2):
            k = 2 * h + j
            here = slice(k * OWN, (k + 1) * OWN)
            dyk = dy[j * OWN:(j + 1) * OWN]
            y = (y0, y1, y2, y3)[k][...]
            du = (dyk - y * jnp.sum(y * dyk, axis=1, keepdims=True)) * (v0, v1, v2, v3)[k][:, 0:1]
            bias = bias + jnp.sum(du, axis=0, keepdims=True)
            left, right = du[:, :WIDE].astype(BF16), du[:, WIDE:].astype(BF16)

            @pl.when(first)
            def _():
                keep_ref[here, :] = left
                give_ref[here, :D - WIDE] = right

            @pl.when(jnp.logical_not(first))
            def _():
                give_ref[here, :] = left
                keep_ref[here, :D - WIDE] = right
    ext[...] = jnp.zeros((ONE, 128), F32)
    for r in range(D // 128):
        ext[r:r + 1, :] = bias[:, r * 128:(r + 1) * 128]
    lane = lax.broadcasted_iota(jnp.int32, (1, 128), 1)
    ext[D // 128:D // 128 + 1, :] = jnp.where(lane == 0, loss, 0.0)
    hi, lo = hi_lo(ext[...])
    rest = jnp.zeros((4 * OWN - 2 * ONE, WIDE - (D - WIDE)), BF16)

    def extras(ref):
        ref[0:ONE, D - WIDE:] = hi
        ref[ONE:2 * ONE, D - WIDE:] = lo
        ref[2 * ONE:, D - WIDE:] = rest

    @pl.when(first)
    def _():
        extras(give_ref)

    @pl.when(jnp.logical_not(first))
    def _():
        extras(keep_ref)


def image_kernel(scal_ref, i0, i1, i2, i3, y0, y1, y2, y3, gs, g0, g1, g2, g3, yb):
    scale = scal_ref[0]
    for k, ref in enumerate((y0, y1, y2, y3)):
        yb[k * OWN:(k + 1) * OWN, :] = ref[...].astype(BF16)
    for h in range(2):
        dx2 = scale * jnp.dot(gs[h * 256:(h + 1) * 256, :], yb[...], preferred_element_type=F32)
        for j in range(2):
            k = 2 * h + j
            dx = dx2[j * OWN:(j + 1) * OWN]
            full = (i0, i1, i2, i3)[k][...].astype(F32)
            inv = lax.rsqrt(jnp.sum(full * full, axis=1, keepdims=True) + EPS)
            full = full * inv
            out = (dx - full * jnp.sum(full * dx, axis=1, keepdims=True)) * inv
            target = (g0, g1, g2, g3)[k]
            target[...] = out.astype(target.dtype)


def head_kernel(idx_ref, t0, t1, t2, t3, keep_ref, got_ref, o0, o1, o2, o3, t_all, both, rw):
    for k, ref in enumerate((t0, t1, t2, t3)):
        rows, swap = slice(k * OWN, (k + 1) * OWN), slice((k ^ 1) * OWN, ((k ^ 1) + 1) * OWN)
        t_all[rows, :] = ref[...]
        both[rows, :] = (keep_ref[rows, :].astype(F32) + got_ref[swap, :].astype(F32)).astype(BF16)
    tail = slice(D - WIDE, WIDE)
    last = idx_ref[0] == 1
    e = keep_ref[0:2 * ONE, tail].astype(F32) + got_ref[0:2 * ONE, tail].astype(F32)
    hi, lo = hi_lo(e[:ONE] + e[ONE:])
    for q in range(4):
        rw[q] = lax.dot_general(
            t_all[:, q * PART:(q + 1) * PART], both[...], (((0,), (0,)), ((), ())), preferred_element_type=F32
        ).astype(BF16)

    @pl.when(last)
    def _():
        for q in range(4):
            rw[q, :, tail] = jnp.zeros((PART, 128), BF16)
        rw[0, 0:ONE, tail] = hi
        rw[0, ONE:2 * ONE, tail] = lo

    for s, ref in enumerate((o0, o1, o2, o3)):
        ref[...] = rw[lax.rem(idx_ref[1] + s, 4)]


def tile_kernel(idx_ref, a0, a1, a2, a3, out):
    total = a0[...].astype(F32) + a1[...].astype(F32) + a2[...].astype(F32) + a3[...].astype(F32)
    for t in range(PART // ONE):
        for l in range(WIDE // 128):
            n = t * (WIDE // 128) + l
            n = 3 * (31 - n // 3) + n % 3
            out[n * ONE:(n + 1) * ONE, :] = total[t * ONE:(t + 1) * ONE, l * 128:(l + 1) * 128].astype(BF16)
    out[:6 * ONE, :] = jnp.zeros((6 * ONE, 128), BF16)

    @pl.when((idx_ref[0] == 1) & (idx_ref[1] == 0))
    def _():
        hi, lo = hi_lo(total[:ONE, D - WIDE:] + total[ONE:2 * ONE, D - WIDE:])
        out[:ONE, :] = hi
        out[ONE:2 * ONE, :] = lo


def last_kernel(idx_ref, clip_ref, p0, p1, p2, p3, q0, q1, q2, q3, w_ref, b_ref, loss_ref,
                slots, wide_slots, out_sem):
    parts = (p0, p1, p2, p3, q0, q1, q2, q3)

    def whole(left, right, at_left, at_right):
        total = jnp.zeros((ONE, 128), F32)
        extra = jnp.zeros((ONE, 128), F32)
        for s in range(4):
            for n, lanes in ((left + s, 5), (right + s, 4)):

                def add(t, acc, n=n, lanes=lanes):
                    v = parts[n][pl.ds(pl.multiple_of(t * 80, ONE), lanes * ONE), :].astype(F32)
                    v = v * v
                    here = [v[l * ONE:(l + 1) * ONE] for l in range(lanes)]
                    while len(here) > 1:
                        here = [sum(here[i:i + 2][1:], here[i]) for i in range(0, len(here), 2)]
                    return acc + here[0]
                total = lax.fori_loop(0, PART // ONE, add, total, unroll=6)
            here = (lax.rem(at_right + 4 - s, 4) == 0).astype(F32)
            pair = parts[right + s][93 * ONE:95 * ONE, :].astype(F32)
            extra = extra + here * (pair[:ONE] + pair[ONE:])
        bias = extra[:D // 128]
        square = jnp.sum(total, keepdims=True) + jnp.sum(bias * bias, keepdims=True)
        factor = jnp.minimum(F32(1.0), clip_ref[0] / jnp.sqrt(square))
        outs = []
        for s in range(4):
            for n, lanes, base, at, slot in ((left + s, 5, 0, at_left, wide_slots), (right + s, 4, WIDE, at_right, slots)):
                def put(t, carry, n=n, lanes=lanes, slot=slot, s=s):
                    v = parts[n][pl.ds(pl.multiple_of(t * 80, ONE), lanes * ONE), :].astype(F32) * factor
                    rows = pl.ds(pl.multiple_of(t * ONE, ONE), ONE)
                    for l in range(lanes):
                        slot[s, rows, l * 128:(l + 1) * 128] = v[l * ONE:(l + 1) * ONE]
                    return carry
                lax.fori_loop(0, PART // ONE, put, 0, unroll=6)
                row0 = pl.multiple_of(lax.rem(at + 4 - s, 4) * PART, PART)
                out = pltpu.make_async_copy(
                    slot.at[s], w_ref.at[pl.ds(row0, PART), base:base + lanes * 128], out_sem.at[len(outs)]
                )
                out.start()
                outs.append(out)
        for r in range(D // 128):
            b_ref[r * 128:(r + 1) * 128] = (bias[r:r + 1] * factor).reshape(128)
        loss_ref[0] = jnp.sum(extra[D // 128:D // 128 + 1, :]) * F32(1.0 / TOTAL)
        for out in outs:
            out.wait()

    @pl.when(idx_ref[0] == 0)
    def _():
        whole(0, 4, idx_ref[1], idx_ref[2])

    @pl.when(idx_ref[0] == 1)
    def _():
        whole(4, 0, idx_ref[2], idx_ref[1])


def sds(shape, kind):
    return jax.ShapeDtypeStruct(shape, kind)


def local(images, texts, head_weight, head_bias, logit_scale, logit_shift, loss_scale, clip_norm):
    core = lax.axis_index("core")
    at_x, at_y = lax.axis_index("x"), lax.axis_index(("yh", "yl"))
    at = jnp.where(core == 0, at_x, at_y)
    at_other = jnp.where(core == 0, at_y, at_x)
    idx = jnp.stack([core, at, at_other]).astype(jnp.int32)
    scal = jnp.stack([logit_scale[0], logit_shift[0], -loss_scale[0] / TOTAL])

    txt = [texts, shifted(texts, "core", 1), shifted(texts, "yh", 1)]
    txt.append(lax.ppermute(texts, ("yh", "core"), [(0, 3), (1, 2), (2, 1), (3, 0)]))
    img = [images] + [shifted(images, "x", s) for s in (2, 1, 3)]

    bias_row = head_bias[None]
    sides = [
        pl.pallas_call(
            text_kernel,
            out_shape=(sds((OWN, D), F32), sds((OWN, 128), F32)),
            in_specs=[VMEM] * 3, out_specs=(VMEM, VMEM), compiler_params=room(10),
            cost_estimate=pl.CostEstimate(flops=2 * OWN * D * D, bytes_accessed=3_600_000, transcendentals=OWN),
            name="text_side",
        )(block, head_weight, bias_row)
        for block in txt
    ]
    ys, invs = [y for y, _ in sides], [v for _, v in sides]
    gs, keep, give = pl.pallas_call(
        pair_kernel,
        out_shape=(sds((4 * OWN, 4 * OWN), BF16),) + (sds((4 * OWN, WIDE), BF16),) * 2,
        in_specs=[SMEM, SMEM] + [VMEM] * 12, out_specs=(VMEM,) * 3, compiler_params=room(20),
        scratch_shapes=[
            pltpu.VMEM((4 * OWN, D), BF16), pltpu.VMEM((4 * OWN, D), BF16), pltpu.VMEM((ONE, 128), F32),
        ],
        cost_estimate=pl.CostEstimate(flops=4 * 512 * 512 * D, bytes_accessed=5_500_000, transcendentals=800_000),
        name="pairs",
    )(idx, scal, *img, *ys, *invs)
    ig0, ig1, ig2, ig3 = pl.pallas_call(
        image_kernel,
        out_shape=(sds((OWN, D), F32),) + (sds((OWN, D), BF16),) * 3,
        in_specs=[SMEM] + [VMEM] * 9, out_specs=(VMEM,) * 4, compiler_params=room(20),
        scratch_shapes=[pltpu.VMEM((4 * OWN, D), BF16)],
        cost_estimate=pl.CostEstimate(flops=2 * 512 * 512 * D, bytes_accessed=5_500_000, transcendentals=512),
        name="image_side",
    )(scal, *img, *ys, gs)

    got = shifted(give, "core", 1)
    parts = pl.pallas_call(
        head_kernel,
        out_shape=(sds((PART, WIDE), BF16),) * 4,
        in_specs=[SMEM] + [VMEM] * 6, out_specs=(VMEM,) * 4, compiler_params=room(14),
        scratch_shapes=[
            pltpu.VMEM((4 * OWN, D), BF16), pltpu.VMEM((4 * OWN, WIDE), BF16), pltpu.VMEM((4, PART, WIDE), BF16),
        ],
        cost_estimate=pl.CostEstimate(flops=2 * 512 * D * WIDE, bytes_accessed=4_000_000, transcendentals=0),
        name="head",
    )(idx, *txt, keep, got)
    r2, r1, r3 = [lax.ppermute(parts[s], ALL, around(s)) for s in (2, 1, 3)]
    tiles = pl.pallas_call(
        tile_kernel,
        out_shape=sds((TILES * ONE, 128), BF16),
        in_specs=[SMEM] + [VMEM] * 4, out_specs=VMEM, compiler_params=room(8),
        cost_estimate=pl.CostEstimate(flops=4 * PART * WIDE, bytes_accessed=1_900_000, transcendentals=0),
        name="tiles",
    )(idx, parts[0], r1, r2, r3)
    ig1, ig2, ig3, tiles = lax.optimization_barrier((ig1, ig2, ig3, tiles))
    back = [shifted(ig1, "x", -2), shifted(ig2, "x", -1), shifted(ig3, "x", -3)]
    sums = lax.all_to_all(tiles.reshape(32, 48, 128), ALL, 0, 0, axis_index_groups=groups_second(), tiled=True)
    sums, back[1], back[2] = lax.optimization_barrier((sums, back[1], back[2]))
    s2 = jnp.sum(sums.astype(F32), axis=0)
    at2 = jnp.where(core == 0, lax.axis_index(("yh", "z", "yl")), lax.axis_index(("x", "z")))
    f_hi, f_lo = hi_lo(s2[:ONE] + s2[ONE:2 * ONE])
    special = jnp.concatenate([f_hi, f_lo, jnp.zeros((ONE, 128), BF16)], 0)
    mine = jnp.where(at2 == 0, special, s2.astype(BF16))
    copies = jnp.broadcast_to(mine, (32, 48, 128))
    turned = [group[::-1] for group in groups_second()]
    a1 = lax.all_to_all(copies, ALL, 0, 0, axis_index_groups=turned, tiled=True)
    a1, back = lax.optimization_barrier((a1, back))
    image_grad = ig0 + back[0].astype(F32) + back[1].astype(F32) + back[2].astype(F32)

    b0 = a1.reshape(TILES * ONE, 128)
    b2, b1, b3 = [lax.ppermute(b0, ALL, around(s)) for s in (2, 1, 3)]
    own_half = (b0, b1, b2, b3)
    other_half = [shifted(b, "core", 1) for b in own_half]
    weight_grad, bias_grad, loss = pl.pallas_call(
        last_kernel,
        out_shape=(sds((D, D), F32), sds((D,), F32), sds((1,), F32)),
        in_specs=[SMEM, SMEM] + [VMEM] * 8, out_specs=(ANY, VMEM, SMEM), compiler_params=room(14),
        scratch_shapes=[
            pltpu.VMEM((4, PART, D - WIDE), F32), pltpu.VMEM((4, PART, WIDE), F32), pltpu.SemaphoreType.DMA((8,)),
        ],
        cost_estimate=pl.CostEstimate(flops=4 * D * D, bytes_accessed=8_500_000, transcendentals=0),
        name="last",
    )(idx, clip_norm, *own_half, *other_half)
    return image_grad, weight_grad, bias_grad, loss


def solution(mesh):
    fine = Mesh(mesh.devices.reshape(NX, NYH, NC, NZ, NYL), ALL)
    placed = (P(ALL, None), P(ALL, None), P(), P(), P(), P(), P(), P())
    return jax.shard_map(
        local, mesh=fine, in_specs=placed, out_specs=(P(ALL, None), P(), P(), P()), check_vma=False
    )
```

time: 125 us -> 115 us (0.920)
  starting transfers between devices: 54.3 us -> 49.6 us
  waiting for transfers between devices: 41.3 us -> 37.2 us
  Pallas kernels: 19.8 us -> 17.1 us
  local copies, waits for them, and re-layouts: 3.96 us -> 6.05 us
    all_to_all x1, waiting for transfers between devices: 10.5 us -> 0.01 us  [local(): lax.all_to_all(tiles.reshape(32, 48, 128), ALL, 0, 0, axis_index_groups=g...]
    ppermute x13, starting transfers between devices: 23.6 us -> 16.2 us  [shifted(): lax.ppermute(block, axis, [(i, (i + distance) % size) for i in range(size)])]
    ppermute x13, waiting for transfers between devices: 17.9 us -> 24 us  [shifted(): lax.ppermute(block, axis, [(i, (i + distance) % size) for i in range(size)])]
    ppermute x3, waiting for transfers between devices: 1.79 us -> 6.85 us  [local(): b2, b1, b3 = [lax.ppermute(b0, ALL, around(s)) for s in (2, 1, 3)]]
    ppermute x1, waiting for transfers between devices: 2.97 us -> 0.01 us  [local(): lax.ppermute(texts, ('yh', 'core'), [(0, 3), (1, 2), (2, 1), (3, 0)])]
    pallas_call x3 -> x7, Pallas kernels: 16.1 us -> 13.5 us  [the longest x1 4.51 us: local(): pl.pallas_call(last_kernel, out_shape=(sds((D, D), F32), sds((D,), F32),...]
    unnamed x8 -> x10, local copies, waits for them, and re-layouts: 2.37 us -> 4.47 us
    ppermute x3, starting transfers between devices: 2.55 us -> 4.61 us  [local(): b2, b1, b3 = [lax.ppermute(b0, ALL, around(s)) for s in (2, 1, 3)]]
  transfers between devices with their start and end apart: 22 -> 22, of which waited for: 11 -> 12; matrix products, arithmetic and copies ran while one was open for 2% -> 2% of each run, Pallas kernels for 3% -> 4%
where the time goes in v3:
time: 115 us
  starting transfers between devices  49.6 us (43%)
  waiting for transfers between devices  37.2 us (32%)
  Pallas kernels  17.1 us (15%)
  local copies, waits for them, and re-layouts  6.05 us (5%)
  between operations  3.55 us (3%)
  other arithmetic  1.24 us (1%)
    ppermute x13, waiting for transfers between devices, shifted(): lax.ppermute(block, axis, [(i, (i + distance) % size) for i in range(size)])  24 us
    ppermute x13, starting transfers between devices, shifted(): lax.ppermute(block, axis, [(i, (i + distance) % size) for i in range(size)])  16.2 us
    all_to_all x1, starting transfers between devices, local(): lax.all_to_all(tiles.reshape(32, 48, 128), ALL, 0, 0, axis_index_groups=g...  10.6 us
    all_to_all x1, starting transfers between devices, local(): a1 = lax.all_to_all(copies, ALL, 0, 0, axis_index_groups=turned, tiled=True)  9.39 us
    ppermute x3, waiting for transfers between devices, local(): b2, b1, b3 = [lax.ppermute(b0, ALL, around(s)) for s in (2, 1, 3)]  6.85 us
    ppermute x3, waiting for transfers between devices, local(): r2, r1, r3 = [lax.ppermute(parts[s], ALL, around(s)) for s in (2, 1, 3)]  6.31 us
    ppermute x3, starting transfers between devices, local(): b2, b1, b3 = [lax.ppermute(b0, ALL, around(s)) for s in (2, 1, 3)]  4.61 us
    pallas_call x1, Pallas kernels, local(): pl.pallas_call(last_kernel, out_shape=(sds((D, D), F32), sds((D,), F32),...  4.51 us
  transfers between devices with their start and end apart: 22, of which 12 were waited for; matrix products, arithmetic and copies ran while one was open for 2% of the time, Pallas kernels for 4%

profile of v3, /device:TPU:1, one launch (start us, length us, event | category | flops | bytes accessed | tf_op | source)
XLA Modules:
  0.0 114.7 jit_solution(2332303640397052191)
XLA Ops:
  0.6 4.4 %collective-permute-start.5 = (bf16[128,1152]{1,0:T(8,128)(2,1)}, bf16[128,1152]{1,0:T(8,128)(2,1)S(1)}, u32[]{:S(2)}, u32[]{:S(2)}) collective-permute-start(bf16[128,1152]{1,0:T(8,128)(2,1)} %t0.1), channel_id=1, source_target_pairs={{0,48},{16,32},{32,16},{48,0},{1,49},{17,33},{33,17},{49,1},{2,50}... | collective-permute-start | bytes 884744 | tf_op jit(solution)/shard_map/ppermute | solution.py:282
  5.0 2.5 %collective-permute-start.2 = (bf16[128,1152]{1,0:T(8,128)(2,1)}, bf16[128,1152]{1,0:T(8,128)(2,1)S(1)}, u32[]{:S(2)}, u32[]{:S(2)}) collective-permute-start(bf16[128,1152]{1,0:T(8,128)(2,1)} %i0.3), channel_id=1, source_target_pairs={{0,192},{64,0},{128,64},{192,128},{1,193},{65,1},{129,65},{193,129... | collective-permute-start | bytes 884744 | tf_op jit(solution)/shard_map/ppermute | solution.py:64
  9.0 1.7 %copy-done = bf16[1152,1152]{1,0:T(8,128)(2,1)S(1)} copy-done((bf16[1152,1152]{1,0:T(8,128)(2,1)S(1)}, bf16[1152,1152]{1,0:T(8,128)(2,1)}, u32[]{:S(2)}) %copy-start) | copy-done | bytes 2654232
  15.8 1.8 %copy-done.1 = bf16[1152,1152]{1,0:T(8,128)(2,1)S(1)} copy-done((bf16[1152,1152]{1,0:T(8,128)(2,1)S(1)}, bf16[1152,1152]{1,0:T(8,128)(2,1)}, u32[]{:S(2)}) %copy-start.1) | copy-done | bytes 2654232
  20.0 3.3 %collective-permute-done.i1 = bf16[128,1152]{1,0:T(8,128)(2,1)S(1)} collective-permute-done((bf16[128,1152]{1,0:T(8,128)(2,1)}, bf16[128,1152]{1,0:T(8,128)(2,1)S(1)}, u32[]{:S(2)}, u32[]{:S(2)}) %collective-permute-start) | collective-permute-done | bytes 294944 | tf_op jit(solution)/shard_map/ppermute | solution.py:64
  23.3 4.3 %pairs.1 = (bf16[512,512]{1,0:T(8,128)(2,1)S(1)}, bf16[512,640]{1,0:T(8,128)(2,1)S(1)}, bf16[512,640]{1,0:T(8,128)(2,1)S(1)}) custom-call(s32[3]{0:T(128)S(1)} %pad_add_fusion.core_ref.idx_ref, f32[3]{0:T(128)S(1)} %pad_maximum_fusion.scal_ref, bf16[128,1152]{1,0:T(8,128)(2,1)S(1)} %copy-done.4, bf16[128,1152]{1,0:T(8,128)(2,1)S(1)} %collective-permute-done.i1, ...), custom_call_target="tpu_custom_call" | custom-call | flops 1207959552 | bytes 5500000 | tf_op jit(solution)/shard_map/pairs/pallas_call | solution.py:297
  27.6 2.3 %collective-permute-start.6 = (bf16[512,640]{1,0:T(8,128)(2,1)S(1)}, bf16[512,640]{1,0:T(8,128)(2,1)S(1)}, u32[]{:S(2)}, u32[]{:S(2)}) collective-permute-start(bf16[512,640]{1,0:T(8,128)(2,1)S(1)} %get-tuple-element.51), channel_id=1, source_target_pairs={{0,16},{16,0},{1,17},{17,1},{2,18},{18,2},{3,19},{19,3},{4,20},{20... | collective-permute-start | bytes 1966088 | tf_op jit(solution)/shard_map/ppermute | solution.py:64
  31.7 2.1 %head.1 = (bf16[288,640]{1,0:T(8,128)(2,1)S(1)}, bf16[288,640]{1,0:T(8,128)(2,1)S(1)}, bf16[288,640]{1,0:T(8,128)(2,1)S(1)}, bf16[288,640]{1,0:T(8,128)(2,1)S(1)}) custom-call(s32[3]{0:T(128)S(1)} %pad_add_fusion.core_ref.idx_ref, bf16[128,1152]{1,0:T(8,128)(2,1)S(1)} %copy-done.3, bf16[128,1152]{1,0:T(8,128)(2,1)S(1)} %collective-permute-done.3.t_ref.t1, ...), custom_call_target="tpu_custom_call" | custom-call | flops 754974720 | bytes 4000000 | tf_op jit(solution)/shard_map/head/pallas_call | solution.py:317
  34.5 2.6 %collective-permute-start.8 = (bf16[288,640]{1,0:T(8,128)(2,1)S(1)}, bf16[288,640]{1,0:T(8,128)(2,1)S(1)}, u32[]{:S(2)}, u32[]{:S(2)}) collective-permute-start(bf16[288,640]{1,0:T(8,128)(2,1)S(1)} %get-tuple-element.54), channel_id=1, source_target_pairs={{0,128},{1,129},{2,130},{3,131},{4,132},{5,133},{6,134},{7,135},{8... | collective-permute-start | bytes 1105928 | tf_op jit(solution)/shard_map/ppermute | solution.py:327
  38.2 1.9 %image_side.1 = (f32[128,1152]{1,0:T(8,128)S(1)}, bf16[128,1152]{1,0:T(8,128)(2,1)S(1)}, bf16[128,1152]{1,0:T(8,128)(2,1)S(1)}, bf16[128,1152]{1,0:T(8,128)(2,1)S(1)}) custom-call(f32[3]{0:T(128)S(1)} %pad_maximum_fusion.scal_ref, bf16[128,1152]{1,0:T(8,128)(2,1)S(1)} %copy-done.4, bf16[128,1152]{1,0:T(8,128)(2,1)S(1)} %collective-permute-done.i1, ...), custom_call_target="tpu_custom_call" | custom-call | flops 603979776 | bytes 5500000 | tf_op jit(solution)/shard_map/image_side/pallas_call | solution.py:307
  40.0 1.7 %collective-permute-done.7.a1 = bf16[288,640]{1,0:T(8,128)(2,1)S(1)} collective-permute-done((bf16[288,640]{1,0:T(8,128)(2,1)S(1)}, bf16[288,640]{1,0:T(8,128)(2,1)S(1)}, u32[]{:S(2)}, u32[]{:S(2)}) %collective-permute-start.7) | collective-permute-done | bytes 368672 | tf_op jit(solution)/shard_map/ppermute | solution.py:327
  41.8 4.5 %collective-permute-done.8.a2 = bf16[288,640]{1,0:T(8,128)(2,1)S(1)} collective-permute-done((bf16[288,640]{1,0:T(8,128)(2,1)S(1)}, bf16[288,640]{1,0:T(8,128)(2,1)S(1)}, u32[]{:S(2)}, u32[]{:S(2)}) %collective-permute-start.8) | collective-permute-done | bytes 368672 | tf_op jit(solution)/shard_map/ppermute | solution.py:327
  47.8 10.6 %all-to-all-start = ((bf16[32,48,128]{2,1,0:T(8,128)(2,1)}), bf16[32,48,128]{2,1,0:T(8,128)(2,1)S(1)}, u32[]{:S(2)}, u32[]{:S(2)}) async-start(bf16[32,48,128]{2,1,0:T(8,128)(2,1)} %bitcast.3), calls=%async_computation | async-start | bytes 786432 | tf_op jit(solution)/shard_map/all_to_all | solution.py:337
  58.4 2.6 %collective-permute-start.10 = (bf16[128,1152]{1,0:T(8,128)(2,1)S(1)}, bf16[128,1152]{1,0:T(8,128)(2,1)S(1)}, u32[]{:S(2)}, u32[]{:S(2)}) collective-permute-start(bf16[128,1152]{1,0:T(8,128)(2,1)S(1)} %get-tuple-element.57), channel_id=1, source_target_pairs={{0,192},{64,0},{128,64},{192,128},{1,193},{65,1},{129,65},{193,129... | collective-permute-start | bytes 884744 | tf_op jit(solution)/shard_map/ppermute | solution.py:64
  61.1 7.2 %collective-permute-done.10 = bf16[128,1152]{1,0:T(8,128)(2,1)S(1)} collective-permute-done((bf16[128,1152]{1,0:T(8,128)(2,1)S(1)}, bf16[128,1152]{1,0:T(8,128)(2,1)S(1)}, u32[]{:S(2)}, u32[]{:S(2)}) %collective-permute-start.10) | collective-permute-done | bytes 294944 | tf_op jit(solution)/shard_map/ppermute | solution.py:64
  68.2 2.7 %collective-permute-done.11 = bf16[128,1152]{1,0:T(8,128)(2,1)S(1)} collective-permute-done((bf16[128,1152]{1,0:T(8,128)(2,1)S(1)}, bf16[128,1152]{1,0:T(8,128)(2,1)S(1)}, u32[]{:S(2)}, u32[]{:S(2)}) %collective-permute-start.11) | collective-permute-done | bytes 294944 | tf_op jit(solution)/shard_map/ppermute | solution.py:64
  71.9 9.4 %all-to-all-start.1 = ((bf16[32,48,128]{2,1,0:T(8,128)(2,1)}), bf16[32,48,128]{2,1,0:T(8,128)(2,1)S(1)}, u32[]{:S(2)}, u32[]{:S(2)}) async-start(bf16[32,48,128]{2,1,0:T(8,128)(2,1)} %broadcast_in_dim.11), calls=%async_computation.1 | async-start | bytes 786432 | tf_op jit(solution)/shard_map/all_to_all | solution.py:346
  82.5 8.4 %collective-permute-done.12 = bf16[128,1152]{1,0:T(8,128)(2,1)S(1)} collective-permute-done((bf16[128,1152]{1,0:T(8,128)(2,1)S(1)}, bf16[128,1152]{1,0:T(8,128)(2,1)S(1)}, u32[]{:S(2)}, u32[]{:S(2)}) %collective-permute-start.12) | collective-permute-done | bytes 294944 | tf_op jit(solution)/shard_map/ppermute | solution.py:64
  90.9 3.2 %collective-permute-start.15 = (bf16[1536,128]{1,0:T(8,128)(2,1)S(1)}, bf16[1536,128]{1,0:T(8,128)(2,1)S(1)}, u32[]{:S(2)}, u32[]{:S(2)}) collective-permute-start(bf16[1536,128]{1,0:T(8,128)(2,1)S(1)} %bitcast.5), channel_id=1, source_target_pairs={{0,192},{1,193},{2,194},{3,195},{4,196},{5,197},{6,198},{7,199},{8... | collective-permute-start | bytes 1179656 | tf_op jit(solution)/shard_map/ppermute | solution.py:351
  96.2 2.3 %collective-permute-start.16 = (bf16[1536,128]{1,0:T(8,128)(2,1)S(1)}, bf16[1536,128]{1,0:T(8,128)(2,1)S(1)}, u32[]{:S(2)}, u32[]{:S(2)}) collective-permute-start(bf16[1536,128]{1,0:T(8,128)(2,1)S(1)} %bitcast.8), channel_id=1, source_target_pairs={{0,16},{16,0},{1,17},{17,1},{2,18},{18,2},{3,19},{19,3},{4,20},{20... | collective-permute-start | bytes 1179656 | tf_op jit(solution)/shard_map/ppermute | solution.py:64
  98.5 4.6 %collective-permute-done.15.p3 = bf16[1536,128]{1,0:T(8,128)(2,1)S(1)} collective-permute-done((bf16[1536,128]{1,0:T(8,128)(2,1)S(1)}, bf16[1536,128]{1,0:T(8,128)(2,1)S(1)}, u32[]{:S(2)}, u32[]{:S(2)}) %collective-permute-start.15) | collective-permute-done | bytes 393248 | tf_op jit(solution)/shard_map/ppermute | solution.py:351
  104.6 2.2 %collective-permute-done.13.p1 = bf16[1536,128]{1,0:T(8,128)(2,1)S(1)} collective-permute-done((bf16[1536,128]{1,0:T(8,128)(2,1)S(1)}, bf16[1536,128]{1,0:T(8,128)(2,1)S(1)}, u32[]{:S(2)}, u32[]{:S(2)}) %collective-permute-start.13) | collective-permute-done | bytes 393248 | tf_op jit(solution)/shard_map/ppermute | solution.py:351
  106.8 1.9 %collective-permute-start.17 = (bf16[1536,128]{1,0:T(8,128)(2,1)S(1)}, bf16[1536,128]{1,0:T(8,128)(2,1)S(1)}, u32[]{:S(2)}, u32[]{:S(2)}) collective-permute-start(bf16[1536,128]{1,0:T(8,128)(2,1)S(1)} %collective-permute-done.13.p1), channel_id=1, source_target_pairs={{0,16},{16,0},{1,17},{17,1},{2,18},{18,2},{3,19},{19,3},{4,20},{20... | collective-permute-start | bytes 1179656 | tf_op jit(solution)/shard_map/ppermute | solution.py:64
  110.1 4.5 %last.1 = (f32[1152,1152]{1,0:T(8,128)}, f32[1152]{0:T(1024)}, f32[1]{0:T(128)}) custom-call(s32[3]{0:T(128)S(1)} %pad_add_fusion.core_ref.idx_ref, f32[1]{0:T(128)S(6)} %copy.15.clip_ref, bf16[1536,128]{1,0:T(8,128)(2,1)S(1)} %bitcast.9, bf16[1536,128]{1,0:T(8,128)(2,1)S(1)} %collective-permute-done.13.p1, ...), custom_call_target="tpu_custom_call" | custom-call | flops 5308416 | bytes 8500000 | tf_op jit(solution)/shard_map/last/pallas_call | solution.py:354
  (49 shorter events, 18.4 us)
Async XLA Ops:
  0.6 13.8 %collective-permute-start.5 = (bf16[128,1152]{1,0:T(8,128)(2,1)}, bf16[128,1152]{1,0:T(8,128)(2,1)S(1)}, u32[]{:S(2)}, u32[]{:S(2)}) collective-permute-start(bf16[128,1152]{1,0:T(8,128)(2,1)} %t0.1), channel_id=1, source_target_pairs={{0,48},{16,32},{32,16},{48,0},{1,49},{17,33},{33,17},{49,1},{2,50}... | collective-permute-start | bytes 884744 | tf_op jit(solution)/shard_map/ppermute | solution.py:282
  5.0 13.3 %collective-permute-start.3 = (bf16[128,1152]{1,0:T(8,128)(2,1)}, bf16[128,1152]{1,0:T(8,128)(2,1)S(1)}, u32[]{:S(2)}, u32[]{:S(2)}) collective-permute-start(bf16[128,1152]{1,0:T(8,128)(2,1)} %t0.1), channel_id=1, source_target_pairs={{0,16},{16,0},{1,17},{17,1},{2,18},{18,2},{3,19},{19,3},{4,20},{20... | collective-permute-start | bytes 884744 | tf_op jit(solution)/shard_map/ppermute | solution.py:64
  5.0 15.0 %collective-permute-start.2 = (bf16[128,1152]{1,0:T(8,128)(2,1)}, bf16[128,1152]{1,0:T(8,128)(2,1)S(1)}, u32[]{:S(2)}, u32[]{:S(2)}) collective-permute-start(bf16[128,1152]{1,0:T(8,128)(2,1)} %i0.3), channel_id=1, source_target_pairs={{0,192},{64,0},{128,64},{192,128},{1,193},{65,1},{129,65},{193,129... | collective-permute-start | bytes 884744 | tf_op jit(solution)/shard_map/ppermute | solution.py:64
  7.5 12.5 %collective-permute-start.1 = (bf16[128,1152]{1,0:T(8,128)(2,1)}, bf16[128,1152]{1,0:T(8,128)(2,1)S(1)}, u32[]{:S(2)}, u32[]{:S(2)}) collective-permute-start(bf16[128,1152]{1,0:T(8,128)(2,1)} %i0.3), channel_id=1, source_target_pairs={{0,64},{64,128},{128,192},{192,0},{1,65},{65,129},{129,193},{193,1... | collective-permute-start | bytes 884744 | tf_op jit(solution)/shard_map/ppermute | solution.py:64
  7.5 11.8 %collective-permute-start.4 = (bf16[128,1152]{1,0:T(8,128)(2,1)}, bf16[128,1152]{1,0:T(8,128)(2,1)S(1)}, u32[]{:S(2)}, u32[]{:S(2)}) collective-permute-start(bf16[128,1152]{1,0:T(8,128)(2,1)} %t0.1), channel_id=1, source_target_pairs={{0,32},{32,0},{1,33},{33,1},{2,34},{34,2},{3,35},{35,3},{4,36},{36... | collective-permute-start | bytes 884744 | tf_op jit(solution)/shard_map/ppermute | solution.py:64
  11.7 11.7 %copy-start.4 = (bf16[128,1152]{1,0:T(8,128)(2,1)S(1)}, bf16[128,1152]{1,0:T(8,128)(2,1)}, u32[]{:S(2)}) copy-start(bf16[128,1152]{1,0:T(8,128)(2,1)} %i0.3) | copy-start | bytes 884740
  14.4 9.0 %collective-permute-start = (bf16[128,1152]{1,0:T(8,128)(2,1)}, bf16[128,1152]{1,0:T(8,128)(2,1)S(1)}, u32[]{:S(2)}, u32[]{:S(2)}) collective-permute-start(bf16[128,1152]{1,0:T(8,128)(2,1)} %i0.3), channel_id=1, source_target_pairs={{0,128},{64,192},{128,0},{192,64},{1,129},{65,193},{129,1},{193,65... | collective-permute-start | bytes 884744 | tf_op jit(solution)/shard_map/ppermute | solution.py:64
  18.3 13.4 %copy-start.3 = (bf16[128,1152]{1,0:T(8,128)(2,1)S(1)}, bf16[128,1152]{1,0:T(8,128)(2,1)}, u32[]{:S(2)}) copy-start(bf16[128,1152]{1,0:T(8,128)(2,1)} %t0.1) | copy-start | bytes 884740
  27.6 4.0 %collective-permute-start.6 = (bf16[512,640]{1,0:T(8,128)(2,1)S(1)}, bf16[512,640]{1,0:T(8,128)(2,1)S(1)}, u32[]{:S(2)}, u32[]{:S(2)}) collective-permute-start(bf16[512,640]{1,0:T(8,128)(2,1)S(1)} %get-tuple-element.51), channel_id=1, source_target_pairs={{0,16},{16,0},{1,17},{17,1},{2,18},{18,2},{3,19},{19,3},{4,20},{20... | collective-permute-start | bytes 1966088 | tf_op jit(solution)/shard_map/ppermute | solution.py:64
  33.8 7.9 %collective-permute-start.7 = (bf16[288,640]{1,0:T(8,128)(2,1)S(1)}, bf16[288,640]{1,0:T(8,128)(2,1)S(1)}, u32[]{:S(2)}, u32[]{:S(2)}) collective-permute-start(bf16[288,640]{1,0:T(8,128)(2,1)S(1)} %get-tuple-element.53), channel_id=1, source_target_pairs={{0,64},{1,65},{2,66},{3,67},{4,68},{5,69},{6,70},{7,71},{8,72},{9,... | collective-permute-start | bytes 1105928 | tf_op jit(solution)/shard_map/ppermute | solution.py:327
  34.5 11.8 %collective-permute-start.8 = (bf16[288,640]{1,0:T(8,128)(2,1)S(1)}, bf16[288,640]{1,0:T(8,128)(2,1)S(1)}, u32[]{:S(2)}, u32[]{:S(2)}) collective-permute-start(bf16[288,640]{1,0:T(8,128)(2,1)S(1)} %get-tuple-element.54), channel_id=1, source_target_pairs={{0,128},{1,129},{2,130},{3,131},{4,132},{5,133},{6,134},{7,135},{8... | collective-permute-start | bytes 1105928 | tf_op jit(solution)/shard_map/ppermute | solution.py:327
  37.1 9.2 %collective-permute-start.9 = (bf16[288,640]{1,0:T(8,128)(2,1)S(1)}, bf16[288,640]{1,0:T(8,128)(2,1)S(1)}, u32[]{:S(2)}, u32[]{:S(2)}) collective-permute-start(bf16[288,640]{1,0:T(8,128)(2,1)S(1)} %get-tuple-element.55), channel_id=1, source_target_pairs={{0,192},{1,193},{2,194},{3,195},{4,196},{5,197},{6,198},{7,199},{8... | collective-permute-start | bytes 1105928 | tf_op jit(solution)/shard_map/ppermute | solution.py:327
  47.8 23.1 %all-to-all-start = ((bf16[32,48,128]{2,1,0:T(8,128)(2,1)}), bf16[32,48,128]{2,1,0:T(8,128)(2,1)S(1)}, u32[]{:S(2)}, u32[]{:S(2)}) async-start(bf16[32,48,128]{2,1,0:T(8,128)(2,1)} %bitcast.3), calls=%async_computation | async-start | bytes 786432 | tf_op jit(solution)/shard_map/all_to_all | solution.py:337
  58.4 9.8 %collective-permute-start.10 = (bf16[128,1152]{1,0:T(8,128)(2,1)S(1)}, bf16[128,1152]{1,0:T(8,128)(2,1)S(1)}, u32[]{:S(2)}, u32[]{:S(2)}) collective-permute-start(bf16[128,1152]{1,0:T(8,128)(2,1)S(1)} %get-tuple-element.57), channel_id=1, source_target_pairs={{0,192},{64,0},{128,64},{192,128},{1,193},{65,1},{129,65},{193,129... | collective-permute-start | bytes 884744 | tf_op jit(solution)/shard_map/ppermute | solution.py:64
  61.0 10.0 %collective-permute-start.11 = (bf16[128,1152]{1,0:T(8,128)(2,1)S(1)}, bf16[128,1152]{1,0:T(8,128)(2,1)S(1)}, u32[]{:S(2)}, u32[]{:S(2)}) collective-permute-start(bf16[128,1152]{1,0:T(8,128)(2,1)S(1)} %get-tuple-element.58), channel_id=1, source_target_pairs={{0,64},{64,128},{128,192},{192,0},{1,65},{65,129},{129,193},{193,1... | collective-permute-start | bytes 884744 | tf_op jit(solution)/shard_map/ppermute | solution.py:64
  71.9 19.0 %all-to-all-start.1 = ((bf16[32,48,128]{2,1,0:T(8,128)(2,1)}), bf16[32,48,128]{2,1,0:T(8,128)(2,1)S(1)}, u32[]{:S(2)}, u32[]{:S(2)}) async-start(bf16[32,48,128]{2,1,0:T(8,128)(2,1)} %broadcast_in_dim.11), calls=%async_computation.1 | async-start | bytes 786432 | tf_op jit(solution)/shard_map/all_to_all | solution.py:346
  81.3 9.6 %collective-permute-start.12 = (bf16[128,1152]{1,0:T(8,128)(2,1)S(1)}, bf16[128,1152]{1,0:T(8,128)(2,1)S(1)}, u32[]{:S(2)}, u32[]{:S(2)}) collective-permute-start(bf16[128,1152]{1,0:T(8,128)(2,1)S(1)} %get-tuple-element.60), channel_id=1, source_target_pairs={{0,128},{64,192},{128,0},{192,64},{1,129},{65,193},{129,1},{193,65... | collective-permute-start | bytes 884744 | tf_op jit(solution)/shard_map/ppermute | solution.py:64
  90.9 12.2 %collective-permute-start.15 = (bf16[1536,128]{1,0:T(8,128)(2,1)S(1)}, bf16[1536,128]{1,0:T(8,128)(2,1)S(1)}, u32[]{:S(2)}, u32[]{:S(2)}) collective-permute-start(bf16[1536,128]{1,0:T(8,128)(2,1)S(1)} %bitcast.5), channel_id=1, source_target_pairs={{0,192},{1,193},{2,194},{3,195},{4,196},{5,197},{6,198},{7,199},{8... | collective-permute-start | bytes 1179656 | tf_op jit(solution)/shard_map/ppermute | solution.py:351
  94.2 8.9 %collective-permute-start.14 = (bf16[1536,128]{1,0:T(8,128)(2,1)S(1)}, bf16[1536,128]{1,0:T(8,128)(2,1)S(1)}, u32[]{:S(2)}, u32[]{:S(2)}) collective-permute-start(bf16[1536,128]{1,0:T(8,128)(2,1)S(1)} %bitcast.6), channel_id=1, source_target_pairs={{0,128},{1,129},{2,130},{3,131},{4,132},{5,133},{6,134},{7,135},{8... | collective-permute-start | bytes 1179656 | tf_op jit(solution)/shard_map/ppermute | solution.py:351
  95.5 11.3 %collective-permute-start.13 = (bf16[1536,128]{1,0:T(8,128)(2,1)S(1)}, bf16[1536,128]{1,0:T(8,128)(2,1)S(1)}, u32[]{:S(2)}, u32[]{:S(2)}) collective-permute-start(bf16[1536,128]{1,0:T(8,128)(2,1)S(1)} %bitcast.7), channel_id=1, source_target_pairs={{0,64},{1,65},{2,66},{3,67},{4,68},{5,69},{6,70},{7,71},{8,72},{9,... | collective-permute-start | bytes 1179656 | tf_op jit(solution)/shard_map/ppermute | solution.py:351
  96.2 13.5 %collective-permute-start.16 = (bf16[1536,128]{1,0:T(8,128)(2,1)S(1)}, bf16[1536,128]{1,0:T(8,128)(2,1)S(1)}, u32[]{:S(2)}, u32[]{:S(2)}) collective-permute-start(bf16[1536,128]{1,0:T(8,128)(2,1)S(1)} %bitcast.8), channel_id=1, source_target_pairs={{0,16},{16,0},{1,17},{17,1},{2,18},{18,2},{3,19},{19,3},{4,20},{20... | collective-permute-start | bytes 1179656 | tf_op jit(solution)/shard_map/ppermute | solution.py:64
  103.1 6.5 %collective-permute-start.19 = (bf16[1536,128]{1,0:T(8,128)(2,1)S(1)}, bf16[1536,128]{1,0:T(8,128)(2,1)S(1)}, u32[]{:S(2)}, u32[]{:S(2)}) collective-permute-start(bf16[1536,128]{1,0:T(8,128)(2,1)S(1)} %collective-permute-done.15.p3), channel_id=1, source_target_pairs={{0,16},{16,0},{1,17},{17,1},{2,18},{18,2},{3,19},{19,3},{4,20},{20... | collective-permute-start | bytes 1179656 | tf_op jit(solution)/shard_map/ppermute | solution.py:64
  103.1 6.5 %collective-permute-start.18 = (bf16[1536,128]{1,0:T(8,128)(2,1)S(1)}, bf16[1536,128]{1,0:T(8,128)(2,1)S(1)}, u32[]{:S(2)}, u32[]{:S(2)}) collective-permute-start(bf16[1536,128]{1,0:T(8,128)(2,1)S(1)} %collective-permute-done.14.p2), channel_id=1, source_target_pairs={{0,16},{16,0},{1,17},{17,1},{2,18},{18,2},{3,19},{19,3},{4,20},{20... | collective-permute-start | bytes 1179656 | tf_op jit(solution)/shard_map/ppermute | solution.py:64
  106.8 3.2 %collective-permute-start.17 = (bf16[1536,128]{1,0:T(8,128)(2,1)S(1)}, bf16[1536,128]{1,0:T(8,128)(2,1)S(1)}, u32[]{:S(2)}, u32[]{:S(2)}) collective-permute-start(bf16[1536,128]{1,0:T(8,128)(2,1)S(1)} %collective-permute-done.13.p1), channel_id=1, source_target_pairs={{0,16},{16,0},{1,17},{17,1},{2,18},{18,2},{3,19},{19,3},{4,20},{20... | collective-permute-start | bytes 1179656 | tf_op jit(solution)/shard_map/ppermute | solution.py:64
  (3 other events, 4.5 us)

commit v4 on v3

--- a/solution.py
+++ b/solution.py
@@ -12,8 +12,12 @@
 D, OWN = 1152, 128
 WIDE = 640
 PART = 288
-TILES = 96
 ONE = 16
+LANES = 4
+HALF = PART // 2
+REAL = 81
+USED = 83 * ONE
+ALLOT = 96 * ONE
 TOTAL = 32768
 
 
@@ -40,10 +44,10 @@
 def groups_second():
     out = []
     for x in range(NX):
-        out.append([place(x, yh, 0, z, yl) for yh in range(NYH) for z in range(NZ) for yl in range(NYL)])
+        out.append([place(x, yh, 0, z, yl) for z in range(NZ) for yh in range(NYH) for yl in range(NYL)])
     for yh in range(NYH):
         for yl in range(NYL):
-            out.append([place(x, yh, 1, z, yl) for x in range(NX) for z in range(NZ)])
+            out.append([place(x, yh, 1, z, yl) for z in range(NZ) for x in range(NX)])
     return out
 
 
@@ -69,7 +73,8 @@
     return hi, (value - hi.astype(F32)).astype(BF16)
 
 
-def text_kernel(t_ref, w_ref, b_ref, y_ref, inv_ref):
+def text_kernel(t_ref, w_ref, b_ref, y_ref, inv_ref, flip_ref):
+    flip_ref[...] = t_ref[...].T
     u = jnp.dot(t_ref[...], w_ref[...], preferred_element_type=F32) + b_ref[...]
     inv = lax.rsqrt(jnp.sum(u * u, axis=1, keepdims=True) + EPS)
     y_ref[...] = u * inv
@@ -120,37 +125,30 @@
             y = (y0, y1, y2, y3)[k][...]
             du = (dyk - y * jnp.sum(y * dyk, axis=1, keepdims=True)) * (v0, v1, v2, v3)[k][:, 0:1]
             bias = bias + jnp.sum(du, axis=0, keepdims=True)
-            left, right = du[:, :WIDE].astype(BF16), du[:, WIDE:].astype(BF16)
+            parts = [du[:, 512 * c:512 * (c + 1)].astype(BF16) for c in range(2)]
+            shared = du[:, 1024:].astype(BF16)
+            keep_ref[here, 512:] = shared
+            give_ref[here, 512:] = shared
 
             @pl.when(first)
             def _():
-                keep_ref[here, :] = left
-                give_ref[here, :D - WIDE] = right
+                keep_ref[here, :512] = parts[0]
+                give_ref[here, :512] = parts[1]
 
             @pl.when(jnp.logical_not(first))
             def _():
-                give_ref[here, :] = left
-                keep_ref[here, :D - WIDE] = right
+                give_ref[here, :512] = parts[0]
+                keep_ref[here, :512] = parts[1]
     ext[...] = jnp.zeros((ONE, 128), F32)
     for r in range(D // 128):
         ext[r:r + 1, :] = bias[:, r * 128:(r + 1) * 128]
     lane = lax.broadcasted_iota(jnp.int32, (1, 128), 1)
     ext[D // 128:D // 128 + 1, :] = jnp.where(lane == 0, loss, 0.0)
     hi, lo = hi_lo(ext[...])
-    rest = jnp.zeros((4 * OWN - 2 * ONE, WIDE - (D - WIDE)), BF16)
-
-    def extras(ref):
-        ref[0:ONE, D - WIDE:] = hi
-        ref[ONE:2 * ONE, D - WIDE:] = lo
-        ref[2 * ONE:, D - WIDE:] = rest
-
-    @pl.when(first)
-    def _():
-        extras(give_ref)
-
-    @pl.when(jnp.logical_not(first))
-    def _():
-        extras(keep_ref)
+    for ref in (keep_ref, give_ref):
+        ref[4 * OWN:, 128:] = jnp.zeros((2 * ONE, WIDE - 128), BF16)
+        ref[4 * OWN:4 * OWN + ONE, :128] = hi
+        ref[4 * OWN + ONE:, :128] = lo
 
 
 def image_kernel(scal_ref, i0, i1, i2, i3, y0, y1, y2, y3, gs, g0, g1, g2, g3, yb):
@@ -170,87 +168,79 @@
             target[...] = out.astype(target.dtype)
 
 
-def head_kernel(idx_ref, t0, t1, t2, t3, keep_ref, got_ref, o0, o1, o2, o3, t_all, both, rw):
-    for k, ref in enumerate((t0, t1, t2, t3)):
+def head_kernel(idx_ref, f0, f1, f2, f3, keep_ref, got_ref, o0, o1, o2, o3, flips, both, rw, shared):
+    for k, ref in enumerate((f0, f1, f2, f3)):
         rows, swap = slice(k * OWN, (k + 1) * OWN), slice((k ^ 1) * OWN, ((k ^ 1) + 1) * OWN)
-        t_all[rows, :] = ref[...]
+        flips[:, rows] = ref[...]
         both[rows, :] = (keep_ref[rows, :].astype(F32) + got_ref[swap, :].astype(F32)).astype(BF16)
-    tail = slice(D - WIDE, WIDE)
-    last = idx_ref[0] == 1
-    e = keep_ref[0:2 * ONE, tail].astype(F32) + got_ref[0:2 * ONE, tail].astype(F32)
+    e = keep_ref[4 * OWN:, :128].astype(F32) + got_ref[4 * OWN:, :128].astype(F32)
     hi, lo = hi_lo(e[:ONE] + e[ONE:])
     for q in range(4):
-        rw[q] = lax.dot_general(
-            t_all[:, q * PART:(q + 1) * PART], both[...], (((0,), (0,)), ((), ())), preferred_element_type=F32
-        ).astype(BF16)
-
-    @pl.when(last)
-    def _():
-        for q in range(4):
-            rw[q, :, tail] = jnp.zeros((PART, 128), BF16)
-        rw[0, 0:ONE, tail] = hi
-        rw[0, ONE:2 * ONE, tail] = lo
-
+        part = jnp.dot(flips[q * PART:(q + 1) * PART, :], both[...], preferred_element_type=F32).astype(BF16)
+        for t in range(PART // ONE):
+            for l in range(LANES):
+                n = t * LANES + l
+                rw[q, n * ONE:(n + 1) * ONE, :] = part[t * ONE:(t + 1) * ONE, l * 128:(l + 1) * 128]
+        shared[q] = part[:, 512:]
+        rw[q, 72 * ONE:REAL * ONE, :] = shared[q, pl.ds(pl.multiple_of(idx_ref[0] * HALF, HALF), HALF), :]
+        rw[q, REAL * ONE:, :] = jnp.zeros((2 * ONE, 128), BF16)
+    rw[0, REAL * ONE:(REAL + 1) * ONE, :] = hi
+    rw[0, (REAL + 1) * ONE:, :] = lo
     for s, ref in enumerate((o0, o1, o2, o3)):
         ref[...] = rw[lax.rem(idx_ref[1] + s, 4)]
 
 
-def tile_kernel(idx_ref, a0, a1, a2, a3, out):
+def tile_kernel(a0, a1, a2, a3, out):
     total = a0[...].astype(F32) + a1[...].astype(F32) + a2[...].astype(F32) + a3[...].astype(F32)
-    for t in range(PART // ONE):
-        for l in range(WIDE // 128):
-            n = t * (WIDE // 128) + l
-            n = 3 * (31 - n // 3) + n % 3
-            out[n * ONE:(n + 1) * ONE, :] = total[t * ONE:(t + 1) * ONE, l * 128:(l + 1) * 128].astype(BF16)
-    out[:6 * ONE, :] = jnp.zeros((6 * ONE, 128), BF16)
-
-    @pl.when((idx_ref[0] == 1) & (idx_ref[1] == 0))
-    def _():
-        hi, lo = hi_lo(total[:ONE, D - WIDE:] + total[ONE:2 * ONE, D - WIDE:])
-        out[:ONE, :] = hi
-        out[ONE:2 * ONE, :] = lo
-
-
-def last_kernel(idx_ref, clip_ref, p0, p1, p2, p3, q0, q1, q2, q3, w_ref, b_ref, loss_ref,
-                slots, wide_slots, out_sem):
+    group = 3 * ONE
+    for j in range(27):
+        out[(31 - j) * group:(32 - j) * group, :] = total[j * group:(j + 1) * group].astype(BF16)
+    hi, lo = hi_lo(total[REAL * ONE:(REAL + 1) * ONE] + total[(REAL + 1) * ONE:])
+    out[4 * group:4 * group + ONE, :] = hi
+    out[4 * group + ONE:4 * group + 2 * ONE, :] = lo
+    out[4 * group + 2 * ONE:5 * group, :] = jnp.zeros((ONE, 128), BF16)
+    out[:4 * group, :] = jnp.zeros((4 * group, 128), BF16)
+
+
+def last_kernel(idx_ref, clip_ref, p0, p1, p2, p3, q0, q1, q2, q3, w_ref, b_ref, loss_ref, slots, shared, out_sem):
     parts = (p0, p1, p2, p3, q0, q1, q2, q3)
 
     def whole(left, right, at_left, at_right):
-        total = jnp.zeros((ONE, 128), F32)
+        total = jnp.zeros((3 * ONE, 128), F32)
         extra = jnp.zeros((ONE, 128), F32)
         for s in range(4):
-            for n, lanes in ((left + s, 5), (right + s, 4)):
-
-                def add(t, acc, n=n, lanes=lanes):
-                    v = parts[n][pl.ds(pl.multiple_of(t * 80, ONE), lanes * ONE), :].astype(F32)
-                    v = v * v
-                    here = [v[l * ONE:(l + 1) * ONE] for l in range(lanes)]
-                    while len(here) > 1:
-                        here = [sum(here[i:i + 2][1:], here[i]) for i in range(0, len(here), 2)]
-                    return acc + here[0]
-                total = lax.fori_loop(0, PART // ONE, add, total, unroll=6)
-            here = (lax.rem(at_right + 4 - s, 4) == 0).astype(F32)
-            pair = parts[right + s][93 * ONE:95 * ONE, :].astype(F32)
+            for n in (left + s, right + s):
+                def add(t, acc, n=n):
+                    v = parts[n][pl.ds(pl.multiple_of(t * 3 * ONE, ONE), 3 * ONE), :].astype(F32)
+                    return acc + v * v
+                total = lax.fori_loop(0, REAL // 3, add, total, unroll=9)
+            here = (lax.rem(at_left + 4 - s, 4) == 0).astype(F32)
+            pair = parts[left + s][REAL * ONE:, :].astype(F32)
             extra = extra + here * (pair[:ONE] + pair[ONE:])
         bias = extra[:D // 128]
         square = jnp.sum(total, keepdims=True) + jnp.sum(bias * bias, keepdims=True)
         factor = jnp.minimum(F32(1.0), clip_ref[0] / jnp.sqrt(square))
         outs = []
         for s in range(4):
-            for n, lanes, base, at, slot in ((left + s, 5, 0, at_left, wide_slots), (right + s, 4, WIDE, at_right, slots)):
-                def put(t, carry, n=n, lanes=lanes, slot=slot, s=s):
-                    v = parts[n][pl.ds(pl.multiple_of(t * 80, ONE), lanes * ONE), :].astype(F32) * factor
+            for side, n, at in ((0, left + s, at_left), (1, right + s, at_right)):
+                def put(t, carry, n=n, side=side, s=s):
+                    v = parts[n][pl.ds(pl.multiple_of(t * LANES * ONE, ONE), LANES * ONE), :].astype(F32) * factor
                     rows = pl.ds(pl.multiple_of(t * ONE, ONE), ONE)
-                    for l in range(lanes):
-                        slot[s, rows, l * 128:(l + 1) * 128] = v[l * ONE:(l + 1) * ONE]
+                    for l in range(LANES):
+                        slots[side, s, rows, l * 128:(l + 1) * 128] = v[l * ONE:(l + 1) * ONE]
                     return carry
                 lax.fori_loop(0, PART // ONE, put, 0, unroll=6)
-                row0 = pl.multiple_of(lax.rem(at + 4 - s, 4) * PART, PART)
-                out = pltpu.make_async_copy(
-                    slot.at[s], w_ref.at[pl.ds(row0, PART), base:base + lanes * 128], out_sem.at[len(outs)]
-                )
-                out.start()
-                outs.append(out)
+                shared[side, s] = parts[n][72 * ONE:REAL * ONE, :].astype(F32) * factor
+                row0 = lax.rem(at + 4 - s, 4) * PART
+                whole_rows = pl.ds(pl.multiple_of(row0, PART), PART)
+                half_rows = pl.ds(pl.multiple_of(row0 + side * HALF, HALF), HALF)
+                for source, target in (
+                    (slots.at[side, s], w_ref.at[whole_rows, side * 512:(side + 1) * 512]),
+                    (shared.at[side, s], w_ref.at[half_rows, 1024:D]),
+                ):
+                    out = pltpu.make_async_copy(source, target, out_sem.at[len(outs)])
+                    out.start()
+                    outs.append(out)
         for r in range(D // 128):
             b_ref[r * 128:(r + 1) * 128] = (bias[r:r + 1] * factor).reshape(128)
         loss_ref[0] = jnp.sum(extra[D // 128:D // 128 + 1, :]) * F32(1.0 / TOTAL)
@@ -278,25 +268,26 @@
     idx = jnp.stack([core, at, at_other]).astype(jnp.int32)
     scal = jnp.stack([logit_scale[0], logit_shift[0], -loss_scale[0] / TOTAL])
 
-    txt = [texts, shifted(texts, "core", 1), shifted(texts, "yh", 1)]
-    txt.append(lax.ppermute(texts, ("yh", "core"), [(0, 3), (1, 2), (2, 1), (3, 0)]))
+    cross = lax.ppermute(texts, ("yh", "core"), [(0, 3), (1, 2), (2, 1), (3, 0)])
+    near, cross = lax.optimization_barrier((texts, cross))
+    txt = [texts, shifted(near, "core", 1), shifted(texts, "yh", 1), cross]
     img = [images] + [shifted(images, "x", s) for s in (2, 1, 3)]
 
     bias_row = head_bias[None]
     sides = [
         pl.pallas_call(
             text_kernel,
-            out_shape=(sds((OWN, D), F32), sds((OWN, 128), F32)),
-            in_specs=[VMEM] * 3, out_specs=(VMEM, VMEM), compiler_params=room(10),
+            out_shape=(sds((OWN, D), F32), sds((OWN, 128), F32), sds((D, OWN), BF16)),
+            in_specs=[VMEM] * 3, out_specs=(VMEM,) * 3, compiler_params=room(10),
             cost_estimate=pl.CostEstimate(flops=2 * OWN * D * D, bytes_accessed=3_600_000, transcendentals=OWN),
             name="text_side",
         )(block, head_weight, bias_row)
         for block in txt
     ]
-    ys, invs = [y for y, _ in sides], [v for _, v in sides]
+    ys, invs, flips = zip(*sides)
     gs, keep, give = pl.pallas_call(
         pair_kernel,
-        out_shape=(sds((4 * OWN, 4 * OWN), BF16),) + (sds((4 * OWN, WIDE), BF16),) * 2,
+        out_shape=(sds((4 * OWN, 4 * OWN), BF16),) + (sds((4 * OWN + 2 * ONE, WIDE), BF16),) * 2,
         in_specs=[SMEM, SMEM] + [VMEM] * 12, out_specs=(VMEM,) * 3, compiler_params=room(20),
         scratch_shapes=[
             pltpu.VMEM((4 * OWN, D), BF16), pltpu.VMEM((4 * OWN, D), BF16), pltpu.VMEM((ONE, 128), F32),
@@ -316,38 +307,39 @@
     got = shifted(give, "core", 1)
     parts = pl.pallas_call(
         head_kernel,
-        out_shape=(sds((PART, WIDE), BF16),) * 4,
+        out_shape=(sds((USED, 128), BF16),) * 4,
         in_specs=[SMEM] + [VMEM] * 6, out_specs=(VMEM,) * 4, compiler_params=room(14),
         scratch_shapes=[
-            pltpu.VMEM((4 * OWN, D), BF16), pltpu.VMEM((4 * OWN, WIDE), BF16), pltpu.VMEM((4, PART, WIDE), BF16),
+            pltpu.VMEM((D, 4 * OWN), BF16), pltpu.VMEM((4 * OWN, WIDE), BF16),
+            pltpu.VMEM((4, USED, 128), BF16), pltpu.VMEM((4, PART, 128), BF16),
         ],
         cost_estimate=pl.CostEstimate(flops=2 * 512 * D * WIDE, bytes_accessed=4_000_000, transcendentals=0),
         name="head",
-    )(idx, *txt, keep, got)
+    )(idx, *flips, keep, got)
     r2, r1, r3 = [lax.ppermute(parts[s], ALL, around(s)) for s in (2, 1, 3)]
     tiles = pl.pallas_call(
         tile_kernel,
-        out_shape=sds((TILES * ONE, 128), BF16),
-        in_specs=[SMEM] + [VMEM] * 4, out_specs=VMEM, compiler_params=room(8),
-        cost_estimate=pl.CostEstimate(flops=4 * PART * WIDE, bytes_accessed=1_900_000, transcendentals=0),
+        out_shape=sds((ALLOT, 128), BF16),
+        in_specs=[VMEM] * 4, out_specs=VMEM, compiler_params=room(8),
+        cost_estimate=pl.CostEstimate(flops=4 * USED * 128, bytes_accessed=1_900_000, transcendentals=0),
         name="tiles",
-    )(idx, parts[0], r1, r2, r3)
+    )(parts[0], r1, r2, r3)
     ig1, ig2, ig3, tiles = lax.optimization_barrier((ig1, ig2, ig3, tiles))
     back = [shifted(ig1, "x", -2), shifted(ig2, "x", -1), shifted(ig3, "x", -3)]
     sums = lax.all_to_all(tiles.reshape(32, 48, 128), ALL, 0, 0, axis_index_groups=groups_second(), tiled=True)
     sums, back[1], back[2] = lax.optimization_barrier((sums, back[1], back[2]))
     s2 = jnp.sum(sums.astype(F32), axis=0)
-    at2 = jnp.where(core == 0, lax.axis_index(("yh", "z", "yl")), lax.axis_index(("x", "z")))
+    at2 = jnp.where(core == 0, lax.axis_index(("z", "yh", "yl")), lax.axis_index(("z", "x")))
     f_hi, f_lo = hi_lo(s2[:ONE] + s2[ONE:2 * ONE])
     special = jnp.concatenate([f_hi, f_lo, jnp.zeros((ONE, 128), BF16)], 0)
-    mine = jnp.where(at2 == 0, special, s2.astype(BF16))
+    mine = jnp.where(at2 == 4, special, s2.astype(BF16))
     copies = jnp.broadcast_to(mine, (32, 48, 128))
     turned = [group[::-1] for group in groups_second()]
     a1 = lax.all_to_all(copies, ALL, 0, 0, axis_index_groups=turned, tiled=True)
     a1, back = lax.optimization_barrier((a1, back))
     image_grad = ig0 + back[0].astype(F32) + back[1].astype(F32) + back[2].astype(F32)
 
-    b0 = a1.reshape(TILES * ONE, 128)
+    b0 = a1.reshape(ALLOT, 128)[:USED]
     b2, b1, b3 = [lax.ppermute(b0, ALL, around(s)) for s in (2, 1, 3)]
     own_half = (b0, b1, b2, b3)
     other_half = [shifted(b, "core", 1) for b in own_half]
@@ -356,7 +348,7 @@
         out_shape=(sds((D, D), F32), sds((D,), F32), sds((1,), F32)),
         in_specs=[SMEM, SMEM] + [VMEM] * 8, out_specs=(ANY, VMEM, SMEM), compiler_params=room(14),
         scratch_shapes=[
-            pltpu.VMEM((4, PART, D - WIDE), F32), pltpu.VMEM((4, PART, WIDE), F32), pltpu.SemaphoreType.DMA((8,)),
+            pltpu.VMEM((2, 4, PART, 512), F32), pltpu.VMEM((2, 4, HALF, 128), F32), pltpu.SemaphoreType.DMA((16,)),
         ],
         cost_estimate=pl.CostEstimate(flops=4 * D * D, bytes_accessed=8_500_000, transcendentals=0),
         name="last",

time: 115 us -> 111 us (0.965)
  waiting for transfers between devices: 37.2 us -> 29.3 us
  starting transfers between devices: 49.6 us -> 53.8 us
    ppermute x13, starting transfers between devices: 16.2 us -> 22.4 us  [shifted(): lax.ppermute(block, axis, [(i, (i + distance) % size) for i in range(size)])]
    ppermute x13, waiting for transfers between devices: 24 us -> 19.4 us  [shifted(): lax.ppermute(block, axis, [(i, (i + distance) % size) for i in range(size)])]
    ppermute x3, waiting for transfers between devices: 6.85 us -> 2.37 us  [local(): b2, b1, b3 = [lax.ppermute(b0, ALL, around(s)) for s in (2, 1, 3)]]
    ppermute x1, waiting for transfers between devices: 0.01 us -> 2.16 us  [local(): lax.ppermute(texts, ('yh', 'core'), [(0, 3), (1, 2), (2, 1), (3, 0)])]
    unnamed x10 -> x8, local copies, waits for them, and re-layouts: 4.47 us -> 4.47 us
  transfers between devices with their start and end apart: 22 -> 22, of which waited for: 12 -> 9; matrix products, arithmetic and copies ran while one was open for 2% -> 2% of each run, Pallas kernels for 4% -> 4%
where the time goes in v4:
time: 111 us; the launch traced here: 110 us
  starting transfers between devices  53.8 us (48%)
  waiting for transfers between devices  29.3 us (26%)
  Pallas kernels  16.2 us (15%)
  local copies, waits for them, and re-layouts  6.07 us (5%)
  between operations  3.56 us (3%)
  other arithmetic  1.24 us (1%)
    ppermute x13, starting transfers between devices, shifted(): lax.ppermute(block, axis, [(i, (i + distance) % size) for i in range(size)])  22.4 us
    ppermute x13, waiting for transfers between devices, shifted(): lax.ppermute(block, axis, [(i, (i + distance) % size) for i in range(size)])  19.4 us
    all_to_all x1, starting transfers between devices, local(): lax.all_to_all(tiles.reshape(32, 48, 128), ALL, 0, 0, axis_index_groups=g...  9.51 us
    all_to_all x1, starting transfers between devices, local(): a1 = lax.all_to_all(copies, ALL, 0, 0, axis_index_groups=turned, tiled=True)  8.45 us
    ppermute x3, waiting for transfers between devices, local(): r2, r1, r3 = [lax.ppermute(parts[s], ALL, around(s)) for s in (2, 1, 3)]  5.33 us
    ppermute x3, starting transfers between devices, local(): r2, r1, r3 = [lax.ppermute(parts[s], ALL, around(s)) for s in (2, 1, 3)]  4.81 us
    pallas_call x1, Pallas kernels, local(): pl.pallas_call(last_kernel, out_shape=(sds((D, D), F32), sds((D,), F32),...  4.5 us
    unnamed x8, local copies, waits for them, and re-layouts  4.47 us
  transfers between devices with their start and end apart: 22, of which 9 were waited for; matrix products, arithmetic and copies ran while one was open for 2% of the time, Pallas kernels for 4%

profile of v4, /device:TPU:1, one launch (start us, length us, event | category | flops | bytes accessed | tf_op | source)
XLA Modules:
  0.0 110.2 jit_solution(18085803101727790382)
XLA Ops:
  0.6 4.4 %collective-permute-start.3 = (bf16[128,1152]{1,0:T(8,128)(2,1)}, bf16[128,1152]{1,0:T(8,128)(2,1)S(1)}, u32[]{:S(2)}, u32[]{:S(2)}) collective-permute-start(bf16[128,1152]{1,0:T(8,128)(2,1)} %t_ref.1), channel_id=1, source_target_pairs={{0,48},{16,32},{32,16},{48,0},{1,49},{17,33},{33,17},{49,1},{2,50}... | collective-permute-start | bytes 884744 | tf_op jit(solution)/shard_map/ppermute | solution.py:271
  5.0 1.8 %collective-permute-start.5 = (bf16[128,1152]{1,0:T(8,128)(2,1)}, bf16[128,1152]{1,0:T(8,128)(2,1)S(1)}, u32[]{:S(2)}, u32[]{:S(2)}) collective-permute-start(bf16[128,1152]{1,0:T(8,128)(2,1)} %t_ref.1), channel_id=1, source_target_pairs={{0,32},{32,0},{1,33},{33,1},{2,34},{34,2},{3,35},{35,3},{4,36},{36... | collective-permute-start | bytes 884744 | tf_op jit(solution)/shard_map/ppermute | solution.py:68
  10.0 2.2 %collective-permute-done.3.t_ref = bf16[128,1152]{1,0:T(8,128)(2,1)S(1)} collective-permute-done((bf16[128,1152]{1,0:T(8,128)(2,1)}, bf16[128,1152]{1,0:T(8,128)(2,1)S(1)}, u32[]{:S(2)}, u32[]{:S(2)}) %collective-permute-start.3) | collective-permute-done | bytes 294944 | tf_op jit(solution)/shard_map/ppermute | solution.py:271
  12.1 2.9 %collective-permute-start.4 = (bf16[128,1152]{1,0:T(8,128)(2,1)}, bf16[128,1152]{1,0:T(8,128)(2,1)S(1)}, u32[]{:S(2)}, u32[]{:S(2)}) collective-permute-start(bf16[128,1152]{1,0:T(8,128)(2,1)} %t_ref.1), channel_id=1, source_target_pairs={{0,16},{16,0},{1,17},{17,1},{2,18},{18,2},{3,19},{19,3},{4,20},{20... | collective-permute-start | bytes 884744 | tf_op jit(solution)/shard_map/ppermute | solution.py:68
  15.0 1.7 %copy-done = bf16[1152,1152]{1,0:T(8,128)(2,1)S(1)} copy-done((bf16[1152,1152]{1,0:T(8,128)(2,1)S(1)}, bf16[1152,1152]{1,0:T(8,128)(2,1)}, u32[]{:S(2)}) %copy-start) | copy-done | bytes 2654232
  20.6 1.8 %copy-done.1 = bf16[1152,1152]{1,0:T(8,128)(2,1)S(1)} copy-done((bf16[1152,1152]{1,0:T(8,128)(2,1)S(1)}, bf16[1152,1152]{1,0:T(8,128)(2,1)}, u32[]{:S(2)}) %copy-start.1) | copy-done | bytes 2654232
  24.6 4.2 %pairs.1 = (bf16[512,512]{1,0:T(8,128)(2,1)S(1)}, bf16[544,640]{1,0:T(8,128)(2,1)S(1)}, bf16[544,640]{1,0:T(8,128)(2,1)S(1)}) custom-call(s32[3]{0:T(128)S(1)} %pad_add_fusion.core_ref.idx_ref, f32[3]{0:T(128)S(1)} %pad_maximum_fusion.scal_ref, bf16[128,1152]{1,0:T(8,128)(2,1)S(1)} %copy-done.3, bf16[128,1152]{1,0:T(8,128)(2,1)S(1)} %collective-permute-done.i1, ...), custom_call_target="tpu_custom_call" | custom-call | flops 1207959552 | bytes 5500000 | tf_op jit(solution)/shard_map/pairs/pallas_call | solution.py:288
  29.0 2.1 %collective-permute-done.6.got_ref = bf16[544,640]{1,0:T(8,128)(2,1)S(1)} collective-permute-done((bf16[544,640]{1,0:T(8,128)(2,1)S(1)}, bf16[544,640]{1,0:T(8,128)(2,1)S(1)}, u32[]{:S(2)}, u32[]{:S(2)}) %collective-permute-start.6) | collective-permute-done | bytes 696352 | tf_op jit(solution)/shard_map/ppermute | solution.py:68
  31.1 1.9 %head.1 = (bf16[1328,128]{1,0:T(8,128)(2,1)S(1)}, bf16[1328,128]{1,0:T(8,128)(2,1)S(1)}, bf16[1328,128]{1,0:T(8,128)(2,1)S(1)}, bf16[1328,128]{1,0:T(8,128)(2,1)S(1)}) custom-call(s32[3]{0:T(128)S(1)} %pad_add_fusion.core_ref.idx_ref, bf16[1152,128]{1,0:T(8,128)(2,1)S(1)} %get-tuple-element.58.f0, bf16[1152,128]{1,0:T(8,128)(2,1)S(1)} %get-tuple-element.59.f1, ...), custom_call_target="tpu_custom_call" | custom-call | flops 754974720 | bytes 4000000 | tf_op jit(solution)/shard_map/head/pallas_call | solution.py:308
  34.0 2.7 %collective-permute-start.8 = (bf16[1328,128]{1,0:T(8,128)(2,1)S(1)}, bf16[1328,128]{1,0:T(8,128)(2,1)S(1)}, u32[]{:S(2)}, u32[]{:S(2)}) collective-permute-start(bf16[1328,128]{1,0:T(8,128)(2,1)S(1)} %get-tuple-element.66), channel_id=1, source_target_pairs={{0,128},{1,129},{2,130},{3,131},{4,132},{5,133},{6,134},{7,135},{8... | collective-permute-start | bytes 1019912 | tf_op jit(solution)/shard_map/ppermute | solution.py:319
  37.8 1.9 %image_side.1 = (f32[128,1152]{1,0:T(8,128)S(1)}, bf16[128,1152]{1,0:T(8,128)(2,1)S(1)}, bf16[128,1152]{1,0:T(8,128)(2,1)S(1)}, bf16[128,1152]{1,0:T(8,128)(2,1)S(1)}) custom-call(f32[3]{0:T(128)S(1)} %pad_maximum_fusion.scal_ref, bf16[128,1152]{1,0:T(8,128)(2,1)S(1)} %copy-done.3, bf16[128,1152]{1,0:T(8,128)(2,1)S(1)} %collective-permute-done.i1, ...), custom_call_target="tpu_custom_call" | custom-call | flops 603979776 | bytes 5500000 | tf_op jit(solution)/shard_map/image_side/pallas_call | solution.py:298
  40.6 4.3 %collective-permute-done.8.a2 = bf16[1328,128]{1,0:T(8,128)(2,1)S(1)} collective-permute-done((bf16[1328,128]{1,0:T(8,128)(2,1)S(1)}, bf16[1328,128]{1,0:T(8,128)(2,1)S(1)}, u32[]{:S(2)}, u32[]{:S(2)}) %collective-permute-start.8) | collective-permute-done | bytes 340000 | tf_op jit(solution)/shard_map/ppermute | solution.py:319
  45.9 9.5 %all-to-all-start = ((bf16[32,48,128]{2,1,0:T(8,128)(2,1)}), bf16[32,48,128]{2,1,0:T(8,128)(2,1)S(1)}, u32[]{:S(2)}, u32[]{:S(2)}) async-start(bf16[32,48,128]{2,1,0:T(8,128)(2,1)} %bitcast.3), calls=%async_computation | async-start | bytes 786432 | tf_op jit(solution)/shard_map/all_to_all | solution.py:329
  55.4 2.5 %collective-permute-start.10 = (bf16[128,1152]{1,0:T(8,128)(2,1)S(1)}, bf16[128,1152]{1,0:T(8,128)(2,1)S(1)}, u32[]{:S(2)}, u32[]{:S(2)}) collective-permute-start(bf16[128,1152]{1,0:T(8,128)(2,1)S(1)} %get-tuple-element.69), channel_id=1, source_target_pairs={{0,192},{64,0},{128,64},{192,128},{1,193},{65,1},{129,65},{193,129... | collective-permute-start | bytes 884744 | tf_op jit(solution)/shard_map/ppermute | solution.py:68
  58.0 6.2 %collective-permute-done.10 = bf16[128,1152]{1,0:T(8,128)(2,1)S(1)} collective-permute-done((bf16[128,1152]{1,0:T(8,128)(2,1)S(1)}, bf16[128,1152]{1,0:T(8,128)(2,1)S(1)}, u32[]{:S(2)}, u32[]{:S(2)}) %collective-permute-start.10) | collective-permute-done | bytes 294944 | tf_op jit(solution)/shard_map/ppermute | solution.py:68
  64.2 3.1 %collective-permute-done.11 = bf16[128,1152]{1,0:T(8,128)(2,1)S(1)} collective-permute-done((bf16[128,1152]{1,0:T(8,128)(2,1)S(1)}, bf16[128,1152]{1,0:T(8,128)(2,1)S(1)}, u32[]{:S(2)}, u32[]{:S(2)}) %collective-permute-start.11) | collective-permute-done | bytes 294944 | tf_op jit(solution)/shard_map/ppermute | solution.py:68
  68.3 8.5 %all-to-all-start.1 = ((bf16[32,48,128]{2,1,0:T(8,128)(2,1)}), bf16[32,48,128]{2,1,0:T(8,128)(2,1)S(1)}, u32[]{:S(2)}, u32[]{:S(2)}) async-start(bf16[32,48,128]{2,1,0:T(8,128)(2,1)} %broadcast_in_dim.11), calls=%async_computation.1 | async-start | bytes 786432 | tf_op jit(solution)/shard_map/all_to_all | solution.py:338
  78.0 7.7 %collective-permute-done.12 = bf16[128,1152]{1,0:T(8,128)(2,1)S(1)} collective-permute-done((bf16[128,1152]{1,0:T(8,128)(2,1)S(1)}, bf16[128,1152]{1,0:T(8,128)(2,1)S(1)}, u32[]{:S(2)}, u32[]{:S(2)}) %collective-permute-start.12) | collective-permute-done | bytes 294944 | tf_op jit(solution)/shard_map/ppermute | solution.py:68
  85.7 3.5 %collective-permute-start.15 = (bf16[1328,128]{1,0:T(8,128)(2,1)S(1)}, bf16[1328,128]{1,0:T(8,128)(2,1)S(1)}, u32[]{:S(2)}, u32[]{:S(2)}) collective-permute-start(bf16[1328,128]{1,0:T(8,128)(2,1)S(1)} %slice.14.p0), channel_id=1, source_target_pairs={{0,192},{1,193},{2,194},{3,195},{4,196},{5,197},{6,198},{7,199},{8... | collective-permute-start | bytes 1019912 | tf_op jit(solution)/shard_map/ppermute | solution.py:343
  90.5 4.1 %collective-permute-start.16 = (bf16[1328,128]{1,0:T(8,128)(2,1)S(1)}, bf16[1328,128]{1,0:T(8,128)(2,1)S(1)}, u32[]{:S(2)}, u32[]{:S(2)}) collective-permute-start(bf16[1328,128]{1,0:T(8,128)(2,1)S(1)} %slice.14.p0), channel_id=1, source_target_pairs={{0,16},{16,0},{1,17},{17,1},{2,18},{18,2},{3,19},{19,3},{4,20},{20... | collective-permute-start | bytes 1019912 | tf_op jit(solution)/shard_map/ppermute | solution.py:68
  94.6 2.4 %collective-permute-done.15.p3 = bf16[1328,128]{1,0:T(8,128)(2,1)S(1)} collective-permute-done((bf16[1328,128]{1,0:T(8,128)(2,1)S(1)}, bf16[1328,128]{1,0:T(8,128)(2,1)S(1)}, u32[]{:S(2)}, u32[]{:S(2)}) %collective-permute-start.15) | collective-permute-done | bytes 340000 | tf_op jit(solution)/shard_map/ppermute | solution.py:343
  97.6 3.1 %collective-permute-start.18 = (bf16[1328,128]{1,0:T(8,128)(2,1)S(1)}, bf16[1328,128]{1,0:T(8,128)(2,1)S(1)}, u32[]{:S(2)}, u32[]{:S(2)}) collective-permute-start(bf16[1328,128]{1,0:T(8,128)(2,1)S(1)} %collective-permute-done.14.p2), channel_id=1, source_target_pairs={{0,16},{16,0},{1,17},{17,1},{2,18},{18,2},{3,19},{19,3},{4,20},{20... | collective-permute-start | bytes 1019912 | tf_op jit(solution)/shard_map/ppermute | solution.py:68
  100.7 3.5 %collective-permute-start.17 = (bf16[1328,128]{1,0:T(8,128)(2,1)S(1)}, bf16[1328,128]{1,0:T(8,128)(2,1)S(1)}, u32[]{:S(2)}, u32[]{:S(2)}) collective-permute-start(bf16[1328,128]{1,0:T(8,128)(2,1)S(1)} %collective-permute-done.13.p1), channel_id=1, source_target_pairs={{0,16},{16,0},{1,17},{17,1},{2,18},{18,2},{3,19},{19,3},{4,20},{20... | collective-permute-start | bytes 1019912 | tf_op jit(solution)/shard_map/ppermute | solution.py:68
  105.5 4.5 %last.1 = (f32[1152,1152]{1,0:T(8,128)}, f32[1152]{0:T(1024)}, f32[1]{0:T(128)}) custom-call(s32[3]{0:T(128)S(1)} %pad_add_fusion.core_ref.idx_ref, f32[1]{0:T(128)S(6)} %copy.15.clip_ref, bf16[1328,128]{1,0:T(8,128)(2,1)S(1)} %slice.14.p0, bf16[1328,128]{1,0:T(8,128)(2,1)S(1)} %collective-permute-done.13.p1, ...), custom_call_target="tpu_custom_call" | custom-call | flops 5308416 | bytes 8500000 | tf_op jit(solution)/shard_map/last/pallas_call | solution.py:346
  (48 shorter events, 16.3 us)
Async XLA Ops:
  0.6 11.5 %collective-permute-start.3 = (bf16[128,1152]{1,0:T(8,128)(2,1)}, bf16[128,1152]{1,0:T(8,128)(2,1)S(1)}, u32[]{:S(2)}, u32[]{:S(2)}) collective-permute-start(bf16[128,1152]{1,0:T(8,128)(2,1)} %t_ref.1), channel_id=1, source_target_pairs={{0,48},{16,32},{32,16},{48,0},{1,49},{17,33},{33,17},{49,1},{2,50}... | collective-permute-start | bytes 884744 | tf_op jit(solution)/shard_map/ppermute | solution.py:271
  5.0 18.1 %collective-permute-start.5 = (bf16[128,1152]{1,0:T(8,128)(2,1)}, bf16[128,1152]{1,0:T(8,128)(2,1)S(1)}, u32[]{:S(2)}, u32[]{:S(2)}) collective-permute-start(bf16[128,1152]{1,0:T(8,128)(2,1)} %t_ref.1), channel_id=1, source_target_pairs={{0,32},{32,0},{1,33},{33,1},{2,34},{34,2},{3,35},{35,3},{4,36},{36... | collective-permute-start | bytes 884744 | tf_op jit(solution)/shard_map/ppermute | solution.py:68
  6.8 17.8 %collective-permute-start.2 = (bf16[128,1152]{1,0:T(8,128)(2,1)}, bf16[128,1152]{1,0:T(8,128)(2,1)S(1)}, u32[]{:S(2)}, u32[]{:S(2)}) collective-permute-start(bf16[128,1152]{1,0:T(8,128)(2,1)} %i0.3), channel_id=1, source_target_pairs={{0,192},{64,0},{128,64},{192,128},{1,193},{65,1},{129,65},{193,129... | collective-permute-start | bytes 884744 | tf_op jit(solution)/shard_map/ppermute | solution.py:68
  7.6 17.0 %collective-permute-start.1 = (bf16[128,1152]{1,0:T(8,128)(2,1)}, bf16[128,1152]{1,0:T(8,128)(2,1)S(1)}, u32[]{:S(2)}, u32[]{:S(2)}) collective-permute-start(bf16[128,1152]{1,0:T(8,128)(2,1)} %i0.3), channel_id=1, source_target_pairs={{0,64},{64,128},{128,192},{192,0},{1,65},{65,129},{129,193},{193,1... | collective-permute-start | bytes 884744 | tf_op jit(solution)/shard_map/ppermute | solution.py:68
  8.3 16.3 %collective-permute-start = (bf16[128,1152]{1,0:T(8,128)(2,1)}, bf16[128,1152]{1,0:T(8,128)(2,1)S(1)}, u32[]{:S(2)}, u32[]{:S(2)}) collective-permute-start(bf16[128,1152]{1,0:T(8,128)(2,1)} %i0.3), channel_id=1, source_target_pairs={{0,128},{64,192},{128,0},{192,64},{1,129},{65,193},{129,1},{193,65... | collective-permute-start | bytes 884744 | tf_op jit(solution)/shard_map/ppermute | solution.py:68
  12.1 11.7 %collective-permute-start.4 = (bf16[128,1152]{1,0:T(8,128)(2,1)}, bf16[128,1152]{1,0:T(8,128)(2,1)S(1)}, u32[]{:S(2)}, u32[]{:S(2)}) collective-permute-start(bf16[128,1152]{1,0:T(8,128)(2,1)} %t_ref.1), channel_id=1, source_target_pairs={{0,16},{16,0},{1,17},{17,1},{2,18},{18,2},{3,19},{19,3},{4,20},{20... | collective-permute-start | bytes 884744 | tf_op jit(solution)/shard_map/ppermute | solution.py:68
  17.8 6.9 %copy-start.3 = (bf16[128,1152]{1,0:T(8,128)(2,1)S(1)}, bf16[128,1152]{1,0:T(8,128)(2,1)}, u32[]{:S(2)}) copy-start(bf16[128,1152]{1,0:T(8,128)(2,1)} %i0.3) | copy-start | bytes 884740
  20.6 1.8 %copy-start.1 = (bf16[1152,1152]{1,0:T(8,128)(2,1)S(1)}, bf16[1152,1152]{1,0:T(8,128)(2,1)}, u32[]{:S(2)}) copy-start(bf16[1152,1152]{1,0:T(8,128)(2,1)} %w_ref.7) | copy-start | bytes 7962628
  28.8 2.2 %collective-permute-start.6 = (bf16[544,640]{1,0:T(8,128)(2,1)S(1)}, bf16[544,640]{1,0:T(8,128)(2,1)S(1)}, u32[]{:S(2)}, u32[]{:S(2)}) collective-permute-start(bf16[544,640]{1,0:T(8,128)(2,1)S(1)} %get-tuple-element.63), channel_id=1, source_target_pairs={{0,16},{16,0},{1,17},{17,1},{2,18},{18,2},{3,19},{19,3},{4,20},{20... | collective-permute-start | bytes 2088968 | tf_op jit(solution)/shard_map/ppermute | solution.py:68
  32.9 7.6 %collective-permute-start.7 = (bf16[1328,128]{1,0:T(8,128)(2,1)S(1)}, bf16[1328,128]{1,0:T(8,128)(2,1)S(1)}, u32[]{:S(2)}, u32[]{:S(2)}) collective-permute-start(bf16[1328,128]{1,0:T(8,128)(2,1)S(1)} %get-tuple-element.65), channel_id=1, source_target_pairs={{0,64},{1,65},{2,66},{3,67},{4,68},{5,69},{6,70},{7,71},{8,72},{9,... | collective-permute-start | bytes 1019912 | tf_op jit(solution)/shard_map/ppermute | solution.py:319
  34.0 10.9 %collective-permute-start.8 = (bf16[1328,128]{1,0:T(8,128)(2,1)S(1)}, bf16[1328,128]{1,0:T(8,128)(2,1)S(1)}, u32[]{:S(2)}, u32[]{:S(2)}) collective-permute-start(bf16[1328,128]{1,0:T(8,128)(2,1)S(1)} %get-tuple-element.66), channel_id=1, source_target_pairs={{0,128},{1,129},{2,130},{3,131},{4,132},{5,133},{6,134},{7,135},{8... | collective-permute-start | bytes 1019912 | tf_op jit(solution)/shard_map/ppermute | solution.py:319
  36.7 8.2 %collective-permute-start.9 = (bf16[1328,128]{1,0:T(8,128)(2,1)S(1)}, bf16[1328,128]{1,0:T(8,128)(2,1)S(1)}, u32[]{:S(2)}, u32[]{:S(2)}) collective-permute-start(bf16[1328,128]{1,0:T(8,128)(2,1)S(1)} %get-tuple-element.67), channel_id=1, source_target_pairs={{0,192},{1,193},{2,194},{3,195},{4,196},{5,197},{6,198},{7,199},{8... | collective-permute-start | bytes 1019912 | tf_op jit(solution)/shard_map/ppermute | solution.py:319
  45.9 21.5 %all-to-all-start = ((bf16[32,48,128]{2,1,0:T(8,128)(2,1)}), bf16[32,48,128]{2,1,0:T(8,128)(2,1)S(1)}, u32[]{:S(2)}, u32[]{:S(2)}) async-start(bf16[32,48,128]{2,1,0:T(8,128)(2,1)} %bitcast.3), calls=%async_computation | async-start | bytes 786432 | tf_op jit(solution)/shard_map/all_to_all | solution.py:329
  55.4 8.8 %collective-permute-start.10 = (bf16[128,1152]{1,0:T(8,128)(2,1)S(1)}, bf16[128,1152]{1,0:T(8,128)(2,1)S(1)}, u32[]{:S(2)}, u32[]{:S(2)}) collective-permute-start(bf16[128,1152]{1,0:T(8,128)(2,1)S(1)} %get-tuple-element.69), channel_id=1, source_target_pairs={{0,192},{64,0},{128,64},{192,128},{1,193},{65,1},{129,65},{193,129... | collective-permute-start | bytes 884744 | tf_op jit(solution)/shard_map/ppermute | solution.py:68
  57.9 9.4 %collective-permute-start.11 = (bf16[128,1152]{1,0:T(8,128)(2,1)S(1)}, bf16[128,1152]{1,0:T(8,128)(2,1)S(1)}, u32[]{:S(2)}, u32[]{:S(2)}) collective-permute-start(bf16[128,1152]{1,0:T(8,128)(2,1)S(1)} %get-tuple-element.70), channel_id=1, source_target_pairs={{0,64},{64,128},{128,192},{192,0},{1,65},{65,129},{129,193},{193,1... | collective-permute-start | bytes 884744 | tf_op jit(solution)/shard_map/ppermute | solution.py:68
  68.3 17.4 %all-to-all-start.1 = ((bf16[32,48,128]{2,1,0:T(8,128)(2,1)}), bf16[32,48,128]{2,1,0:T(8,128)(2,1)S(1)}, u32[]{:S(2)}, u32[]{:S(2)}) async-start(bf16[32,48,128]{2,1,0:T(8,128)(2,1)} %broadcast_in_dim.11), calls=%async_computation.1 | async-start | bytes 786432 | tf_op jit(solution)/shard_map/all_to_all | solution.py:338
  76.8 8.9 %collective-permute-start.12 = (bf16[128,1152]{1,0:T(8,128)(2,1)S(1)}, bf16[128,1152]{1,0:T(8,128)(2,1)S(1)}, u32[]{:S(2)}, u32[]{:S(2)}) collective-permute-start(bf16[128,1152]{1,0:T(8,128)(2,1)S(1)} %get-tuple-element.72), channel_id=1, source_target_pairs={{0,128},{64,192},{128,0},{192,64},{1,129},{65,193},{129,1},{193,65... | collective-permute-start | bytes 884744 | tf_op jit(solution)/shard_map/ppermute | solution.py:68
  85.7 11.3 %collective-permute-start.15 = (bf16[1328,128]{1,0:T(8,128)(2,1)S(1)}, bf16[1328,128]{1,0:T(8,128)(2,1)S(1)}, u32[]{:S(2)}, u32[]{:S(2)}) collective-permute-start(bf16[1328,128]{1,0:T(8,128)(2,1)S(1)} %slice.14.p0), channel_id=1, source_target_pairs={{0,192},{1,193},{2,194},{3,195},{4,196},{5,197},{6,198},{7,199},{8... | collective-permute-start | bytes 1019912 | tf_op jit(solution)/shard_map/ppermute | solution.py:343
  89.2 8.4 %collective-permute-start.14 = (bf16[1328,128]{1,0:T(8,128)(2,1)S(1)}, bf16[1328,128]{1,0:T(8,128)(2,1)S(1)}, u32[]{:S(2)}, u32[]{:S(2)}) collective-permute-start(bf16[1328,128]{1,0:T(8,128)(2,1)S(1)} %slice.14.p0), channel_id=1, source_target_pairs={{0,128},{1,129},{2,130},{3,131},{4,132},{5,133},{6,134},{7,135},{8... | collective-permute-start | bytes 1019912 | tf_op jit(solution)/shard_map/ppermute | solution.py:343
  89.2 11.5 %collective-permute-start.13 = (bf16[1328,128]{1,0:T(8,128)(2,1)S(1)}, bf16[1328,128]{1,0:T(8,128)(2,1)S(1)}, u32[]{:S(2)}, u32[]{:S(2)}) collective-permute-start(bf16[1328,128]{1,0:T(8,128)(2,1)S(1)} %slice.14.p0), channel_id=1, source_target_pairs={{0,64},{1,65},{2,66},{3,67},{4,68},{5,69},{6,70},{7,71},{8,72},{9,... | collective-permute-start | bytes 1019912 | tf_op jit(solution)/shard_map/ppermute | solution.py:343
  90.5 14.7 %collective-permute-start.16 = (bf16[1328,128]{1,0:T(8,128)(2,1)S(1)}, bf16[1328,128]{1,0:T(8,128)(2,1)S(1)}, u32[]{:S(2)}, u32[]{:S(2)}) collective-permute-start(bf16[1328,128]{1,0:T(8,128)(2,1)S(1)} %slice.14.p0), channel_id=1, source_target_pairs={{0,16},{16,0},{1,17},{17,1},{2,18},{18,2},{3,19},{19,3},{4,20},{20... | collective-permute-start | bytes 1019912 | tf_op jit(solution)/shard_map/ppermute | solution.py:68
  97.0 8.2 %collective-permute-start.19 = (bf16[1328,128]{1,0:T(8,128)(2,1)S(1)}, bf16[1328,128]{1,0:T(8,128)(2,1)S(1)}, u32[]{:S(2)}, u32[]{:S(2)}) collective-permute-start(bf16[1328,128]{1,0:T(8,128)(2,1)S(1)} %collective-permute-done.15.p3), channel_id=1, source_target_pairs={{0,16},{16,0},{1,17},{17,1},{2,18},{18,2},{3,19},{19,3},{4,20},{20... | collective-permute-start | bytes 1019912 | tf_op jit(solution)/shard_map/ppermute | solution.py:68
  97.6 7.6 %collective-permute-start.18 = (bf16[1328,128]{1,0:T(8,128)(2,1)S(1)}, bf16[1328,128]{1,0:T(8,128)(2,1)S(1)}, u32[]{:S(2)}, u32[]{:S(2)}) collective-permute-start(bf16[1328,128]{1,0:T(8,128)(2,1)S(1)} %collective-permute-done.14.p2), channel_id=1, source_target_pairs={{0,16},{16,0},{1,17},{17,1},{2,18},{18,2},{3,19},{19,3},{4,20},{20... | collective-permute-start | bytes 1019912 | tf_op jit(solution)/shard_map/ppermute | solution.py:68
  100.7 4.8 %collective-permute-start.17 = (bf16[1328,128]{1,0:T(8,128)(2,1)S(1)}, bf16[1328,128]{1,0:T(8,128)(2,1)S(1)}, u32[]{:S(2)}, u32[]{:S(2)}) collective-permute-start(bf16[1328,128]{1,0:T(8,128)(2,1)S(1)} %collective-permute-done.13.p1), channel_id=1, source_target_pairs={{0,16},{16,0},{1,17},{17,1},{2,18},{18,2},{3,19},{19,3},{4,20},{20... | collective-permute-start | bytes 1019912 | tf_op jit(solution)/shard_map/ppermute | solution.py:68
  (2 other events, 2.7 us)

commit v5 on v4

--- a/solution.py
+++ b/solution.py
@@ -61,6 +61,12 @@
             to = place(x, y // 2, core, z, y % 2)
         route.append((place(x, yh, core, z, yl), to))
     return route
+
+
+def spot():
+    core = lax.axis_index("core")
+    x, y = lax.axis_index("x"), 2 * lax.axis_index("yh") + lax.axis_index("yl")
+    return core, jnp.where(core == 0, x, y), jnp.where(core == 0, y, x)
 
 
 def shifted(block, axis, distance):
@@ -168,7 +174,8 @@
             target[...] = out.astype(target.dtype)
 
 
-def head_kernel(idx_ref, f0, f1, f2, f3, keep_ref, got_ref, o0, o1, o2, o3, flips, both, rw, shared):
+def head_kernel(f0, f1, f2, f3, keep_ref, got_ref, o0, o1, o2, o3, flips, both, rw, shared):
+    core, at, _ = spot()
     for k, ref in enumerate((f0, f1, f2, f3)):
         rows, swap = slice(k * OWN, (k + 1) * OWN), slice((k ^ 1) * OWN, ((k ^ 1) + 1) * OWN)
         flips[:, rows] = ref[...]
@@ -182,12 +189,12 @@
                 n = t * LANES + l
                 rw[q, n * ONE:(n + 1) * ONE, :] = part[t * ONE:(t + 1) * ONE, l * 128:(l + 1) * 128]
         shared[q] = part[:, 512:]
-        rw[q, 72 * ONE:REAL * ONE, :] = shared[q, pl.ds(pl.multiple_of(idx_ref[0] * HALF, HALF), HALF), :]
+        rw[q, 72 * ONE:REAL * ONE, :] = shared[q, pl.ds(pl.multiple_of(core * HALF, HALF), HALF), :]
         rw[q, REAL * ONE:, :] = jnp.zeros((2 * ONE, 128), BF16)
     rw[0, REAL * ONE:(REAL + 1) * ONE, :] = hi
     rw[0, (REAL + 1) * ONE:, :] = lo
     for s, ref in enumerate((o0, o1, o2, o3)):
-        ref[...] = rw[lax.rem(idx_ref[1] + s, 4)]
+        ref[...] = rw[lax.rem(at + s, 4)]
 
 
 def tile_kernel(a0, a1, a2, a3, out):
@@ -202,8 +209,26 @@
     out[:4 * group, :] = jnp.zeros((4 * group, 128), BF16)
 
 
-def last_kernel(idx_ref, clip_ref, p0, p1, p2, p3, q0, q1, q2, q3, w_ref, b_ref, loss_ref, slots, shared, out_sem):
+def copy_kernel(sums_ref, out):
+    total = jnp.sum(sums_ref[...].astype(F32), axis=0)
+    core, _, _ = spot()
+    z = lax.axis_index("z")
+    place_in = jnp.where(core == 0, 4 * z + 2 * lax.axis_index("yh") + lax.axis_index("yl"), 4 * z + lax.axis_index("x"))
+    hi, lo = hi_lo(total[:ONE] + total[ONE:2 * ONE])
+    plain = total.astype(BF16)
+    for k in range(32):
+        out[k] = plain
+
+    @pl.when(place_in == 4)
+    def _():
+        for k in range(32):
+            out[k, :ONE, :] = hi
+            out[k, ONE:2 * ONE, :] = lo
+
+
+def last_kernel(clip_ref, p0, p1, p2, p3, q0, q1, q2, q3, w_ref, b_ref, loss_ref, slots, shared, out_sem):
     parts = (p0, p1, p2, p3, q0, q1, q2, q3)
+    core, at_here, at_there = spot()
 
     def whole(left, right, at_left, at_right):
         total = jnp.zeros((3 * ONE, 128), F32)
@@ -247,13 +272,13 @@
         for out in outs:
             out.wait()
 
-    @pl.when(idx_ref[0] == 0)
+    @pl.when(core == 0)
     def _():
-        whole(0, 4, idx_ref[1], idx_ref[2])
-
-    @pl.when(idx_ref[0] == 1)
+        whole(0, 4, at_here, at_there)
+
+    @pl.when(core == 1)
     def _():
-        whole(4, 0, idx_ref[2], idx_ref[1])
+        whole(4, 0, at_there, at_here)
 
 
 def sds(shape, kind):
@@ -261,10 +286,7 @@
 
 
 def local(images, texts, head_weight, head_bias, logit_scale, logit_shift, loss_scale, clip_norm):
-    core = lax.axis_index("core")
-    at_x, at_y = lax.axis_index("x"), lax.axis_index(("yh", "yl"))
-    at = jnp.where(core == 0, at_x, at_y)
-    at_other = jnp.where(core == 0, at_y, at_x)
+    core, at, at_other = spot()
     idx = jnp.stack([core, at, at_other]).astype(jnp.int32)
     scal = jnp.stack([logit_scale[0], logit_shift[0], -loss_scale[0] / TOTAL])
 
@@ -308,14 +330,14 @@
     parts = pl.pallas_call(
         head_kernel,
         out_shape=(sds((USED, 128), BF16),) * 4,
-        in_specs=[SMEM] + [VMEM] * 6, out_specs=(VMEM,) * 4, compiler_params=room(14),
+        in_specs=[VMEM] * 6, out_specs=(VMEM,) * 4, compiler_params=room(14),
         scratch_shapes=[
             pltpu.VMEM((D, 4 * OWN), BF16), pltpu.VMEM((4 * OWN, WIDE), BF16),
             pltpu.VMEM((4, USED, 128), BF16), pltpu.VMEM((4, PART, 128), BF16),
         ],
         cost_estimate=pl.CostEstimate(flops=2 * 512 * D * WIDE, bytes_accessed=4_000_000, transcendentals=0),
         name="head",
-    )(idx, *flips, keep, got)
+    )(*flips, keep, got)
     r2, r1, r3 = [lax.ppermute(parts[s], ALL, around(s)) for s in (2, 1, 3)]
     tiles = pl.pallas_call(
         tile_kernel,
@@ -328,12 +350,13 @@
     back = [shifted(ig1, "x", -2), shifted(ig2, "x", -1), shifted(ig3, "x", -3)]
     sums = lax.all_to_all(tiles.reshape(32, 48, 128), ALL, 0, 0, axis_index_groups=groups_second(), tiled=True)
     sums, back[1], back[2] = lax.optimization_barrier((sums, back[1], back[2]))
-    s2 = jnp.sum(sums.astype(F32), axis=0)
-    at2 = jnp.where(core == 0, lax.axis_index(("z", "yh", "yl")), lax.axis_index(("z", "x")))
-    f_hi, f_lo = hi_lo(s2[:ONE] + s2[ONE:2 * ONE])
-    special = jnp.concatenate([f_hi, f_lo, jnp.zeros((ONE, 128), BF16)], 0)
-    mine = jnp.where(at2 == 4, special, s2.astype(BF16))
-    copies = jnp.broadcast_to(mine, (32, 48, 128))
+    copies = pl.pallas_call(
+        copy_kernel,
+        out_shape=sds((32, 48, 128), BF16),
+        in_specs=[VMEM], out_specs=VMEM, compiler_params=room(4),
+        cost_estimate=pl.CostEstimate(flops=32 * 48 * 128, bytes_accessed=800_000, transcendentals=0),
+        name="copies",
+    )(sums)
     turned = [group[::-1] for group in groups_second()]
     a1 = lax.all_to_all(copies, ALL, 0, 0, axis_index_groups=turned, tiled=True)
     a1, back = lax.optimization_barrier((a1, back))
@@ -346,13 +369,13 @@
     weight_grad, bias_grad, loss = pl.pallas_call(
         last_kernel,
         out_shape=(sds((D, D), F32), sds((D,), F32), sds((1,), F32)),
-        in_specs=[SMEM, SMEM] + [VMEM] * 8, out_specs=(ANY, VMEM, SMEM), compiler_params=room(14),
+        in_specs=[SMEM] + [VMEM] * 8, out_specs=(ANY, VMEM, SMEM), compiler_params=room(14),
         scratch_shapes=[
             pltpu.VMEM((2, 4, PART, 512), F32), pltpu.VMEM((2, 4, HALF, 128), F32), pltpu.SemaphoreType.DMA((16,)),
         ],
         cost_estimate=pl.CostEstimate(flops=4 * D * D, bytes_accessed=8_500_000, transcendentals=0),
         name="last",
-    )(idx, clip_norm, *own_half, *other_half)
+    )(clip_norm, *own_half, *other_half)
     return image_grad, weight_grad, bias_grad, loss
 
 

time: 111 us -> 109 us (0.982)
  no operation moved by 1% of the time
where the time goes in v5:
time: 109 us
  starting transfers between devices  53.5 us (49%)
  waiting for transfers between devices  29.7 us (27%)
  Pallas kernels  16 us (15%)
  local copies, waits for them, and re-layouts  5.19 us (5%)
  between operations  3.54 us (3%)
    ppermute x13, starting transfers between devices, shifted(): lax.ppermute(block, axis, [(i, (i + distance) % size) for i in range(size)])  22 us
    ppermute x13, waiting for transfers between devices, shifted(): lax.ppermute(block, axis, [(i, (i + distance) % size) for i in range(size)])  19.5 us
    all_to_all x1, starting transfers between devices, local(): lax.all_to_all(tiles.reshape(32, 48, 128), ALL, 0, 0, axis_index_groups=g...  9.49 us
    all_to_all x1, starting transfers between devices, local(): a1 = lax.all_to_all(copies, ALL, 0, 0, axis_index_groups=turned, tiled=True)  8.47 us
    ppermute x3, waiting for transfers between devices, local(): r2, r1, r3 = [lax.ppermute(parts[s], ALL, around(s)) for s in (2, 1, 3)]  5.32 us
    ppermute x3, starting transfers between devices, local(): r2, r1, r3 = [lax.ppermute(parts[s], ALL, around(s)) for s in (2, 1, 3)]  4.8 us
    unnamed x8, local copies, waits for them, and re-layouts  4.47 us
    ppermute x1, starting transfers between devices, local(): lax.ppermute(texts, ('yh', 'core'), [(0, 3), (1, 2), (2, 1), (3, 0)])  4.39 us
  transfers between devices with their start and end apart: 22, of which 9 were waited for; matrix products, arithmetic and copies ran while one was open for 2% of the time, Pallas kernels for 4%

profile of v5, /device:TPU:1, one launch (start us, length us, event | category | flops | bytes accessed | tf_op | source)
XLA Modules:
  0.0 109.0 jit_solution(3681819973435623484)
XLA Ops:
  0.6 4.4 %collective-permute-start.3 = (bf16[128,1152]{1,0:T(8,128)(2,1)}, bf16[128,1152]{1,0:T(8,128)(2,1)S(1)}, u32[]{:S(2)}, u32[]{:S(2)}) collective-permute-start(bf16[128,1152]{1,0:T(8,128)(2,1)} %t_ref.1), channel_id=1, source_target_pairs={{0,48},{16,32},{32,16},{48,0},{1,49},{17,33},{33,17},{49,1},{2,50}... | collective-permute-start | bytes 884744 | tf_op jit(solution)/shard_map/ppermute | solution.py:293
  5.0 1.8 %collective-permute-start.5 = (bf16[128,1152]{1,0:T(8,128)(2,1)}, bf16[128,1152]{1,0:T(8,128)(2,1)S(1)}, u32[]{:S(2)}, u32[]{:S(2)}) collective-permute-start(bf16[128,1152]{1,0:T(8,128)(2,1)} %t_ref.1), channel_id=1, source_target_pairs={{0,32},{32,0},{1,33},{33,1},{2,34},{34,2},{3,35},{35,3},{4,36},{36... | collective-permute-start | bytes 884744 | tf_op jit(solution)/shard_map/ppermute | solution.py:74
  10.0 2.2 %collective-permute-done.3.t_ref = bf16[128,1152]{1,0:T(8,128)(2,1)S(1)} collective-permute-done((bf16[128,1152]{1,0:T(8,128)(2,1)}, bf16[128,1152]{1,0:T(8,128)(2,1)S(1)}, u32[]{:S(2)}, u32[]{:S(2)}) %collective-permute-start.3) | collective-permute-done | bytes 294944 | tf_op jit(solution)/shard_map/ppermute | solution.py:293
  12.1 2.9 %collective-permute-start.4 = (bf16[128,1152]{1,0:T(8,128)(2,1)}, bf16[128,1152]{1,0:T(8,128)(2,1)S(1)}, u32[]{:S(2)}, u32[]{:S(2)}) collective-permute-start(bf16[128,1152]{1,0:T(8,128)(2,1)} %t_ref.1), channel_id=1, source_target_pairs={{0,16},{16,0},{1,17},{17,1},{2,18},{18,2},{3,19},{19,3},{4,20},{20... | collective-permute-start | bytes 884744 | tf_op jit(solution)/shard_map/ppermute | solution.py:74
  15.0 1.7 %copy-done = bf16[1152,1152]{1,0:T(8,128)(2,1)S(1)} copy-done((bf16[1152,1152]{1,0:T(8,128)(2,1)S(1)}, bf16[1152,1152]{1,0:T(8,128)(2,1)}, u32[]{:S(2)}) %copy-start) | copy-done | bytes 2654232
  20.6 1.8 %copy-done.1 = bf16[1152,1152]{1,0:T(8,128)(2,1)S(1)} copy-done((bf16[1152,1152]{1,0:T(8,128)(2,1)S(1)}, bf16[1152,1152]{1,0:T(8,128)(2,1)}, u32[]{:S(2)}) %copy-start.1) | copy-done | bytes 2654232
  24.6 4.2 %pairs.1 = (bf16[512,512]{1,0:T(8,128)(2,1)S(1)}, bf16[544,640]{1,0:T(8,128)(2,1)S(1)}, bf16[544,640]{1,0:T(8,128)(2,1)S(1)}) custom-call(s32[3]{0:T(128)S(1)} %pad_add_fusion.core_ref, f32[3]{0:T(128)S(1)} %pad_maximum_fusion.scal_ref, bf16[128,1152]{1,0:T(8,128)(2,1)S(1)} %copy-done.3, bf16[128,1152]{1,0:T(8,128)(2,1)S(1)} %collective-permute-done.i1, ...), custom_call_target="tpu_custom_call" | custom-call | flops 1207959552 | bytes 5500000 | tf_op jit(solution)/shard_map/pairs/pallas_call | solution.py:310
  29.0 2.1 %collective-permute-done.6.got_ref = bf16[544,640]{1,0:T(8,128)(2,1)S(1)} collective-permute-done((bf16[544,640]{1,0:T(8,128)(2,1)S(1)}, bf16[544,640]{1,0:T(8,128)(2,1)S(1)}, u32[]{:S(2)}, u32[]{:S(2)}) %collective-permute-start.6) | collective-permute-done | bytes 696352 | tf_op jit(solution)/shard_map/ppermute | solution.py:74
  31.1 1.4 %head.1 = (bf16[1328,128]{1,0:T(8,128)(2,1)S(1)}, bf16[1328,128]{1,0:T(8,128)(2,1)S(1)}, bf16[1328,128]{1,0:T(8,128)(2,1)S(1)}, bf16[1328,128]{1,0:T(8,128)(2,1)S(1)}) custom-call(bf16[1152,128]{1,0:T(8,128)(2,1)S(1)} %get-tuple-element.58.f0, bf16[1152,128]{1,0:T(8,128)(2,1)S(1)} %get-tuple-element.59.f1, bf16[1152,128]{1,0:T(8,128)(2,1)S(1)} %get-tuple-element.60.f2, ...), custom_call_target="tpu_custom_call" | custom-call | flops 754974720 | bytes 4000000 | tf_op jit(solution)/shard_map/head/pallas_call | solution.py:330
  33.5 2.6 %collective-permute-start.8 = (bf16[1328,128]{1,0:T(8,128)(2,1)S(1)}, bf16[1328,128]{1,0:T(8,128)(2,1)S(1)}, u32[]{:S(2)}, u32[]{:S(2)}) collective-permute-start(bf16[1328,128]{1,0:T(8,128)(2,1)S(1)} %get-tuple-element.66), channel_id=1, source_target_pairs={{0,128},{1,129},{2,130},{3,131},{4,132},{5,133},{6,134},{7,135},{8... | collective-permute-start | bytes 1019912 | tf_op jit(solution)/shard_map/ppermute | solution.py:341
  37.2 1.9 %image_side.1 = (f32[128,1152]{1,0:T(8,128)S(1)}, bf16[128,1152]{1,0:T(8,128)(2,1)S(1)}, bf16[128,1152]{1,0:T(8,128)(2,1)S(1)}, bf16[128,1152]{1,0:T(8,128)(2,1)S(1)}) custom-call(f32[3]{0:T(128)S(1)} %pad_maximum_fusion.scal_ref, bf16[128,1152]{1,0:T(8,128)(2,1)S(1)} %copy-done.3, bf16[128,1152]{1,0:T(8,128)(2,1)S(1)} %collective-permute-done.i1, ...), custom_call_target="tpu_custom_call" | custom-call | flops 603979776 | bytes 5500000 | tf_op jit(solution)/shard_map/image_side/pallas_call | solution.py:320
  40.1 4.3 %collective-permute-done.8.a2 = bf16[1328,128]{1,0:T(8,128)(2,1)S(1)} collective-permute-done((bf16[1328,128]{1,0:T(8,128)(2,1)S(1)}, bf16[1328,128]{1,0:T(8,128)(2,1)S(1)}, u32[]{:S(2)}, u32[]{:S(2)}) %collective-permute-start.8) | collective-permute-done | bytes 340000 | tf_op jit(solution)/shard_map/ppermute | solution.py:341
  45.4 9.5 %all-to-all-start = ((bf16[32,48,128]{2,1,0:T(8,128)(2,1)}), bf16[32,48,128]{2,1,0:T(8,128)(2,1)S(1)}, u32[]{:S(2)}, u32[]{:S(2)}) async-start(bf16[32,48,128]{2,1,0:T(8,128)(2,1)} %bitcast.3), calls=%async_computation | async-start | bytes 786432 | tf_op jit(solution)/shard_map/all_to_all | solution.py:351
  54.9 2.5 %collective-permute-start.10 = (bf16[128,1152]{1,0:T(8,128)(2,1)S(1)}, bf16[128,1152]{1,0:T(8,128)(2,1)S(1)}, u32[]{:S(2)}, u32[]{:S(2)}) collective-permute-start(bf16[128,1152]{1,0:T(8,128)(2,1)S(1)} %get-tuple-element.69), channel_id=1, source_target_pairs={{0,192},{64,0},{128,64},{192,128},{1,193},{65,1},{129,65},{193,129... | collective-permute-start | bytes 884744 | tf_op jit(solution)/shard_map/ppermute | solution.py:74
  57.4 6.3 %collective-permute-done.10 = bf16[128,1152]{1,0:T(8,128)(2,1)S(1)} collective-permute-done((bf16[128,1152]{1,0:T(8,128)(2,1)S(1)}, bf16[128,1152]{1,0:T(8,128)(2,1)S(1)}, u32[]{:S(2)}, u32[]{:S(2)}) %collective-permute-start.10) | collective-permute-done | bytes 294944 | tf_op jit(solution)/shard_map/ppermute | solution.py:74
  63.7 3.1 %collective-permute-done.11 = bf16[128,1152]{1,0:T(8,128)(2,1)S(1)} collective-permute-done((bf16[128,1152]{1,0:T(8,128)(2,1)S(1)}, bf16[128,1152]{1,0:T(8,128)(2,1)S(1)}, u32[]{:S(2)}, u32[]{:S(2)}) %collective-permute-start.11) | collective-permute-done | bytes 294944 | tf_op jit(solution)/shard_map/ppermute | solution.py:74
  67.6 8.5 %all-to-all-start.1 = ((bf16[32,48,128]{2,1,0:T(8,128)(2,1)}), bf16[32,48,128]{2,1,0:T(8,128)(2,1)S(1)}, u32[]{:S(2)}, u32[]{:S(2)}) async-start(bf16[32,48,128]{2,1,0:T(8,128)(2,1)} %copies.1), calls=%async_computation.1 | async-start | bytes 786432 | tf_op jit(solution)/shard_map/all_to_all | solution.py:361
  77.4 7.7 %collective-permute-done.12 = bf16[128,1152]{1,0:T(8,128)(2,1)S(1)} collective-permute-done((bf16[128,1152]{1,0:T(8,128)(2,1)S(1)}, bf16[128,1152]{1,0:T(8,128)(2,1)S(1)}, u32[]{:S(2)}, u32[]{:S(2)}) %collective-permute-start.12) | collective-permute-done | bytes 294944 | tf_op jit(solution)/shard_map/ppermute | solution.py:74
  85.1 3.6 %collective-permute-start.15 = (bf16[1328,128]{1,0:T(8,128)(2,1)S(1)}, bf16[1328,128]{1,0:T(8,128)(2,1)S(1)}, u32[]{:S(2)}, u32[]{:S(2)}) collective-permute-start(bf16[1328,128]{1,0:T(8,128)(2,1)S(1)} %slice.4.p0), channel_id=1, source_target_pairs={{0,192},{1,193},{2,194},{3,195},{4,196},{5,197},{6,198},{7,199},{8... | collective-permute-start | bytes 1019912 | tf_op jit(solution)/shard_map/ppermute | solution.py:366
  90.0 3.8 %collective-permute-start.16 = (bf16[1328,128]{1,0:T(8,128)(2,1)S(1)}, bf16[1328,128]{1,0:T(8,128)(2,1)S(1)}, u32[]{:S(2)}, u32[]{:S(2)}) collective-permute-start(bf16[1328,128]{1,0:T(8,128)(2,1)S(1)} %slice.4.p0), channel_id=1, source_target_pairs={{0,16},{16,0},{1,17},{17,1},{2,18},{18,2},{3,19},{19,3},{4,20},{20... | collective-permute-start | bytes 1019912 | tf_op jit(solution)/shard_map/ppermute | solution.py:74
  93.8 2.6 %collective-permute-done.15.p3 = bf16[1328,128]{1,0:T(8,128)(2,1)S(1)} collective-permute-done((bf16[1328,128]{1,0:T(8,128)(2,1)S(1)}, bf16[1328,128]{1,0:T(8,128)(2,1)S(1)}, u32[]{:S(2)}, u32[]{:S(2)}) %collective-permute-start.15) | collective-permute-done | bytes 340000 | tf_op jit(solution)/shard_map/ppermute | solution.py:366
  96.9 3.1 %collective-permute-start.18 = (bf16[1328,128]{1,0:T(8,128)(2,1)S(1)}, bf16[1328,128]{1,0:T(8,128)(2,1)S(1)}, u32[]{:S(2)}, u32[]{:S(2)}) collective-permute-start(bf16[1328,128]{1,0:T(8,128)(2,1)S(1)} %collective-permute-done.14.p2), channel_id=1, source_target_pairs={{0,16},{16,0},{1,17},{17,1},{2,18},{18,2},{3,19},{19,3},{4,20},{20... | collective-permute-start | bytes 1019912 | tf_op jit(solution)/shard_map/ppermute | solution.py:74
  100.0 3.5 %collective-permute-start.17 = (bf16[1328,128]{1,0:T(8,128)(2,1)S(1)}, bf16[1328,128]{1,0:T(8,128)(2,1)S(1)}, u32[]{:S(2)}, u32[]{:S(2)}) collective-permute-start(bf16[1328,128]{1,0:T(8,128)(2,1)S(1)} %collective-permute-done.13.p1), channel_id=1, source_target_pairs={{0,16},{16,0},{1,17},{17,1},{2,18},{18,2},{3,19},{19,3},{4,20},{20... | collective-permute-start | bytes 1019912 | tf_op jit(solution)/shard_map/ppermute | solution.py:74
  104.9 3.9 %last.1 = (f32[1152,1152]{1,0:T(8,128)}, f32[1152]{0:T(1024)}, f32[1]{0:T(128)}) custom-call(f32[1]{0:T(128)S(6)} %copy.15.clip_ref, bf16[1328,128]{1,0:T(8,128)(2,1)S(1)} %slice.4.p0, bf16[1328,128]{1,0:T(8,128)(2,1)S(1)} %collective-permute-done.13.p1, bf16[1328,128]{1,0:T(8,128)(2,1)S(1)} %collective-permute-done.14.p2, ...), custom_call_target="tpu_custom_call" | custom-call | flops 5308416 | bytes 8500000 | tf_op jit(solution)/shard_map/last/pallas_call | solution.py:369
  (43 shorter events, 15.9 us)
Async XLA Ops:
  0.6 11.5 %collective-permute-start.3 = (bf16[128,1152]{1,0:T(8,128)(2,1)}, bf16[128,1152]{1,0:T(8,128)(2,1)S(1)}, u32[]{:S(2)}, u32[]{:S(2)}) collective-permute-start(bf16[128,1152]{1,0:T(8,128)(2,1)} %t_ref.1), channel_id=1, source_target_pairs={{0,48},{16,32},{32,16},{48,0},{1,49},{17,33},{33,17},{49,1},{2,50}... | collective-permute-start | bytes 884744 | tf_op jit(solution)/shard_map/ppermute | solution.py:293
  5.0 18.1 %collective-permute-start.5 = (bf16[128,1152]{1,0:T(8,128)(2,1)}, bf16[128,1152]{1,0:T(8,128)(2,1)S(1)}, u32[]{:S(2)}, u32[]{:S(2)}) collective-permute-start(bf16[128,1152]{1,0:T(8,128)(2,1)} %t_ref.1), channel_id=1, source_target_pairs={{0,32},{32,0},{1,33},{33,1},{2,34},{34,2},{3,35},{35,3},{4,36},{36... | collective-permute-start | bytes 884744 | tf_op jit(solution)/shard_map/ppermute | solution.py:74
  6.8 17.8 %collective-permute-start.2 = (bf16[128,1152]{1,0:T(8,128)(2,1)}, bf16[128,1152]{1,0:T(8,128)(2,1)S(1)}, u32[]{:S(2)}, u32[]{:S(2)}) collective-permute-start(bf16[128,1152]{1,0:T(8,128)(2,1)} %i0.3), channel_id=1, source_target_pairs={{0,192},{64,0},{128,64},{192,128},{1,193},{65,1},{129,65},{193,129... | collective-permute-start | bytes 884744 | tf_op jit(solution)/shard_map/ppermute | solution.py:74
  7.6 17.0 %collective-permute-start.1 = (bf16[128,1152]{1,0:T(8,128)(2,1)}, bf16[128,1152]{1,0:T(8,128)(2,1)S(1)}, u32[]{:S(2)}, u32[]{:S(2)}) collective-permute-start(bf16[128,1152]{1,0:T(8,128)(2,1)} %i0.3), channel_id=1, source_target_pairs={{0,64},{64,128},{128,192},{192,0},{1,65},{65,129},{129,193},{193,1... | collective-permute-start | bytes 884744 | tf_op jit(solution)/shard_map/ppermute | solution.py:74
  8.3 16.3 %collective-permute-start = (bf16[128,1152]{1,0:T(8,128)(2,1)}, bf16[128,1152]{1,0:T(8,128)(2,1)S(1)}, u32[]{:S(2)}, u32[]{:S(2)}) collective-permute-start(bf16[128,1152]{1,0:T(8,128)(2,1)} %i0.3), channel_id=1, source_target_pairs={{0,128},{64,192},{128,0},{192,64},{1,129},{65,193},{129,1},{193,65... | collective-permute-start | bytes 884744 | tf_op jit(solution)/shard_map/ppermute | solution.py:74
  12.1 11.7 %collective-permute-start.4 = (bf16[128,1152]{1,0:T(8,128)(2,1)}, bf16[128,1152]{1,0:T(8,128)(2,1)S(1)}, u32[]{:S(2)}, u32[]{:S(2)}) collective-permute-start(bf16[128,1152]{1,0:T(8,128)(2,1)} %t_ref.1), channel_id=1, source_target_pairs={{0,16},{16,0},{1,17},{17,1},{2,18},{18,2},{3,19},{19,3},{4,20},{20... | collective-permute-start | bytes 884744 | tf_op jit(solution)/shard_map/ppermute | solution.py:74
  17.8 6.9 %copy-start.3 = (bf16[128,1152]{1,0:T(8,128)(2,1)S(1)}, bf16[128,1152]{1,0:T(8,128)(2,1)}, u32[]{:S(2)}) copy-start(bf16[128,1152]{1,0:T(8,128)(2,1)} %i0.3) | copy-start | bytes 884740
  20.6 1.8 %copy-start.1 = (bf16[1152,1152]{1,0:T(8,128)(2,1)S(1)}, bf16[1152,1152]{1,0:T(8,128)(2,1)}, u32[]{:S(2)}) copy-start(bf16[1152,1152]{1,0:T(8,128)(2,1)} %w_ref.7) | copy-start | bytes 7962628
  28.8 2.2 %collective-permute-start.6 = (bf16[544,640]{1,0:T(8,128)(2,1)S(1)}, bf16[544,640]{1,0:T(8,128)(2,1)S(1)}, u32[]{:S(2)}, u32[]{:S(2)}) collective-permute-start(bf16[544,640]{1,0:T(8,128)(2,1)S(1)} %get-tuple-element.63), channel_id=1, source_target_pairs={{0,16},{16,0},{1,17},{17,1},{2,18},{18,2},{3,19},{19,3},{4,20},{20... | collective-permute-start | bytes 2088968 | tf_op jit(solution)/shard_map/ppermute | solution.py:74
  32.4 7.6 %collective-permute-start.7 = (bf16[1328,128]{1,0:T(8,128)(2,1)S(1)}, bf16[1328,128]{1,0:T(8,128)(2,1)S(1)}, u32[]{:S(2)}, u32[]{:S(2)}) collective-permute-start(bf16[1328,128]{1,0:T(8,128)(2,1)S(1)} %get-tuple-element.65), channel_id=1, source_target_pairs={{0,64},{1,65},{2,66},{3,67},{4,68},{5,69},{6,70},{7,71},{8,72},{9,... | collective-permute-start | bytes 1019912 | tf_op jit(solution)/shard_map/ppermute | solution.py:341
  33.5 10.9 %collective-permute-start.8 = (bf16[1328,128]{1,0:T(8,128)(2,1)S(1)}, bf16[1328,128]{1,0:T(8,128)(2,1)S(1)}, u32[]{:S(2)}, u32[]{:S(2)}) collective-permute-start(bf16[1328,128]{1,0:T(8,128)(2,1)S(1)} %get-tuple-element.66), channel_id=1, source_target_pairs={{0,128},{1,129},{2,130},{3,131},{4,132},{5,133},{6,134},{7,135},{8... | collective-permute-start | bytes 1019912 | tf_op jit(solution)/shard_map/ppermute | solution.py:341
  36.2 8.2 %collective-permute-start.9 = (bf16[1328,128]{1,0:T(8,128)(2,1)S(1)}, bf16[1328,128]{1,0:T(8,128)(2,1)S(1)}, u32[]{:S(2)}, u32[]{:S(2)}) collective-permute-start(bf16[1328,128]{1,0:T(8,128)(2,1)S(1)} %get-tuple-element.67), channel_id=1, source_target_pairs={{0,192},{1,193},{2,194},{3,195},{4,196},{5,197},{6,198},{7,199},{8... | collective-permute-start | bytes 1019912 | tf_op jit(solution)/shard_map/ppermute | solution.py:341
  45.4 21.5 %all-to-all-start = ((bf16[32,48,128]{2,1,0:T(8,128)(2,1)}), bf16[32,48,128]{2,1,0:T(8,128)(2,1)S(1)}, u32[]{:S(2)}, u32[]{:S(2)}) async-start(bf16[32,48,128]{2,1,0:T(8,128)(2,1)} %bitcast.3), calls=%async_computation | async-start | bytes 786432 | tf_op jit(solution)/shard_map/all_to_all | solution.py:351
  54.9 8.8 %collective-permute-start.10 = (bf16[128,1152]{1,0:T(8,128)(2,1)S(1)}, bf16[128,1152]{1,0:T(8,128)(2,1)S(1)}, u32[]{:S(2)}, u32[]{:S(2)}) collective-permute-start(bf16[128,1152]{1,0:T(8,128)(2,1)S(1)} %get-tuple-element.69), channel_id=1, source_target_pairs={{0,192},{64,0},{128,64},{192,128},{1,193},{65,1},{129,65},{193,129... | collective-permute-start | bytes 884744 | tf_op jit(solution)/shard_map/ppermute | solution.py:74
  57.4 9.4 %collective-permute-start.11 = (bf16[128,1152]{1,0:T(8,128)(2,1)S(1)}, bf16[128,1152]{1,0:T(8,128)(2,1)S(1)}, u32[]{:S(2)}, u32[]{:S(2)}) collective-permute-start(bf16[128,1152]{1,0:T(8,128)(2,1)S(1)} %get-tuple-element.70), channel_id=1, source_target_pairs={{0,64},{64,128},{128,192},{192,0},{1,65},{65,129},{129,193},{193,1... | collective-permute-start | bytes 884744 | tf_op jit(solution)/shard_map/ppermute | solution.py:74
  67.6 17.4 %all-to-all-start.1 = ((bf16[32,48,128]{2,1,0:T(8,128)(2,1)}), bf16[32,48,128]{2,1,0:T(8,128)(2,1)S(1)}, u32[]{:S(2)}, u32[]{:S(2)}) async-start(bf16[32,48,128]{2,1,0:T(8,128)(2,1)} %copies.1), calls=%async_computation.1 | async-start | bytes 786432 | tf_op jit(solution)/shard_map/all_to_all | solution.py:361
  76.1 8.9 %collective-permute-start.12 = (bf16[128,1152]{1,0:T(8,128)(2,1)S(1)}, bf16[128,1152]{1,0:T(8,128)(2,1)S(1)}, u32[]{:S(2)}, u32[]{:S(2)}) collective-permute-start(bf16[128,1152]{1,0:T(8,128)(2,1)S(1)} %get-tuple-element.72), channel_id=1, source_target_pairs={{0,128},{64,192},{128,0},{192,64},{1,129},{65,193},{129,1},{193,65... | collective-permute-start | bytes 884744 | tf_op jit(solution)/shard_map/ppermute | solution.py:74
  85.1 11.4 %collective-permute-start.15 = (bf16[1328,128]{1,0:T(8,128)(2,1)S(1)}, bf16[1328,128]{1,0:T(8,128)(2,1)S(1)}, u32[]{:S(2)}, u32[]{:S(2)}) collective-permute-start(bf16[1328,128]{1,0:T(8,128)(2,1)S(1)} %slice.4.p0), channel_id=1, source_target_pairs={{0,192},{1,193},{2,194},{3,195},{4,196},{5,197},{6,198},{7,199},{8... | collective-permute-start | bytes 1019912 | tf_op jit(solution)/shard_map/ppermute | solution.py:366
  88.7 8.3 %collective-permute-start.14 = (bf16[1328,128]{1,0:T(8,128)(2,1)S(1)}, bf16[1328,128]{1,0:T(8,128)(2,1)S(1)}, u32[]{:S(2)}, u32[]{:S(2)}) collective-permute-start(bf16[1328,128]{1,0:T(8,128)(2,1)S(1)} %slice.4.p0), channel_id=1, source_target_pairs={{0,128},{1,129},{2,130},{3,131},{4,132},{5,133},{6,134},{7,135},{8... | collective-permute-start | bytes 1019912 | tf_op jit(solution)/shard_map/ppermute | solution.py:366
  88.7 11.4 %collective-permute-start.13 = (bf16[1328,128]{1,0:T(8,128)(2,1)S(1)}, bf16[1328,128]{1,0:T(8,128)(2,1)S(1)}, u32[]{:S(2)}, u32[]{:S(2)}) collective-permute-start(bf16[1328,128]{1,0:T(8,128)(2,1)S(1)} %slice.4.p0), channel_id=1, source_target_pairs={{0,64},{1,65},{2,66},{3,67},{4,68},{5,69},{6,70},{7,71},{8,72},{9,... | collective-permute-start | bytes 1019912 | tf_op jit(solution)/shard_map/ppermute | solution.py:366
  90.0 14.5 %collective-permute-start.16 = (bf16[1328,128]{1,0:T(8,128)(2,1)S(1)}, bf16[1328,128]{1,0:T(8,128)(2,1)S(1)}, u32[]{:S(2)}, u32[]{:S(2)}) collective-permute-start(bf16[1328,128]{1,0:T(8,128)(2,1)S(1)} %slice.4.p0), channel_id=1, source_target_pairs={{0,16},{16,0},{1,17},{17,1},{2,18},{18,2},{3,19},{19,3},{4,20},{20... | collective-permute-start | bytes 1019912 | tf_op jit(solution)/shard_map/ppermute | solution.py:74
  96.5 8.1 %collective-permute-start.19 = (bf16[1328,128]{1,0:T(8,128)(2,1)S(1)}, bf16[1328,128]{1,0:T(8,128)(2,1)S(1)}, u32[]{:S(2)}, u32[]{:S(2)}) collective-permute-start(bf16[1328,128]{1,0:T(8,128)(2,1)S(1)} %collective-permute-done.15.p3), channel_id=1, source_target_pairs={{0,16},{16,0},{1,17},{17,1},{2,18},{18,2},{3,19},{19,3},{4,20},{20... | collective-permute-start | bytes 1019912 | tf_op jit(solution)/shard_map/ppermute | solution.py:74
  96.9 7.6 %collective-permute-start.18 = (bf16[1328,128]{1,0:T(8,128)(2,1)S(1)}, bf16[1328,128]{1,0:T(8,128)(2,1)S(1)}, u32[]{:S(2)}, u32[]{:S(2)}) collective-permute-start(bf16[1328,128]{1,0:T(8,128)(2,1)S(1)} %collective-permute-done.14.p2), channel_id=1, source_target_pairs={{0,16},{16,0},{1,17},{17,1},{2,18},{18,2},{3,19},{19,3},{4,20},{20... | collective-permute-start | bytes 1019912 | tf_op jit(solution)/shard_map/ppermute | solution.py:74
  100.0 4.8 %collective-permute-start.17 = (bf16[1328,128]{1,0:T(8,128)(2,1)S(1)}, bf16[1328,128]{1,0:T(8,128)(2,1)S(1)}, u32[]{:S(2)}, u32[]{:S(2)}) collective-permute-start(bf16[1328,128]{1,0:T(8,128)(2,1)S(1)} %collective-permute-done.13.p1), channel_id=1, source_target_pairs={{0,16},{16,0},{1,17},{17,1},{2,18},{18,2},{3,19},{19,3},{4,20},{20... | collective-permute-start | bytes 1019912 | tf_op jit(solution)/shard_map/ppermute | solution.py:74
  (2 other events, 2.7 us)

commit v6 on v5

--- a/solution.py
+++ b/solution.py
@@ -87,7 +87,7 @@
     inv_ref[...] = jnp.broadcast_to(inv, (OWN, 128))
 
 
-def pair_kernel(core_ref, scal_ref, i0, i1, i2, i3, y0, y1, y2, y3, v0, v1, v2, v3,
+def pair_kernel(scal_ref, i0, i1, i2, i3, y0, y1, y2, y3, v0, v1, v2, v3,
                 gs, keep_ref, give_ref, xb, yb, ext):
     scale, shift, gfac = scal_ref[0], scal_ref[1], scal_ref[2]
     for k, ref in enumerate((i0, i1, i2, i3)):
@@ -118,7 +118,7 @@
         part = 1.0 / (1.0 + e)
         gs[rows, :] = (gfac * signs * jnp.where(v >= 0, part, e * part)).astype(BF16)
     bias = jnp.zeros((1, D), F32)
-    first = core_ref[0] == 0
+    first = scal_ref[3] < 0.5
     for h in range(2):
         rows = slice(h * 256, (h + 1) * 256)
         dy = scale * lax.dot_general(
@@ -287,8 +287,8 @@
 
 def local(images, texts, head_weight, head_bias, logit_scale, logit_shift, loss_scale, clip_norm):
     core, at, at_other = spot()
-    idx = jnp.stack([core, at, at_other]).astype(jnp.int32)
-    scal = jnp.stack([logit_scale[0], logit_shift[0], -loss_scale[0] / TOTAL])
+    spots = jnp.stack([core, at, at_other]).astype(F32)
+    scal = jnp.concatenate([jnp.stack([logit_scale[0], logit_shift[0], -loss_scale[0] / TOTAL]), spots])
 
     cross = lax.ppermute(texts, ("yh", "core"), [(0, 3), (1, 2), (2, 1), (3, 0)])
     near, cross = lax.optimization_barrier((texts, cross))
@@ -310,13 +310,13 @@
     gs, keep, give = pl.pallas_call(
         pair_kernel,
         out_shape=(sds((4 * OWN, 4 * OWN), BF16),) + (sds((4 * OWN + 2 * ONE, WIDE), BF16),) * 2,
-        in_specs=[SMEM, SMEM] + [VMEM] * 12, out_specs=(VMEM,) * 3, compiler_params=room(20),
+        in_specs=[SMEM] + [VMEM] * 12, out_specs=(VMEM,) * 3, compiler_params=room(20),
         scratch_shapes=[
             pltpu.VMEM((4 * OWN, D), BF16), pltpu.VMEM((4 * OWN, D), BF16), pltpu.VMEM((ONE, 128), F32),
         ],
         cost_estimate=pl.CostEstimate(flops=4 * 512 * 512 * D, bytes_accessed=5_500_000, transcendentals=800_000),
         name="pairs",
-    )(idx, scal, *img, *ys, *invs)
+    )(scal, *img, *ys, *invs)
     ig0, ig1, ig2, ig3 = pl.pallas_call(
         image_kernel,
         out_shape=(sds((OWN, D), F32),) + (sds((OWN, D), BF16),) * 3,

time: 109 us -> 109 us (level)
  no operation moved by 1% of the time
where the time goes in v6:
time: 109 us
  starting transfers between devices  53.4 us (49%)
  waiting for transfers between devices  29.6 us (27%)
  Pallas kernels  16.1 us (15%)
  local copies, waits for them, and re-layouts  5.19 us (5%)
  between operations  3.54 us (3%)
  other arithmetic  1.09 us (1%)
    ppermute x13, starting transfers between devices, shifted(): lax.ppermute(block, axis, [(i, (i + distance) % size) for i in range(size)])  22 us
    ppermute x13, waiting for transfers between devices, shifted(): lax.ppermute(block, axis, [(i, (i + distance) % size) for i in range(size)])  19.5 us
    all_to_all x1, starting transfers between devices, local(): lax.all_to_all(tiles.reshape(32, 48, 128), ALL, 0, 0, axis_index_groups=g...  9.51 us
    all_to_all x1, starting transfers between devices, local(): a1 = lax.all_to_all(copies, ALL, 0, 0, axis_index_groups=turned, tiled=True)  8.47 us
    ppermute x3, waiting for transfers between devices, local(): r2, r1, r3 = [lax.ppermute(parts[s], ALL, around(s)) for s in (2, 1, 3)]  5.22 us
    ppermute x3, starting transfers between devices, local(): r2, r1, r3 = [lax.ppermute(parts[s], ALL, around(s)) for s in (2, 1, 3)]  4.79 us
    unnamed x8, local copies, waits for them, and re-layouts  4.47 us
    ppermute x1, starting transfers between devices, local(): lax.ppermute(texts, ('yh', 'core'), [(0, 3), (1, 2), (2, 1), (3, 0)])  4.39 us
  transfers between devices with their start and end apart: 22, of which 9 were waited for; matrix products, arithmetic and copies ran while one was open for 2% of the time, Pallas kernels for 4%

profile of v6, /device:TPU:1, one launch (start us, length us, event | category | flops | bytes accessed | tf_op | source)
XLA Modules:
  0.0 108.9 jit_solution(9187153074642204114)
XLA Ops:
  0.6 4.4 %collective-permute-start.3 = (bf16[128,1152]{1,0:T(8,128)(2,1)}, bf16[128,1152]{1,0:T(8,128)(2,1)S(1)}, u32[]{:S(2)}, u32[]{:S(2)}) collective-permute-start(bf16[128,1152]{1,0:T(8,128)(2,1)} %t_ref.1), channel_id=1, source_target_pairs={{0,48},{16,32},{32,16},{48,0},{1,49},{17,33},{33,17},{49,1},{2,50}... | collective-permute-start | bytes 884744 | tf_op jit(solution)/shard_map/ppermute | solution.py:293
  5.0 1.8 %collective-permute-start.5 = (bf16[128,1152]{1,0:T(8,128)(2,1)}, bf16[128,1152]{1,0:T(8,128)(2,1)S(1)}, u32[]{:S(2)}, u32[]{:S(2)}) collective-permute-start(bf16[128,1152]{1,0:T(8,128)(2,1)} %t_ref.1), channel_id=1, source_target_pairs={{0,32},{32,0},{1,33},{33,1},{2,34},{34,2},{3,35},{35,3},{4,36},{36... | collective-permute-start | bytes 884744 | tf_op jit(solution)/shard_map/ppermute | solution.py:74
  10.0 2.2 %collective-permute-done.3.t_ref = bf16[128,1152]{1,0:T(8,128)(2,1)S(1)} collective-permute-done((bf16[128,1152]{1,0:T(8,128)(2,1)}, bf16[128,1152]{1,0:T(8,128)(2,1)S(1)}, u32[]{:S(2)}, u32[]{:S(2)}) %collective-permute-start.3) | collective-permute-done | bytes 294944 | tf_op jit(solution)/shard_map/ppermute | solution.py:293
  12.1 2.9 %collective-permute-start.4 = (bf16[128,1152]{1,0:T(8,128)(2,1)}, bf16[128,1152]{1,0:T(8,128)(2,1)S(1)}, u32[]{:S(2)}, u32[]{:S(2)}) collective-permute-start(bf16[128,1152]{1,0:T(8,128)(2,1)} %t_ref.1), channel_id=1, source_target_pairs={{0,16},{16,0},{1,17},{17,1},{2,18},{18,2},{3,19},{19,3},{4,20},{20... | collective-permute-start | bytes 884744 | tf_op jit(solution)/shard_map/ppermute | solution.py:74
  15.0 1.7 %copy-done = bf16[1152,1152]{1,0:T(8,128)(2,1)S(1)} copy-done((bf16[1152,1152]{1,0:T(8,128)(2,1)S(1)}, bf16[1152,1152]{1,0:T(8,128)(2,1)}, u32[]{:S(2)}) %copy-start) | copy-done | bytes 2654232
  20.6 1.8 %copy-done.1 = bf16[1152,1152]{1,0:T(8,128)(2,1)S(1)} copy-done((bf16[1152,1152]{1,0:T(8,128)(2,1)S(1)}, bf16[1152,1152]{1,0:T(8,128)(2,1)}, u32[]{:S(2)}) %copy-start.1) | copy-done | bytes 2654232
  24.6 4.2 %pairs.1 = (bf16[512,512]{1,0:T(8,128)(2,1)S(1)}, bf16[544,640]{1,0:T(8,128)(2,1)S(1)}, bf16[544,640]{1,0:T(8,128)(2,1)S(1)}) custom-call(f32[6]{0:T(128)S(1)} %pad_maximum_fusion.scal_ref, bf16[128,1152]{1,0:T(8,128)(2,1)S(1)} %copy-done.3, bf16[128,1152]{1,0:T(8,128)(2,1)S(1)} %collective-permute-done.i1, bf16[128,1152]{1,0:T(8,128)(2,1)S(1)} %collective-permute-done.1.i2, ...), custom_call_target="tpu_custom_call" | custom-call | flops 1207959552 | bytes 5500000 | tf_op jit(solution)/shard_map/pairs/pallas_call | solution.py:310
  29.0 2.1 %collective-permute-done.6.got_ref = bf16[544,640]{1,0:T(8,128)(2,1)S(1)} collective-permute-done((bf16[544,640]{1,0:T(8,128)(2,1)S(1)}, bf16[544,640]{1,0:T(8,128)(2,1)S(1)}, u32[]{:S(2)}, u32[]{:S(2)}) %collective-permute-start.6) | collective-permute-done | bytes 696352 | tf_op jit(solution)/shard_map/ppermute | solution.py:74
  31.1 1.4 %head.1 = (bf16[1328,128]{1,0:T(8,128)(2,1)S(1)}, bf16[1328,128]{1,0:T(8,128)(2,1)S(1)}, bf16[1328,128]{1,0:T(8,128)(2,1)S(1)}, bf16[1328,128]{1,0:T(8,128)(2,1)S(1)}) custom-call(bf16[1152,128]{1,0:T(8,128)(2,1)S(1)} %get-tuple-element.58.f0, bf16[1152,128]{1,0:T(8,128)(2,1)S(1)} %get-tuple-element.59.f1, bf16[1152,128]{1,0:T(8,128)(2,1)S(1)} %get-tuple-element.60.f2, ...), custom_call_target="tpu_custom_call" | custom-call | flops 754974720 | bytes 4000000 | tf_op jit(solution)/shard_map/head/pallas_call | solution.py:330
  33.6 2.6 %collective-permute-start.8 = (bf16[1328,128]{1,0:T(8,128)(2,1)S(1)}, bf16[1328,128]{1,0:T(8,128)(2,1)S(1)}, u32[]{:S(2)}, u32[]{:S(2)}) collective-permute-start(bf16[1328,128]{1,0:T(8,128)(2,1)S(1)} %get-tuple-element.66), channel_id=1, source_target_pairs={{0,128},{1,129},{2,130},{3,131},{4,132},{5,133},{6,134},{7,135},{8... | collective-permute-start | bytes 1019912 | tf_op jit(solution)/shard_map/ppermute | solution.py:341
  37.3 2.0 %image_side.1 = (f32[128,1152]{1,0:T(8,128)S(1)}, bf16[128,1152]{1,0:T(8,128)(2,1)S(1)}, bf16[128,1152]{1,0:T(8,128)(2,1)S(1)}, bf16[128,1152]{1,0:T(8,128)(2,1)S(1)}) custom-call(f32[6]{0:T(128)S(1)} %pad_maximum_fusion.scal_ref, bf16[128,1152]{1,0:T(8,128)(2,1)S(1)} %copy-done.3, bf16[128,1152]{1,0:T(8,128)(2,1)S(1)} %collective-permute-done.i1, ...), custom_call_target="tpu_custom_call" | custom-call | flops 603979776 | bytes 5500000 | tf_op jit(solution)/shard_map/image_side/pallas_call | solution.py:320
  40.1 4.3 %collective-permute-done.8.a2 = bf16[1328,128]{1,0:T(8,128)(2,1)S(1)} collective-permute-done((bf16[1328,128]{1,0:T(8,128)(2,1)S(1)}, bf16[1328,128]{1,0:T(8,128)(2,1)S(1)}, u32[]{:S(2)}, u32[]{:S(2)}) %collective-permute-start.8) | collective-permute-done | bytes 340000 | tf_op jit(solution)/shard_map/ppermute | solution.py:341
  45.4 9.5 %all-to-all-start = ((bf16[32,48,128]{2,1,0:T(8,128)(2,1)}), bf16[32,48,128]{2,1,0:T(8,128)(2,1)S(1)}, u32[]{:S(2)}, u32[]{:S(2)}) async-start(bf16[32,48,128]{2,1,0:T(8,128)(2,1)} %bitcast.3), calls=%async_computation | async-start | bytes 786432 | tf_op jit(solution)/shard_map/all_to_all | solution.py:351
  54.9 2.5 %collective-permute-start.10 = (bf16[128,1152]{1,0:T(8,128)(2,1)S(1)}, bf16[128,1152]{1,0:T(8,128)(2,1)S(1)}, u32[]{:S(2)}, u32[]{:S(2)}) collective-permute-start(bf16[128,1152]{1,0:T(8,128)(2,1)S(1)} %get-tuple-element.69), channel_id=1, source_target_pairs={{0,192},{64,0},{128,64},{192,128},{1,193},{65,1},{129,65},{193,129... | collective-permute-start | bytes 884744 | tf_op jit(solution)/shard_map/ppermute | solution.py:74
  57.4 6.3 %collective-permute-done.10 = bf16[128,1152]{1,0:T(8,128)(2,1)S(1)} collective-permute-done((bf16[128,1152]{1,0:T(8,128)(2,1)S(1)}, bf16[128,1152]{1,0:T(8,128)(2,1)S(1)}, u32[]{:S(2)}, u32[]{:S(2)}) %collective-permute-start.10) | collective-permute-done | bytes 294944 | tf_op jit(solution)/shard_map/ppermute | solution.py:74
  63.7 3.1 %collective-permute-done.11 = bf16[128,1152]{1,0:T(8,128)(2,1)S(1)} collective-permute-done((bf16[128,1152]{1,0:T(8,128)(2,1)S(1)}, bf16[128,1152]{1,0:T(8,128)(2,1)S(1)}, u32[]{:S(2)}, u32[]{:S(2)}) %collective-permute-start.11) | collective-permute-done | bytes 294944 | tf_op jit(solution)/shard_map/ppermute | solution.py:74
  67.7 8.5 %all-to-all-start.1 = ((bf16[32,48,128]{2,1,0:T(8,128)(2,1)}), bf16[32,48,128]{2,1,0:T(8,128)(2,1)S(1)}, u32[]{:S(2)}, u32[]{:S(2)}) async-start(bf16[32,48,128]{2,1,0:T(8,128)(2,1)} %copies.1), calls=%async_computation.1 | async-start | bytes 786432 | tf_op jit(solution)/shard_map/all_to_all | solution.py:361
  77.4 7.7 %collective-permute-done.12 = bf16[128,1152]{1,0:T(8,128)(2,1)S(1)} collective-permute-done((bf16[128,1152]{1,0:T(8,128)(2,1)S(1)}, bf16[128,1152]{1,0:T(8,128)(2,1)S(1)}, u32[]{:S(2)}, u32[]{:S(2)}) %collective-permute-start.12) | collective-permute-done | bytes 294944 | tf_op jit(solution)/shard_map/ppermute | solution.py:74
  85.1 3.6 %collective-permute-start.15 = (bf16[1328,128]{1,0:T(8,128)(2,1)S(1)}, bf16[1328,128]{1,0:T(8,128)(2,1)S(1)}, u32[]{:S(2)}, u32[]{:S(2)}) collective-permute-start(bf16[1328,128]{1,0:T(8,128)(2,1)S(1)} %slice.4.p0), channel_id=1, source_target_pairs={{0,192},{1,193},{2,194},{3,195},{4,196},{5,197},{6,198},{7,199},{8... | collective-permute-start | bytes 1019912 | tf_op jit(solution)/shard_map/ppermute | solution.py:366
  90.0 3.8 %collective-permute-start.16 = (bf16[1328,128]{1,0:T(8,128)(2,1)S(1)}, bf16[1328,128]{1,0:T(8,128)(2,1)S(1)}, u32[]{:S(2)}, u32[]{:S(2)}) collective-permute-start(bf16[1328,128]{1,0:T(8,128)(2,1)S(1)} %slice.4.p0), channel_id=1, source_target_pairs={{0,16},{16,0},{1,17},{17,1},{2,18},{18,2},{3,19},{19,3},{4,20},{20... | collective-permute-start | bytes 1019912 | tf_op jit(solution)/shard_map/ppermute | solution.py:74
  93.8 2.6 %collective-permute-done.15.p3 = bf16[1328,128]{1,0:T(8,128)(2,1)S(1)} collective-permute-done((bf16[1328,128]{1,0:T(8,128)(2,1)S(1)}, bf16[1328,128]{1,0:T(8,128)(2,1)S(1)}, u32[]{:S(2)}, u32[]{:S(2)}) %collective-permute-start.15) | collective-permute-done | bytes 340000 | tf_op jit(solution)/shard_map/ppermute | solution.py:366
  97.0 3.1 %collective-permute-start.18 = (bf16[1328,128]{1,0:T(8,128)(2,1)S(1)}, bf16[1328,128]{1,0:T(8,128)(2,1)S(1)}, u32[]{:S(2)}, u32[]{:S(2)}) collective-permute-start(bf16[1328,128]{1,0:T(8,128)(2,1)S(1)} %collective-permute-done.14.p2), channel_id=1, source_target_pairs={{0,16},{16,0},{1,17},{17,1},{2,18},{18,2},{3,19},{19,3},{4,20},{20... | collective-permute-start | bytes 1019912 | tf_op jit(solution)/shard_map/ppermute | solution.py:74
  100.0 3.5 %collective-permute-start.17 = (bf16[1328,128]{1,0:T(8,128)(2,1)S(1)}, bf16[1328,128]{1,0:T(8,128)(2,1)S(1)}, u32[]{:S(2)}, u32[]{:S(2)}) collective-permute-start(bf16[1328,128]{1,0:T(8,128)(2,1)S(1)} %collective-permute-done.13.p1), channel_id=1, source_target_pairs={{0,16},{16,0},{1,17},{17,1},{2,18},{18,2},{3,19},{19,3},{4,20},{20... | collective-permute-start | bytes 1019912 | tf_op jit(solution)/shard_map/ppermute | solution.py:74
  104.8 3.9 %last.1 = (f32[1152,1152]{1,0:T(8,128)}, f32[1152]{0:T(1024)}, f32[1]{0:T(128)}) custom-call(f32[1]{0:T(128)S(6)} %copy.15.clip_ref, bf16[1328,128]{1,0:T(8,128)(2,1)S(1)} %slice.4.p0, bf16[1328,128]{1,0:T(8,128)(2,1)S(1)} %collective-permute-done.13.p1, bf16[1328,128]{1,0:T(8,128)(2,1)S(1)} %collective-permute-done.14.p2, ...), custom_call_target="tpu_custom_call" | custom-call | flops 5308416 | bytes 8500000 | tf_op jit(solution)/shard_map/last/pallas_call | solution.py:369
  (43 shorter events, 15.9 us)
Async XLA Ops:
  0.6 11.5 %collective-permute-start.3 = (bf16[128,1152]{1,0:T(8,128)(2,1)}, bf16[128,1152]{1,0:T(8,128)(2,1)S(1)}, u32[]{:S(2)}, u32[]{:S(2)}) collective-permute-start(bf16[128,1152]{1,0:T(8,128)(2,1)} %t_ref.1), channel_id=1, source_target_pairs={{0,48},{16,32},{32,16},{48,0},{1,49},{17,33},{33,17},{49,1},{2,50}... | collective-permute-start | bytes 884744 | tf_op jit(solution)/shard_map/ppermute | solution.py:293
  5.0 18.1 %collective-permute-start.5 = (bf16[128,1152]{1,0:T(8,128)(2,1)}, bf16[128,1152]{1,0:T(8,128)(2,1)S(1)}, u32[]{:S(2)}, u32[]{:S(2)}) collective-permute-start(bf16[128,1152]{1,0:T(8,128)(2,1)} %t_ref.1), channel_id=1, source_target_pairs={{0,32},{32,0},{1,33},{33,1},{2,34},{34,2},{3,35},{35,3},{4,36},{36... | collective-permute-start | bytes 884744 | tf_op jit(solution)/shard_map/ppermute | solution.py:74
  6.8 17.8 %collective-permute-start.2 = (bf16[128,1152]{1,0:T(8,128)(2,1)}, bf16[128,1152]{1,0:T(8,128)(2,1)S(1)}, u32[]{:S(2)}, u32[]{:S(2)}) collective-permute-start(bf16[128,1152]{1,0:T(8,128)(2,1)} %i0.3), channel_id=1, source_target_pairs={{0,192},{64,0},{128,64},{192,128},{1,193},{65,1},{129,65},{193,129... | collective-permute-start | bytes 884744 | tf_op jit(solution)/shard_map/ppermute | solution.py:74
  7.6 17.0 %collective-permute-start.1 = (bf16[128,1152]{1,0:T(8,128)(2,1)}, bf16[128,1152]{1,0:T(8,128)(2,1)S(1)}, u32[]{:S(2)}, u32[]{:S(2)}) collective-permute-start(bf16[128,1152]{1,0:T(8,128)(2,1)} %i0.3), channel_id=1, source_target_pairs={{0,64},{64,128},{128,192},{192,0},{1,65},{65,129},{129,193},{193,1... | collective-permute-start | bytes 884744 | tf_op jit(solution)/shard_map/ppermute | solution.py:74
  8.3 16.3 %collective-permute-start = (bf16[128,1152]{1,0:T(8,128)(2,1)}, bf16[128,1152]{1,0:T(8,128)(2,1)S(1)}, u32[]{:S(2)}, u32[]{:S(2)}) collective-permute-start(bf16[128,1152]{1,0:T(8,128)(2,1)} %i0.3), channel_id=1, source_target_pairs={{0,128},{64,192},{128,0},{192,64},{1,129},{65,193},{129,1},{193,65... | collective-permute-start | bytes 884744 | tf_op jit(solution)/shard_map/ppermute | solution.py:74
  12.1 11.7 %collective-permute-start.4 = (bf16[128,1152]{1,0:T(8,128)(2,1)}, bf16[128,1152]{1,0:T(8,128)(2,1)S(1)}, u32[]{:S(2)}, u32[]{:S(2)}) collective-permute-start(bf16[128,1152]{1,0:T(8,128)(2,1)} %t_ref.1), channel_id=1, source_target_pairs={{0,16},{16,0},{1,17},{17,1},{2,18},{18,2},{3,19},{19,3},{4,20},{20... | collective-permute-start | bytes 884744 | tf_op jit(solution)/shard_map/ppermute | solution.py:74
  17.8 6.9 %copy-start.3 = (bf16[128,1152]{1,0:T(8,128)(2,1)S(1)}, bf16[128,1152]{1,0:T(8,128)(2,1)}, u32[]{:S(2)}) copy-start(bf16[128,1152]{1,0:T(8,128)(2,1)} %i0.3) | copy-start | bytes 884740
  20.6 1.8 %copy-start.1 = (bf16[1152,1152]{1,0:T(8,128)(2,1)S(1)}, bf16[1152,1152]{1,0:T(8,128)(2,1)}, u32[]{:S(2)}) copy-start(bf16[1152,1152]{1,0:T(8,128)(2,1)} %w_ref.7) | copy-start | bytes 7962628
  28.9 2.2 %collective-permute-start.6 = (bf16[544,640]{1,0:T(8,128)(2,1)S(1)}, bf16[544,640]{1,0:T(8,128)(2,1)S(1)}, u32[]{:S(2)}, u32[]{:S(2)}) collective-permute-start(bf16[544,640]{1,0:T(8,128)(2,1)S(1)} %get-tuple-element.63), channel_id=1, source_target_pairs={{0,16},{16,0},{1,17},{17,1},{2,18},{18,2},{3,19},{19,3},{4,20},{20... | collective-permute-start | bytes 2088968 | tf_op jit(solution)/shard_map/ppermute | solution.py:74
  32.5 7.6 %collective-permute-start.7 = (bf16[1328,128]{1,0:T(8,128)(2,1)S(1)}, bf16[1328,128]{1,0:T(8,128)(2,1)S(1)}, u32[]{:S(2)}, u32[]{:S(2)}) collective-permute-start(bf16[1328,128]{1,0:T(8,128)(2,1)S(1)} %get-tuple-element.65), channel_id=1, source_target_pairs={{0,64},{1,65},{2,66},{3,67},{4,68},{5,69},{6,70},{7,71},{8,72},{9,... | collective-permute-start | bytes 1019912 | tf_op jit(solution)/shard_map/ppermute | solution.py:341
  33.6 10.9 %collective-permute-start.8 = (bf16[1328,128]{1,0:T(8,128)(2,1)S(1)}, bf16[1328,128]{1,0:T(8,128)(2,1)S(1)}, u32[]{:S(2)}, u32[]{:S(2)}) collective-permute-start(bf16[1328,128]{1,0:T(8,128)(2,1)S(1)} %get-tuple-element.66), channel_id=1, source_target_pairs={{0,128},{1,129},{2,130},{3,131},{4,132},{5,133},{6,134},{7,135},{8... | collective-permute-start | bytes 1019912 | tf_op jit(solution)/shard_map/ppermute | solution.py:341
  36.2 8.2 %collective-permute-start.9 = (bf16[1328,128]{1,0:T(8,128)(2,1)S(1)}, bf16[1328,128]{1,0:T(8,128)(2,1)S(1)}, u32[]{:S(2)}, u32[]{:S(2)}) collective-permute-start(bf16[1328,128]{1,0:T(8,128)(2,1)S(1)} %get-tuple-element.67), channel_id=1, source_target_pairs={{0,192},{1,193},{2,194},{3,195},{4,196},{5,197},{6,198},{7,199},{8... | collective-permute-start | bytes 1019912 | tf_op jit(solution)/shard_map/ppermute | solution.py:341
  45.4 21.5 %all-to-all-start = ((bf16[32,48,128]{2,1,0:T(8,128)(2,1)}), bf16[32,48,128]{2,1,0:T(8,128)(2,1)S(1)}, u32[]{:S(2)}, u32[]{:S(2)}) async-start(bf16[32,48,128]{2,1,0:T(8,128)(2,1)} %bitcast.3), calls=%async_computation | async-start | bytes 786432 | tf_op jit(solution)/shard_map/all_to_all | solution.py:351
  54.9 8.8 %collective-permute-start.10 = (bf16[128,1152]{1,0:T(8,128)(2,1)S(1)}, bf16[128,1152]{1,0:T(8,128)(2,1)S(1)}, u32[]{:S(2)}, u32[]{:S(2)}) collective-permute-start(bf16[128,1152]{1,0:T(8,128)(2,1)S(1)} %get-tuple-element.69), channel_id=1, source_target_pairs={{0,192},{64,0},{128,64},{192,128},{1,193},{65,1},{129,65},{193,129... | collective-permute-start | bytes 884744 | tf_op jit(solution)/shard_map/ppermute | solution.py:74
  57.4 9.4 %collective-permute-start.11 = (bf16[128,1152]{1,0:T(8,128)(2,1)S(1)}, bf16[128,1152]{1,0:T(8,128)(2,1)S(1)}, u32[]{:S(2)}, u32[]{:S(2)}) collective-permute-start(bf16[128,1152]{1,0:T(8,128)(2,1)S(1)} %get-tuple-element.70), channel_id=1, source_target_pairs={{0,64},{64,128},{128,192},{192,0},{1,65},{65,129},{129,193},{193,1... | collective-permute-start | bytes 884744 | tf_op jit(solution)/shard_map/ppermute | solution.py:74
  67.7 17.4 %all-to-all-start.1 = ((bf16[32,48,128]{2,1,0:T(8,128)(2,1)}), bf16[32,48,128]{2,1,0:T(8,128)(2,1)S(1)}, u32[]{:S(2)}, u32[]{:S(2)}) async-start(bf16[32,48,128]{2,1,0:T(8,128)(2,1)} %copies.1), calls=%async_computation.1 | async-start | bytes 786432 | tf_op jit(solution)/shard_map/all_to_all | solution.py:361
  76.1 8.9 %collective-permute-start.12 = (bf16[128,1152]{1,0:T(8,128)(2,1)S(1)}, bf16[128,1152]{1,0:T(8,128)(2,1)S(1)}, u32[]{:S(2)}, u32[]{:S(2)}) collective-permute-start(bf16[128,1152]{1,0:T(8,128)(2,1)S(1)} %get-tuple-element.72), channel_id=1, source_target_pairs={{0,128},{64,192},{128,0},{192,64},{1,129},{65,193},{129,1},{193,65... | collective-permute-start | bytes 884744 | tf_op jit(solution)/shard_map/ppermute | solution.py:74
  85.1 11.4 %collective-permute-start.15 = (bf16[1328,128]{1,0:T(8,128)(2,1)S(1)}, bf16[1328,128]{1,0:T(8,128)(2,1)S(1)}, u32[]{:S(2)}, u32[]{:S(2)}) collective-permute-start(bf16[1328,128]{1,0:T(8,128)(2,1)S(1)} %slice.4.p0), channel_id=1, source_target_pairs={{0,192},{1,193},{2,194},{3,195},{4,196},{5,197},{6,198},{7,199},{8... | collective-permute-start | bytes 1019912 | tf_op jit(solution)/shard_map/ppermute | solution.py:366
  88.7 8.3 %collective-permute-start.14 = (bf16[1328,128]{1,0:T(8,128)(2,1)S(1)}, bf16[1328,128]{1,0:T(8,128)(2,1)S(1)}, u32[]{:S(2)}, u32[]{:S(2)}) collective-permute-start(bf16[1328,128]{1,0:T(8,128)(2,1)S(1)} %slice.4.p0), channel_id=1, source_target_pairs={{0,128},{1,129},{2,130},{3,131},{4,132},{5,133},{6,134},{7,135},{8... | collective-permute-start | bytes 1019912 | tf_op jit(solution)/shard_map/ppermute | solution.py:366
  88.7 11.3 %collective-permute-start.13 = (bf16[1328,128]{1,0:T(8,128)(2,1)S(1)}, bf16[1328,128]{1,0:T(8,128)(2,1)S(1)}, u32[]{:S(2)}, u32[]{:S(2)}) collective-permute-start(bf16[1328,128]{1,0:T(8,128)(2,1)S(1)} %slice.4.p0), channel_id=1, source_target_pairs={{0,64},{1,65},{2,66},{3,67},{4,68},{5,69},{6,70},{7,71},{8,72},{9,... | collective-permute-start | bytes 1019912 | tf_op jit(solution)/shard_map/ppermute | solution.py:366
  90.0 14.5 %collective-permute-start.16 = (bf16[1328,128]{1,0:T(8,128)(2,1)S(1)}, bf16[1328,128]{1,0:T(8,128)(2,1)S(1)}, u32[]{:S(2)}, u32[]{:S(2)}) collective-permute-start(bf16[1328,128]{1,0:T(8,128)(2,1)S(1)} %slice.4.p0), channel_id=1, source_target_pairs={{0,16},{16,0},{1,17},{17,1},{2,18},{18,2},{3,19},{19,3},{4,20},{20... | collective-permute-start | bytes 1019912 | tf_op jit(solution)/shard_map/ppermute | solution.py:74
  96.5 8.0 %collective-permute-start.19 = (bf16[1328,128]{1,0:T(8,128)(2,1)S(1)}, bf16[1328,128]{1,0:T(8,128)(2,1)S(1)}, u32[]{:S(2)}, u32[]{:S(2)}) collective-permute-start(bf16[1328,128]{1,0:T(8,128)(2,1)S(1)} %collective-permute-done.15.p3), channel_id=1, source_target_pairs={{0,16},{16,0},{1,17},{17,1},{2,18},{18,2},{3,19},{19,3},{4,20},{20... | collective-permute-start | bytes 1019912 | tf_op jit(solution)/shard_map/ppermute | solution.py:74
  97.0 7.5 %collective-permute-start.18 = (bf16[1328,128]{1,0:T(8,128)(2,1)S(1)}, bf16[1328,128]{1,0:T(8,128)(2,1)S(1)}, u32[]{:S(2)}, u32[]{:S(2)}) collective-permute-start(bf16[1328,128]{1,0:T(8,128)(2,1)S(1)} %collective-permute-done.14.p2), channel_id=1, source_target_pairs={{0,16},{16,0},{1,17},{17,1},{2,18},{18,2},{3,19},{19,3},{4,20},{20... | collective-permute-start | bytes 1019912 | tf_op jit(solution)/shard_map/ppermute | solution.py:74
  100.0 4.8 %collective-permute-start.17 = (bf16[1328,128]{1,0:T(8,128)(2,1)S(1)}, bf16[1328,128]{1,0:T(8,128)(2,1)S(1)}, u32[]{:S(2)}, u32[]{:S(2)}) collective-permute-start(bf16[1328,128]{1,0:T(8,128)(2,1)S(1)} %collective-permute-done.13.p1), channel_id=1, source_target_pairs={{0,16},{16,0},{1,17},{17,1},{2,18},{18,2},{3,19},{19,3},{4,20},{20... | collective-permute-start | bytes 1019912 | tf_op jit(solution)/shard_map/ppermute | solution.py:74
  (2 other events, 2.7 us)
